TPU v7x, 128 devices: a whole 4x4x4 slice. The times are simulated.
128 devices in a mesh: cluster: 4 (over z), member: 32 (over y, x, core).
Axes of the slice: x: 4, y: 4, z: 4, core: 2. Of those that a mesh axis runs over, the one named last changes fastest.
Arguments:
- embeddings: bfloat16 [32768, 768], P(('cluster', 'member')), may hold values from -6 to 6
- destination: int32 [32768, 1], P(('cluster', 'member')), may hold values from 0 to 127; in each aligned block of 256 rows (0 to 255, 256 to 511, ...) at most 4 rows name the same one
Outputs:
- dup_score: float32 [32768], P(('cluster', 'member'))
Inputs may be any that keep to these rules, and one draw needn't show every extreme that they name: In the rows of one device, no destination is named more than 4 times, a bound that some block reaches.
All inputs are finite; a program needn't handle non-finite values.
Results may differ from a plain program's by a relative error of at most 0.0003.
Values may be sent and summed in bfloat16 or wider, within the bound.
No kernel may reach another device: no remote copies, remote signals or barrier semaphores. Data moves between devices by JAX's collectives and lax.ppermute only.
A program may use at most 128 MiB of HBM per device.

v0:
```python
import jax
import jax.numpy as jnp
from jax import lax
from jax.sharding import PartitionSpec as P

sharpness = 30.0


def pair_weights(left_units, left_labels, right_units, right_labels):
    scores = lax.dot_general(
        left_units, right_units, (((1,), (1,)), ((), ())), preferred_element_type=jnp.float32
    )
    matching = (left_labels[:, None] == right_labels[None, :]) & (right_labels[None, :] >= 0.0)
    return jnp.where(matching, jnp.exp(sharpness * scores), jnp.zeros_like(scores))


def shards(embeddings, destination):
    group_count = lax.axis_size("cluster")
    member_count = lax.axis_size("member")
    device_count = group_count * member_count
    row_count, features = embeddings.shape
    capacity = max(2, 2 * row_count // device_count)
    slot_count = device_count * capacity
    vectors = embeddings.astype(jnp.float32)
    unit_rows = (
        vectors * lax.rsqrt(jnp.sum(vectors * vectors, axis=1, keepdims=True) + 1e-06)
    ).astype(jnp.bfloat16)
    target = destination[:, 0]
    onehot = (target[:, None] == jnp.arange(device_count, dtype=jnp.int32)[None, :]).astype(
        jnp.int32
    )
    position = jnp.sum(jnp.cumsum(onehot, axis=0) * onehot, axis=1) - 1
    send_units = (
        jnp.zeros((device_count, capacity, features), jnp.bfloat16)
        .at[target, position]
        .set(unit_rows)
    )
    send_labels = (
        jnp.full((device_count, capacity), -1.0, jnp.bfloat16)
        .at[target, position]
        .set(jnp.zeros((row_count,), jnp.bfloat16))
    )
    got_units, got_labels = (
        lax.all_to_all(send_units, ("cluster", "member"), split_axis=0, concat_axis=0, tiled=True),
        lax.all_to_all(send_labels, ("cluster", "member"), split_axis=0, concat_axis=0, tiled=True),
    )
    local_units = got_units.reshape(slot_count, features)
    wire_labels = got_labels.reshape(slot_count)
    local_labels = wire_labels.astype(jnp.float32)
    row_ids = jnp.arange(slot_count, dtype=jnp.int32)
    first_slot = lax.axis_index("member") * slot_count
    piece_units = lax.all_gather(local_units, "member", axis=0, tiled=True)
    piece_labels = lax.all_gather(wire_labels, "member", axis=0, tiled=True)
    weights = pair_weights(local_units, local_labels, piece_units, piece_labels.astype(jnp.float32))
    column_ids = jnp.arange(piece_units.shape[0], dtype=jnp.int32)
    weights = jnp.where((first_slot + row_ids)[:, None] == column_ids[None, :], 0.0, weights)
    density = jnp.sum(weights, axis=1)
    back_scores = lax.all_to_all(
        density.reshape(device_count, capacity),
        ("cluster", "member"),
        split_axis=0,
        concat_axis=0,
        tiled=True,
    )
    own_density = back_scores[target, position]
    return jnp.log1p(own_density)


def solution(mesh):
    in_specs = (P(("cluster", "member"), None), P(("cluster", "member"), None))
    out_specs = P(("cluster", "member"))
    return jax.shard_map(shards, mesh=mesh, in_specs=in_specs, out_specs=out_specs, check_vma=False)
```

profile of v0, /device:TPU:1, one launch (start us, length us, event | category | flops | bytes accessed | tf_op | source)
XLA Modules:
  0.0 194.7 jit_solution(8016221065746308527)
XLA Ops:
  6.5 0.0 all-gather.3.cloned.1.call-start
  6.5 1.2 fusion
  7.7 0.8 copy.8
  8.5 0.2 fusion.2
  8.8 0.9 fusion.3
  9.7 1.1 fusion.1
  10.8 0.7 or_select_fusion
  11.5 0.2 broadcast_in_dim.12
  11.7 14.2 %scatter_fusion.1 = bf16[128,4,768]{2,1,0:T(4,128)(2,1)S(1)} fusion(bf16[128,4,768]{2,1,0:T(4,128)(2,1)S(1)} %broadcast_in_dim.12, s32[256]{0:T(256)S(1)} %bitcast.26, bf16[256,768]{1,0:T(8,128)(2,1)S(1)} %fusion.1), kind=kCustom, calls=%fused_computation.2 | custom fusion | bytes 1181696 | tf_op jit(solution)/shard_map/scatter | solution.py:36
  25.9 27.8 %all_to_all.26 = bf16[128,4,768]{2,1,0:T(4,128)(2,1)S(1)} all-to-all(bf16[128,4,768]{2,1,0:T(4,128)(2,1)S(1)} %scatter_fusion.1), channel_id=1, replica_groups=mesh['cluster'=4,'member'=32] {'cluster','member'}, dimensions={0} | all-to-all | bytes 1572864 | tf_op jit(solution)/shard_map/all_to_all | solution.py:44
  53.7 1.1 reshape.70
  54.8 0.0 all-gather.3.cloned.1.call-update
  54.9 11.4 %scatter_fusion = bf16[128,4]{0,1:T(4,128)(2,1)S(1)} fusion(bf16[128,4]{0,1:T(4,128)(2,1)S(1)} %broadcast_in_dim.10, s32[256]{0:T(256)S(1)} %bitcast.27, bf16[256]{0:T(256)(128)(2,1)S(1)} %broadcast.114), kind=kCustom, calls=%fused_computation.1 | custom fusion | bytes 3584 | tf_op jit(solution)/shard_map/scatter | solution.py:41
  66.3 0.8 copy.10
  67.1 4.4 %all-to-all-start = ((bf16[128,1,4]{2,1,0:T(2,128)(2,1)}), bf16[128,1,4]{2,1,0:T(2,128)(2,1)S(1)}, u32[]{:S(2)}, u32[]{:S(2)}) async-start(bf16[128,1,4]{2,1,0:T(2,128)(2,1)} %copy.10), calls=%async_computation | async-start | bytes 131072 | tf_op jit(solution)/shard_map/all_to_all | solution.py:45
  71.5 9.9 %all-to-all-done = bf16[128,1,4]{2,1,0:T(2,128)(2,1)S(1)} async-done(((bf16[128,1,4]{2,1,0:T(2,128)(2,1)}), bf16[128,1,4]{2,1,0:T(2,128)(2,1)S(1)}, u32[]{:S(2)}, u32[]{:S(2)}) %all-to-all-start) | async-done | bytes 1056 | tf_op jit(solution)/shard_map/all_to_all | solution.py:45
  81.4 0.2 reduce.1
  81.6 0.1 reshape.89
  81.7 0.2 convert_reduce_fusion
  81.9 0.1 reshape.93
  82.0 22.8 %all-gather = bf16[32,1,512]{2,1,0:T(2,128)(2,1)S(1)} all-gather(bf16[1,1,512]{2,1,0:T(2,128)(2,1)S(1)} %reshape.89), channel_id=1, replica_groups=mesh['cluster'=4,'member'=32] {'member'}, dimensions={0}, use_global_device_ids=true | all-gather | bytes 33792 | tf_op jit(solution)/shard_map/all_gather | solution.py:53
  104.8 0.1 convert_element_type.26
  104.9 39.4 %all-gather.3.cloned.1.call-done = bf16[16384,768]{1,0:T(8,128)(2,1)} async-done(((bf16[512,768]{1,0:T(8,128)(2,1)}), bf16[16384,768]{1,0:T(8,128)(2,1)}) %all-gather.3.cloned.1.call-update) | async-done | bytes 25165840 | tf_op jit(solution)/shard_map/all_gather | solution.py:52
  144.3 24.2 %select_reduce_fusion = f32[512]{0:T(512)S(1)} fusion(bf16[512,768]{1,0:T(8,128)(2,1)} %reshape.70, bf16[16384,768]{1,0:T(8,128)(2,1)} %all-gather.3.cloned.1.call-done, f32[16384]{0:T(1024)S(1)} %bitcast.33, s32[512]{0:T(512)S(1)} %iota_add_fusion, f32[512]{0:T(512)S(1)} %reshape.93, pred[16384]{0:T(1024)(128)(4,1)S(1)} %broadcast_compare_fusion), kind=kOutput, calls=%fused_computation.3 | convolution fusion | flops 12943622144 | bytes 26040320 | tf_op jit(solution)/shard_map/dot_general | solution.py:10
  168.5 0.1 all_to_all.20
  168.7 16.7 %all_to_all.27 = f32[128,1,4]{2,1,0:T(1,128)S(1)} all-to-all(f32[128,1,4]{2,1,0:T(1,128)S(1)} %bitcast.34), channel_id=1, replica_groups=mesh['cluster'=4,'member'=32] {'cluster','member'}, dimensions={0} | all-to-all | bytes 4096 | tf_op jit(solution)/shard_map/all_to_all | solution.py:58
  185.3 1.9 gather_fusion
  187.3 0.6 log1p.3
  (12 shorter events, 0.1 us)
Async XLA Ops:
  6.5 137.8 %all-gather.3.cloned.1.call-start = ((), (), s32[]{:S(2)}) async-start(), calls=%async_computation.3 | async-start | bytes 25952256 | tf_op jit(solution)/shard_map/all_gather | solution.py:52
  67.1 14.3 %all-to-all-start = ((bf16[128,1,4]{2,1,0:T(2,128)(2,1)}), bf16[128,1,4]{2,1,0:T(2,128)(2,1)S(1)}, u32[]{:S(2)}, u32[]{:S(2)}) async-start(bf16[128,1,4]{2,1,0:T(2,128)(2,1)} %copy.10), calls=%async_computation | async-start | bytes 131072 | tf_op jit(solution)/shard_map/all_to_all | solution.py:45
Sparse Core Ops, SparseCore 0:
  55.0 89.2 all-gather.2
where the time goes:
time: 195 us
  blocking collectives  67.3 us (35%)
  waiting for transfers between devices  49.3 us (25%)
  local copies, waits for them, and re-layouts  31.3 us (16%)
  matrix products  24.2 us (12%)
  between operations  13.5 us (7%)
  other arithmetic  4.55 us (2%)
  starting transfers between devices  4.42 us (2%)
    all_gather x1, waiting for transfers between devices, shards(): piece_units = lax.all_gather(local_units, 'member', axis=0, tiled=True)  39.4 us
    all_to_all x1, blocking collectives, shards(): lax.all_to_all(send_units, ('cluster', 'member'), split_axis=0, concat_ax...  27.8 us
    dot_general x1, matrix products, pair_weights(): lax.dot_general(left_units, right_units, (((1,), (1,)), ((), ())), prefer...  24.2 us
    all_gather x1, blocking collectives, shards(): piece_labels = lax.all_gather(wire_labels, 'member', axis=0, tiled=True)  22.8 us
    all_to_all x1, blocking collectives, shards(): lax.all_to_all(density.reshape(device_count, capacity), ('cluster', 'memb...  16.7 us
    scatter x1, local copies, waits for them, and re-layouts, shards(): send_units = jnp.zeros((device_count, capacity, features), jnp.bfloat16)....  14.2 us
    scatter x1, local copies, waits for them, and re-layouts, shards(): send_labels = jnp.full((device_count, capacity), -1.0, jnp.bfloat16).at[t...  11.4 us
    all_to_all x1, waiting for transfers between devices, shards(): lax.all_to_all(send_labels, ('cluster', 'member'), split_axis=0, concat_a...  9.88 us
  transfers between devices with their start and end apart: 2, of which 2 were waited for; matrix products, arithmetic and copies ran while one was open for 7% of the time, Pallas kernels for 0%

commit v1 on v0

v1 whole, which is shorter than its diff:
```python
import functools
import math

import jax
import jax.numpy as jnp
import numpy as np
from jax import lax
from jax.experimental import pallas as pl
from jax.experimental.pallas import tpu as pltpu
from jax.sharding import PartitionSpec as P

sharpness = 30.0
EXP2_SCALE = sharpness * math.log2(math.e)
ROWS, WIDTH, LABEL_ROWS, LANES = 256, 768, 16, 128
BOTH = ("cluster", "member")
CLUSTER_SHIFT = 5

PLAN = (
    (0, 5, 51),
    (0, 28, 28),
    (0, 51, 5),
    (3, 48, 4),
    (3, 12, 3),
    (1, 12, 48),
    (0, 3, 1),
    (2, 16, 16),
    (1, 4, 12),
    (0, 4, 3),
)


def shift(place, by):
    return sum(((place >> s) + (by >> s) & 3) << s for s in (0, 2, 4))


def minus(place):
    return sum((-(place >> s) & 3) << s for s in (0, 2, 4))


def device(place, core):
    x, y, z = place & 3, place >> 2 & 3, place >> 4
    return ((z * 4 + y) * 4 + x) * 2 + core


def fetch(jumps):
    return [(device(shift(p, jumps[c]), c), device(p, c)) for p in range(64) for c in (0, 1)]


def give(jumps):
    return [(b, a) for a, b in fetch(jumps)]


CORE_SWAP = [(d, d ^ 1) for d in range(128)]


def held_offsets():
    held = ([0], [0])
    for source, *jumps in PLAN:
        for core in (0, 1):
            held[core].append(shift(held[core][source], jumps[core]))
    return held


HELD = held_offsets()
BLOCKS = len(HELD[0])
OFFSETS = sorted(HELD[0])
assert OFFSETS == sorted(HELD[1])


def slot(core, offset, kind):
    return HELD[kind].index(offset) + (0 if core == kind else BLOCKS)


def class_pairs():
    found = {}
    for a in OFFSETS:
        for b in OFFSETS:
            d = shift(a, minus(b))
            if d and minus(d) not in found and d not in found:
                found[d] = (a, b)
    assert len(found) == 35
    return found


def tables():
    wide, narrow = [], []
    for variant in range(16):
        core, high = variant & 1, variant >> 1
        w, n = [], []
        for d, (a, b) in class_pairs().items():
            if d == minus(d):
                bit = next(i for i in range(3) if d >> (2 * i) & 3 == 2)
                kind = high >> bit & 1
                ka, kb = (0, 1) if core == 0 else (kind, kind)
                n.append((slot(core, a, ka), slot(core, b, kb)))
            else:
                w.append((slot(core, a, core), slot(core, b, 0), slot(core, b, 1)))
        wide.append(w)
        narrow.append(n)
    return np.array(wide, np.int32), np.array(narrow, np.int32)


def pack_body(rows_ref, target_ref, out_ref):
    vectors = rows_ref[...].astype(jnp.float32)
    norms = jnp.sum(vectors * vectors, axis=1, keepdims=True)
    out_ref[0:ROWS, :] = (vectors * lax.rsqrt(norms + 1e-06)).astype(jnp.bfloat16)
    labels = (target_ref[...] >> CLUSTER_SHIFT).astype(jnp.float32)
    columns = jnp.broadcast_to(labels, (ROWS, LANES))
    out_ref[ROWS:, :] = jnp.zeros((LABEL_ROWS, WIDTH), jnp.bfloat16)
    for half in range(ROWS // LANES):
        part = slice(half * LANES, (half + 1) * LANES)
        out_ref[ROWS:, part] = columns[part].T[0:LABEL_ROWS].astype(jnp.bfloat16)


def pack(embeddings, destination):
    return pl.pallas_call(
        pack_body,
        out_shape=jax.ShapeDtypeStruct((ROWS + LABEL_ROWS, WIDTH), jnp.bfloat16),
        name="pack",
    )(embeddings, destination)


def halves():
    return [slice(h * LANES, (h + 1) * LANES) for h in range(ROWS // LANES)]


def pairs_body(slots, wide_count, narrow_count, variant_ref, wide_ref, narrow_ref, *refs):
    blocks, out_ref = refs[:slots], refs[slots]
    held, row_labels, column_labels, row_sums, column_sums, arrived = refs[slots + 1 :]
    variant = variant_ref[0]
    copies = [pltpu.make_async_copy(blocks[k], held.at[k], arrived.at[k]) for k in range(slots)]
    for copy in copies:
        copy.start()
    row_sums[...] = jnp.zeros_like(row_sums)
    column_sums[...] = jnp.zeros_like(column_sums)
    for k in range(slots):
        copies[k].wait()
        labels = held[k, ROWS:, 0:ROWS].astype(jnp.float32)
        row_labels[k] = labels[0:8]
        for part in halves():
            column_labels[k, part, :] = jnp.broadcast_to(labels[0:1, part], (LANES, LANES)).T

    def weights(a, b):
        scores = lax.dot_general(
            held[a, 0:ROWS], held[b, 0:ROWS], (((1,), (1,)), ((), ())), preferred_element_type=jnp.float32
        )
        left = column_labels[a]
        return [
            jnp.where(left == row_labels[b, 0:1, part], jnp.exp2(scores[:, part] * EXP2_SCALE), 0.0)
            for part in halves()
        ]

    def add_columns(b, values):
        for part, value in zip(halves(), values):
            column_sums[b, :, part] += jnp.sum(value.reshape(ROWS // 8, 8, LANES), axis=0)

    def wide_unit(i, _):
        at = (variant * wide_count + i) * 3
        a = wide_ref[at]
        total = row_sums[a]
        for b in (wide_ref[at + 1], wide_ref[at + 2]):
            values = weights(a, b)
            total += values[0] + values[1]
            add_columns(b, values)
        row_sums[a] = total
        return 0

    def narrow_unit(i, _):
        at = (variant * narrow_count + i) * 2
        a, b = narrow_ref[at], narrow_ref[at + 1]
        values = weights(a, b)
        row_sums[a] += values[0] + values[1]
        add_columns(b, values)
        return 0

    lax.fori_loop(0, wide_count, wide_unit, 0)
    lax.fori_loop(0, narrow_count, narrow_unit, 0)

    own = weights(0, 0)
    rows = lax.broadcasted_iota(jnp.int32, (ROWS, LANES), 0)
    lanes = lax.broadcasted_iota(jnp.int32, (ROWS, LANES), 1)
    for h in range(len(own)):
        row_sums[0] += jnp.where(rows == lanes + h * LANES, 0.0, own[h])

    @pl.when(lax.rem(variant, 2) == 0)
    def _():
        values = weights(0, BLOCKS)
        row_sums[0] += values[0] + values[1]
        add_columns(BLOCKS, values)

    for k in range(slots):
        for part in halves():
            by_lane = jnp.sum(row_sums[k, part, :].T, axis=0, keepdims=True)
            out_ref[k : k + 1, part] = by_lane + jnp.sum(column_sums[k, :, part], axis=0, keepdims=True)


def pair_sums(variant, blocks):
    wide, narrow = tables()
    slots = len(blocks)
    smem, anywhere = pl.BlockSpec(memory_space=pltpu.SMEM), pl.BlockSpec(memory_space=pl.ANY)
    units = 2 * wide.shape[1] + narrow.shape[1] + 2
    return pl.pallas_call(
        functools.partial(pairs_body, slots, wide.shape[1], narrow.shape[1]),
        out_shape=jax.ShapeDtypeStruct((slots, ROWS), jnp.float32),
        in_specs=[smem] * 3 + [anywhere] * slots,
        out_specs=pl.BlockSpec(memory_space=pltpu.VMEM),
        scratch_shapes=[
            pltpu.VMEM((slots, ROWS + LABEL_ROWS, WIDTH), jnp.bfloat16),
            pltpu.VMEM((slots, 8, ROWS), jnp.float32),
            pltpu.VMEM((slots, ROWS, LANES), jnp.float32),
            pltpu.VMEM((slots, ROWS, LANES), jnp.float32),
            pltpu.VMEM((slots, 8, ROWS), jnp.float32),
            pltpu.SemaphoreType.DMA((slots,)),
        ],
        compiler_params=pltpu.CompilerParams(vmem_limit_bytes=32 * 1024 * 1024),
        cost_estimate=pl.CostEstimate(
            flops=2 * units * ROWS * ROWS * WIDTH,
            bytes_accessed=2 * slots * ROWS * WIDTH,
            transcendentals=units * ROWS * ROWS,
        ),
        name="pair_sums",
    )(variant, jnp.asarray(wide.reshape(-1)), jnp.asarray(narrow.reshape(-1)), *blocks)


def shards(embeddings, destination):
    member = lax.axis_index("member")
    core = member & 1
    place = (member >> 1) + 16 * lax.axis_index("cluster")
    high = (place >> 1 & 1) + 2 * (place >> 3 & 1) + 4 * (place >> 5 & 1)
    variant = (core + 2 * high).astype(jnp.int32).reshape(1)

    mine = [pack(embeddings, destination)]
    for source, *jumps in PLAN:
        mine.append(lax.ppermute(mine[source], BOTH, fetch(jumps)))
    others = [lax.ppermute(block, BOTH, CORE_SWAP) for block in mine]
    sums = pair_sums(variant, mine + others)

    shares = [OFFSETS[1::2], OFFSETS[2::2]]
    assert len(shares[0]) == len(shares[1])

    def rows_of(offsets_of, kind_of):
        by_core = [
            np.array([slot(c, offset, kind) for offset in offsets_of(c) for kind in kind_of(c)], np.int32)
            for c in (0, 1)
        ]
        index = jnp.where(core == 0, jnp.asarray(by_core[0]), jnp.asarray(by_core[1]))
        return jnp.take(sums, index, axis=0)

    kinds = lambda c: (0, 1)
    kept = rows_of(lambda c: shares[c], kinds)
    given = rows_of(lambda c: shares[1 - c], kinds)
    kept = (kept + lax.ppermute(given, BOTH, CORE_SWAP)).reshape(-1, 2 * ROWS)
    home = jnp.where(core == 0, sums[0], sums[BLOCKS]), jnp.where(core == 0, sums[BLOCKS], sums[0])
    total = jnp.concatenate(home)
    for k in range(len(shares[0])):
        total += lax.ppermute(kept[k : k + 1], BOTH, give((shares[0][k], shares[1][k])))[0]
    total = total.reshape(2, ROWS)
    own = jnp.where(core == 0, total[0], total[1])
    other = jnp.where(core == 0, total[1], total[0])
    density = own + lax.ppermute(other, BOTH, CORE_SWAP)
    return jnp.log1p(density)


def solution(mesh):
    in_specs = (P(BOTH, None), P(BOTH, None))
    return jax.shard_map(shards, mesh=mesh, in_specs=in_specs, out_specs=P(BOTH), check_vma=False)
```

time: 195 us -> 93.4 us (0.48)
  blocking collectives: 67.3 us -> 0 us
  starting transfers between devices: 4.42 us -> 42.4 us
  waiting for transfers between devices: 49.3 us -> 17.2 us
  Pallas kernels: 0 us -> 24.8 us
  matrix products: 24.2 us -> 0 us
  local copies, waits for them, and re-layouts: 31.3 us -> 7.43 us
  between operations: 13.5 us -> 0.17 us
  other arithmetic: 4.55 us -> 0.78 us
    all_to_all x2 -> x0, blocking collectives: 44.5 us -> none  [the longest x1 27.8 us: shards(): lax.all_to_all(send_units, ('cluster', 'member'), split_axis=0, concat_ax...]
    ppermute x0 -> x28, starting transfers between devices: none -> 42.4 us  [the longest x11 14.8 us: shards(): others = [lax.ppermute(block, BOTH, CORE_SWAP) for block in mine]]
    all_gather x1 -> x0, waiting for transfers between devices: 39.4 us -> none  [shards(): piece_units = lax.all_gather(local_units, 'member', axis=0, tiled=True)]
    scatter x2 -> x0, local copies, waits for them, and re-layouts: 25.6 us -> none  [the longest x1 14.2 us: shards(): send_units = jnp.zeros((device_count, capacity, features), jnp.bfloat16)....]
    pallas_call x0 -> x2, Pallas kernels: none -> 24.8 us  [the longest x1 22.7 us: pair_sums(): pl.pallas_call(functools.partial(pairs_body, slots, wide.shape[1], narrow...]
    dot_general x1 -> x0, matrix products: 24.2 us -> none  [pair_weights(): lax.dot_general(left_units, right_units, (((1,), (1,)), ((), ())), prefer...]
    all_gather x1 -> x0, blocking collectives: 22.8 us -> none  [shards(): piece_labels = lax.all_gather(wire_labels, 'member', axis=0, tiled=True)]
    ppermute x0 -> x28, waiting for transfers between devices: none -> 17.2 us  [the longest x10 13.1 us: shards(): mine.append(lax.ppermute(mine[source], BOTH, fetch(jumps)))]
  transfers between devices with their start and end apart: 2 -> 28, of which waited for: 2 -> 12; matrix products, arithmetic and copies ran while one was open for 7% -> 1% of each run, Pallas kernels for 0% -> 0%
where the time goes in v1:
time: 93.4 us; the launch traced here: 92.9 us
  starting transfers between devices  42.4 us (45%)
  Pallas kernels  24.8 us (27%)
  waiting for transfers between devices  17.2 us (18%)
  local copies, waits for them, and re-layouts  7.43 us (8%)
    pallas_call x1, Pallas kernels, pair_sums(): pl.pallas_call(functools.partial(pairs_body, slots, wide.shape[1], narrow...  22.7 us
    ppermute x11, starting transfers between devices, shards(): others = [lax.ppermute(block, BOTH, CORE_SWAP) for block in mine]  14.8 us
    ppermute x10, starting transfers between devices, shards(): mine.append(lax.ppermute(mine[source], BOTH, fetch(jumps)))  13.9 us
    ppermute x10, waiting for transfers between devices, shards(): mine.append(lax.ppermute(mine[source], BOTH, fetch(jumps)))  13.1 us
    ppermute x5, starting transfers between devices, shards(): lax.ppermute(kept[k:k + 1], BOTH, give((shares[0][k], shares[1][k])))[0]  11.3 us
    unnamed x33, local copies, waits for them, and re-layouts  6.3 us
    ppermute x11, waiting for transfers between devices, shards(): others = [lax.ppermute(block, BOTH, CORE_SWAP) for block in mine]  2.34 us
    pallas_call x1, Pallas kernels, pack(): pl.pallas_call(pack_body, out_shape=jax.ShapeDtypeStruct((ROWS + LABEL_RO...  2.07 us
  transfers between devices with their start and end apart: 28, of which 12 were waited for; matrix products, arithmetic and copies ran while one was open for 1% of the time, Pallas kernels for 0%

profile of v1, /device:TPU:1, one launch (start us, length us, event | category | flops | bytes accessed | tf_op | source)
XLA Modules:
  0.0 92.9 jit_solution(15866790792852296320)
XLA Ops:
  0.0 1.5 %copy.9.target_ref = s32[256,1]{1,0:T(8,128)} copy(s32[256,1]{0,1:T(1,128)} %param.11) | data formatting | bytes 2048 | tf_op args[1]
  1.5 2.1 %pack.1.refs_0_ = bf16[272,768]{1,0:T(8,128)(2,1)} custom-call(bf16[256,768]{1,0:T(8,128)(2,1)} %rows_ref.1, s32[256,1]{1,0:T(8,128)} %copy.9.target_ref), custom_call_target="tpu_custom_call" | custom-call | tf_op jit(solution)/shard_map/pack/pallas_call | solution.py:116
  3.5 5.8 %collective-permute-start.2 = (bf16[272,768]{1,0:T(8,128)(2,1)}, bf16[272,768]{1,0:T(8,128)(2,1)S(1)}, u32[]{:S(2)}, u32[]{:S(2)}) collective-permute-start(bf16[272,768]{1,0:T(8,128)(2,1)} %pack.1.refs_0_), channel_id=1, source_target_pairs={{102,0},{11,1},{96,2},{13,3},{98,4},{15,5},{100,6},{9,7},{110,8},{... | collective-permute-start | bytes 1253384 | tf_op jit(solution)/shard_map/ppermute | solution.py:234
  9.3 0.3 collective-permute-start
  9.6 1.9 %collective-permute-start.1 = (bf16[272,768]{1,0:T(8,128)(2,1)}, bf16[272,768]{1,0:T(8,128)(2,1)S(1)}, u32[]{:S(2)}, u32[]{:S(2)}) collective-permute-start(bf16[272,768]{1,0:T(8,128)(2,1)} %pack.1.refs_0_), channel_id=1, source_target_pairs={{56,0},{57,1},{58,2},{59,3},{60,4},{61,5},{62,6},{63,7},{32,8},{33... | collective-permute-start | bytes 1253384 | tf_op jit(solution)/shard_map/ppermute | solution.py:234
  11.5 1.8 %collective-permute-start.6 = (bf16[272,768]{1,0:T(8,128)(2,1)}, bf16[272,768]{1,0:T(8,128)(2,1)S(1)}, u32[]{:S(2)}, u32[]{:S(2)}) collective-permute-start(bf16[272,768]{1,0:T(8,128)(2,1)} %pack.1.refs_0_), channel_id=1, source_target_pairs={{6,0},{3,1},{0,2},{5,3},{2,4},{7,5},{4,6},{1,7},{14,8},{11,9},{8,1... | collective-permute-start | bytes 1253384 | tf_op jit(solution)/shard_map/ppermute | solution.py:234
  13.3 2.7 %collective-permute-done.2.refs_3_ = bf16[272,768]{1,0:T(8,128)(2,1)S(1)} collective-permute-done((bf16[272,768]{1,0:T(8,128)(2,1)}, bf16[272,768]{1,0:T(8,128)(2,1)S(1)}, u32[]{:S(2)}, u32[]{:S(2)}) %collective-permute-start.2) | collective-permute-done | bytes 417824 | tf_op jit(solution)/shard_map/ppermute | solution.py:234
  16.0 3.0 %collective-permute-start.10 = (bf16[272,768]{1,0:T(8,128)(2,1)}, bf16[272,768]{1,0:T(8,128)(2,1)S(1)}, u32[]{:S(2)}, u32[]{:S(2)}) collective-permute-start(bf16[272,768]{1,0:T(8,128)(2,1)} %pack.1.refs_0_), channel_id=1, source_target_pairs={{0,1},{1,0},{2,3},{3,2},{4,5},{5,4},{6,7},{7,6},{8,9},{9,8},{10,11... | collective-permute-start | bytes 1253384 | tf_op jit(solution)/shard_map/ppermute | solution.py:235
  19.0 5.1 %collective-permute-done.refs_1_ = bf16[272,768]{1,0:T(8,128)(2,1)S(1)} collective-permute-done((bf16[272,768]{1,0:T(8,128)(2,1)}, bf16[272,768]{1,0:T(8,128)(2,1)S(1)}, u32[]{:S(2)}, u32[]{:S(2)}) %collective-permute-start) | collective-permute-done | bytes 417824 | tf_op jit(solution)/shard_map/ppermute | solution.py:234
  24.1 0.5 collective-permute-start.3
  24.6 0.6 collective-permute-start.4
  25.3 3.6 %collective-permute-done.9.refs_10_ = bf16[272,768]{1,0:T(8,128)(2,1)S(1)} collective-permute-done((bf16[272,768]{1,0:T(8,128)(2,1)}, bf16[272,768]{1,0:T(8,128)(2,1)S(1)}, u32[]{:S(2)}, u32[]{:S(2)}) %collective-permute-start.9) | collective-permute-done | bytes 417824 | tf_op jit(solution)/shard_map/ppermute | solution.py:234
  28.9 1.3 %collective-permute-start.8 = (bf16[272,768]{1,0:T(8,128)(2,1)S(1)}, bf16[272,768]{1,0:T(8,128)(2,1)S(1)}, u32[]{:S(2)}, u32[]{:S(2)}) collective-permute-start(bf16[272,768]{1,0:T(8,128)(2,1)S(1)} %collective-permute-done.refs_1_), channel_id=1, source_target_pairs={{8,0},{25,1},{10,2},{27,3},{12,4},{29,5},{14,6},{31,7},{16,8},{1,9... | collective-permute-start | bytes 1253384 | tf_op jit(solution)/shard_map/ppermute | solution.py:234
  30.2 1.6 %collective-permute-start.7 = (bf16[272,768]{1,0:T(8,128)(2,1)S(1)}, bf16[272,768]{1,0:T(8,128)(2,1)S(1)}, u32[]{:S(2)}, u32[]{:S(2)}) collective-permute-start(bf16[272,768]{1,0:T(8,128)(2,1)S(1)} %collective-permute-done.1.refs_2_), channel_id=1, source_target_pairs={{32,0},{33,1},{34,2},{35,3},{36,4},{37,5},{38,6},{39,7},{40,8},{41... | collective-permute-start | bytes 1253384 | tf_op jit(solution)/shard_map/ppermute | solution.py:234
  31.8 2.1 %collective-permute-start.11 = (bf16[272,768]{1,0:T(8,128)(2,1)S(1)}, bf16[272,768]{1,0:T(8,128)(2,1)}, u32[]{:S(2)}, u32[]{:S(2)}) collective-permute-start(bf16[272,768]{1,0:T(8,128)(2,1)S(1)} %collective-permute-done.refs_1_), channel_id=1, source_target_pairs={{0,1},{1,0},{2,3},{3,2},{4,5},{5,4},{6,7},{7,6},{8,9},{9,8},{10,11... | collective-permute-start | bytes 1253384 | tf_op jit(solution)/shard_map/ppermute | solution.py:235
  33.9 0.2 collective-permute-start.13
  34.2 1.7 %collective-permute-done.5.refs_6_ = bf16[272,768]{1,0:T(8,128)(2,1)S(1)} collective-permute-done((bf16[272,768]{1,0:T(8,128)(2,1)S(1)}, bf16[272,768]{1,0:T(8,128)(2,1)S(1)}, u32[]{:S(2)}, u32[]{:S(2)}) %collective-permute-start.5) | collective-permute-done | bytes 417824 | tf_op jit(solution)/shard_map/ppermute | solution.py:234
  35.8 6.9 %collective-permute-start.12 = (bf16[272,768]{1,0:T(8,128)(2,1)S(1)}, bf16[272,768]{1,0:T(8,128)(2,1)}, u32[]{:S(2)}, u32[]{:S(2)}) collective-permute-start(bf16[272,768]{1,0:T(8,128)(2,1)S(1)} %collective-permute-done.1.refs_2_), channel_id=1, source_target_pairs={{0,1},{1,0},{2,3},{3,2},{4,5},{5,4},{6,7},{7,6},{8,9},{9,8},{10,11... | collective-permute-start | bytes 1253384 | tf_op jit(solution)/shard_map/ppermute | solution.py:235
  42.8 0.7 collective-permute-start.20
  43.5 0.1 copy-done.5
  43.6 0.6 collective-permute-start.14
  44.3 0.1 collective-permute-start.15
  44.4 0.4 collective-permute-start.16
  44.8 0.4 collective-permute-start.19
  45.2 0.2 collective-permute-done.20.refs_21_
  45.4 0.4 collective-permute-start.18
  45.9 0.6 copy-done.9
  46.5 0.7 collective-permute-done.15.refs_16_
  47.2 0.2 collective-permute-done.16.refs_17_
  47.4 0.6 collective-permute-done.19.refs_20_
  48.0 0.6 collective-permute-done.18.refs_19_
  48.6 1.0 %copy-done = bf16[272,768]{1,0:T(8,128)(2,1)S(1)} copy-done((bf16[272,768]{1,0:T(8,128)(2,1)S(1)}, bf16[272,768]{1,0:T(8,128)(2,1)}, u32[]{:S(2)}) %copy-start) | copy-done | bytes 417816
  49.6 1.0 %copy-done.2 = bf16[272,768]{1,0:T(8,128)(2,1)S(1)} copy-done((bf16[272,768]{1,0:T(8,128)(2,1)S(1)}, bf16[272,768]{1,0:T(8,128)(2,1)}, u32[]{:S(2)}) %copy-start.2) | copy-done | bytes 417816
  50.6 1.0 %copy-done.4 = bf16[272,768]{1,0:T(8,128)(2,1)S(1)} copy-done((bf16[272,768]{1,0:T(8,128)(2,1)S(1)}, bf16[272,768]{1,0:T(8,128)(2,1)}, u32[]{:S(2)}) %copy-start.4) | copy-done | bytes 417816
  51.6 1.0 %copy-done.6 = bf16[272,768]{1,0:T(8,128)(2,1)S(1)} copy-done((bf16[272,768]{1,0:T(8,128)(2,1)S(1)}, bf16[272,768]{1,0:T(8,128)(2,1)}, u32[]{:S(2)}) %copy-start.6) | copy-done | bytes 417816
  52.6 22.7 %pair_sums.1 = f32[22,256]{1,0:T(8,128)S(1)} custom-call(s32[1]{0:T(128)} %bitcast.variant_ref, s32[1344]{0:T(1024)S(1)} %copy-done.7, s32[224]{0:T(256)S(1)} %copy-done.8, bf16[272,768]{1,0:T(8,128)(2,1)S(1)} %copy-done, bf16[272,768]{1,0:T(8,128)(2,1)S(1)} %collective-permute-done.refs_1_, bf16[272,768]{1,0:T(8,128)(2,1)S(1)} %collective-permute-done.1.refs_2_, ...), custom_call_target="tpu_custom_call" | custom-call | flops 6543114240 | bytes 8650752 | tf_op jit(solution)/shard_map/pair_sums/pallas_call | solution.py:202
  75.4 0.6 gather_fusion.1
  76.0 0.7 collective-permute-start.21
  76.8 0.6 gather_fusion
  77.3 0.3 collective-permute-done.21
  77.7 3.3 %collective-permute-start.22 = (f32[1,512]{1,0:T(1,128)S(1)}, f32[1,512]{1,0:T(1,128)S(1)}, u32[]{:S(2)}, u32[]{:S(2)}) collective-permute-start(f32[1,512]{1,0:T(1,128)S(1)} %bitcast.35), channel_id=1, source_target_pairs={{0,2},{1,7},{2,4},{3,1},{4,6},{5,3},{6,0},{7,5},{8,10},{9,15},{10,... | collective-permute-start | bytes 6152 | tf_op jit(solution)/shard_map/ppermute | solution.py:256
  81.0 2.3 %collective-permute-start.24 = (f32[1,512]{1,0:T(1,128)S(1)}, f32[1,512]{1,0:T(1,128)S(1)}, u32[]{:S(2)}, u32[]{:S(2)}) collective-permute-start(f32[1,512]{1,0:T(1,128)S(1)} %bitcast.37), channel_id=1, source_target_pairs={{0,18},{1,57},{2,20},{3,59},{4,22},{5,61},{6,16},{7,63},{8,26},{9,... | collective-permute-start | bytes 6152 | tf_op jit(solution)/shard_map/ppermute | solution.py:256
  83.3 1.1 %collective-permute-start.25 = (f32[1,512]{1,0:T(1,128)S(1)}, f32[1,512]{1,0:T(1,128)S(1)}, u32[]{:S(2)}, u32[]{:S(2)}) collective-permute-start(f32[1,512]{1,0:T(1,128)S(1)} %bitcast.38), channel_id=1, source_target_pairs={{0,70},{1,89},{2,64},{3,91},{4,66},{5,93},{6,68},{7,95},{8,78},{9,... | collective-permute-start | bytes 6152 | tf_op jit(solution)/shard_map/ppermute | solution.py:256
  84.4 4.5 %collective-permute-start.26 = (f32[1,512]{1,0:T(1,128)S(1)}, f32[1,512]{1,0:T(1,128)S(1)}, u32[]{:S(2)}, u32[]{:S(2)}) collective-permute-start(f32[1,512]{1,0:T(1,128)S(1)} %bitcast.39), channel_id=1, source_target_pairs={{0,102},{1,127},{2,96},{3,121},{4,98},{5,123},{6,100},{7,125},{8,1... | collective-permute-start | bytes 6152 | tf_op jit(solution)/shard_map/ppermute | solution.py:256
  89.0 0.7 collective-permute-done.26
  89.8 1.7 %collective-permute-start.27 = (f32[256]{0:T(256)S(1)}, f32[256]{0:T(256)S(1)}, u32[]{:S(2)}, u32[]{:S(2)}) collective-permute-start(f32[256]{0:T(256)S(1)} %broadcast_select_fusion.5), channel_id=1, source_target_pairs={{0,1},{1,0},{2,3},{3,2},{4,5},{5,4},{6,7},{7,6},{8,9},{9,8},{10,11... | collective-permute-start | bytes 3080 | tf_op jit(solution)/shard_map/ppermute | solution.py:260
  91.5 0.8 collective-permute-done.27
  92.3 0.6 add_log-plus-one_fusion
  (55 shorter events, 0.5 us)
Async XLA Ops:
  3.5 12.5 %collective-permute-start.2 = (bf16[272,768]{1,0:T(8,128)(2,1)}, bf16[272,768]{1,0:T(8,128)(2,1)S(1)}, u32[]{:S(2)}, u32[]{:S(2)}) collective-permute-start(bf16[272,768]{1,0:T(8,128)(2,1)} %pack.1.refs_0_), channel_id=1, source_target_pairs={{102,0},{11,1},{96,2},{13,3},{98,4},{15,5},{100,6},{9,7},{110,8},{... | collective-permute-start | bytes 1253384 | tf_op jit(solution)/shard_map/ppermute | solution.py:234
  9.3 14.8 %collective-permute-start = (bf16[272,768]{1,0:T(8,128)(2,1)}, bf16[272,768]{1,0:T(8,128)(2,1)S(1)}, u32[]{:S(2)}, u32[]{:S(2)}) collective-permute-start(bf16[272,768]{1,0:T(8,128)(2,1)} %pack.1.refs_0_), channel_id=1, source_target_pairs={{10,0},{103,1},{12,2},{97,3},{14,4},{99,5},{8,6},{101,7},{18,8},{1... | collective-permute-start | bytes 1253384 | tf_op jit(solution)/shard_map/ppermute | solution.py:234
  9.6 15.0 %collective-permute-start.1 = (bf16[272,768]{1,0:T(8,128)(2,1)}, bf16[272,768]{1,0:T(8,128)(2,1)S(1)}, u32[]{:S(2)}, u32[]{:S(2)}) collective-permute-start(bf16[272,768]{1,0:T(8,128)(2,1)} %pack.1.refs_0_), channel_id=1, source_target_pairs={{56,0},{57,1},{58,2},{59,3},{60,4},{61,5},{62,6},{63,7},{32,8},{33... | collective-permute-start | bytes 1253384 | tf_op jit(solution)/shard_map/ppermute | solution.py:234
  11.5 13.7 %collective-permute-start.6 = (bf16[272,768]{1,0:T(8,128)(2,1)}, bf16[272,768]{1,0:T(8,128)(2,1)S(1)}, u32[]{:S(2)}, u32[]{:S(2)}) collective-permute-start(bf16[272,768]{1,0:T(8,128)(2,1)} %pack.1.refs_0_), channel_id=1, source_target_pairs={{6,0},{3,1},{0,2},{5,3},{2,4},{7,5},{4,6},{1,7},{14,8},{11,9},{8,1... | collective-permute-start | bytes 1253384 | tf_op jit(solution)/shard_map/ppermute | solution.py:234
  13.3 15.6 %collective-permute-start.9 = (bf16[272,768]{1,0:T(8,128)(2,1)}, bf16[272,768]{1,0:T(8,128)(2,1)S(1)}, u32[]{:S(2)}, u32[]{:S(2)}) collective-permute-start(bf16[272,768]{1,0:T(8,128)(2,1)} %pack.1.refs_0_), channel_id=1, source_target_pairs={{8,0},{7,1},{10,2},{1,3},{12,4},{3,5},{14,6},{5,7},{16,8},{15,9},{... | collective-permute-start | bytes 1253384 | tf_op jit(solution)/shard_map/ppermute | solution.py:234
  16.0 14.2 %collective-permute-start.10 = (bf16[272,768]{1,0:T(8,128)(2,1)}, bf16[272,768]{1,0:T(8,128)(2,1)S(1)}, u32[]{:S(2)}, u32[]{:S(2)}) collective-permute-start(bf16[272,768]{1,0:T(8,128)(2,1)} %pack.1.refs_0_), channel_id=1, source_target_pairs={{0,1},{1,0},{2,3},{3,2},{4,5},{5,4},{6,7},{7,6},{8,9},{9,8},{10,11... | collective-permute-start | bytes 1253384 | tf_op jit(solution)/shard_map/ppermute | solution.py:235
  24.1 7.7 %collective-permute-start.3 = (bf16[272,768]{1,0:T(8,128)(2,1)S(1)}, bf16[272,768]{1,0:T(8,128)(2,1)S(1)}, u32[]{:S(2)}, u32[]{:S(2)}) collective-permute-start(bf16[272,768]{1,0:T(8,128)(2,1)S(1)} %collective-permute-done.2.refs_3_), channel_id=1, source_target_pairs={{96,0},{9,1},{98,2},{11,3},{100,4},{13,5},{102,6},{15,7},{104,8},{... | collective-permute-start | bytes 1253384 | tf_op jit(solution)/shard_map/ppermute | solution.py:234
  24.6 9.3 %collective-permute-start.4 = (bf16[272,768]{1,0:T(8,128)(2,1)S(1)}, bf16[272,768]{1,0:T(8,128)(2,1)S(1)}, u32[]{:S(2)}, u32[]{:S(2)}) collective-permute-start(bf16[272,768]{1,0:T(8,128)(2,1)S(1)} %collective-permute-done.2.refs_3_), channel_id=1, source_target_pairs={{24,0},{7,1},{26,2},{1,3},{28,4},{3,5},{30,6},{5,7},{0,8},{15,9},{... | collective-permute-start | bytes 1253384 | tf_op jit(solution)/shard_map/ppermute | solution.py:234
  25.2 10.6 %collective-permute-start.5 = (bf16[272,768]{1,0:T(8,128)(2,1)S(1)}, bf16[272,768]{1,0:T(8,128)(2,1)S(1)}, u32[]{:S(2)}, u32[]{:S(2)}) collective-permute-start(bf16[272,768]{1,0:T(8,128)(2,1)S(1)} %collective-permute-done.refs_1_), channel_id=1, source_target_pairs={{24,0},{97,1},{26,2},{99,3},{28,4},{101,5},{30,6},{103,7},{0,8},{1... | collective-permute-start | bytes 1253384 | tf_op jit(solution)/shard_map/ppermute | solution.py:234
  28.9 13.8 %collective-permute-start.8 = (bf16[272,768]{1,0:T(8,128)(2,1)S(1)}, bf16[272,768]{1,0:T(8,128)(2,1)S(1)}, u32[]{:S(2)}, u32[]{:S(2)}) collective-permute-start(bf16[272,768]{1,0:T(8,128)(2,1)S(1)} %collective-permute-done.refs_1_), channel_id=1, source_target_pairs={{8,0},{25,1},{10,2},{27,3},{12,4},{29,5},{14,6},{31,7},{16,8},{1,9... | collective-permute-start | bytes 1253384 | tf_op jit(solution)/shard_map/ppermute | solution.py:234
  30.2 12.6 %collective-permute-start.7 = (bf16[272,768]{1,0:T(8,128)(2,1)S(1)}, bf16[272,768]{1,0:T(8,128)(2,1)S(1)}, u32[]{:S(2)}, u32[]{:S(2)}) collective-permute-start(bf16[272,768]{1,0:T(8,128)(2,1)S(1)} %collective-permute-done.1.refs_2_), channel_id=1, source_target_pairs={{32,0},{33,1},{34,2},{35,3},{36,4},{37,5},{38,6},{39,7},{40,8},{41... | collective-permute-start | bytes 1253384 | tf_op jit(solution)/shard_map/ppermute | solution.py:234
  31.8 11.8 %collective-permute-start.11 = (bf16[272,768]{1,0:T(8,128)(2,1)S(1)}, bf16[272,768]{1,0:T(8,128)(2,1)}, u32[]{:S(2)}, u32[]{:S(2)}) collective-permute-start(bf16[272,768]{1,0:T(8,128)(2,1)S(1)} %collective-permute-done.refs_1_), channel_id=1, source_target_pairs={{0,1},{1,0},{2,3},{3,2},{4,5},{5,4},{6,7},{7,6},{8,9},{9,8},{10,11... | collective-permute-start | bytes 1253384 | tf_op jit(solution)/shard_map/ppermute | solution.py:235
  33.9 10.3 %collective-permute-start.13 = (bf16[272,768]{1,0:T(8,128)(2,1)S(1)}, bf16[272,768]{1,0:T(8,128)(2,1)}, u32[]{:S(2)}, u32[]{:S(2)}) collective-permute-start(bf16[272,768]{1,0:T(8,128)(2,1)S(1)} %collective-permute-done.2.refs_3_), channel_id=1, source_target_pairs={{0,1},{1,0},{2,3},{3,2},{4,5},{5,4},{6,7},{7,6},{8,9},{9,8},{10,11... | collective-permute-start | bytes 1253384 | tf_op jit(solution)/shard_map/ppermute | solution.py:235
  35.8 7.0 %copy-start.1 = (bf16[272,768]{1,0:T(8,128)(2,1)}, bf16[272,768]{1,0:T(8,128)(2,1)S(1)}, u32[]{:S(2)}) copy-start(bf16[272,768]{1,0:T(8,128)(2,1)S(1)} %collective-permute-done.5.refs_6_) | copy-start | bytes 1253380
  35.8 8.5 %collective-permute-start.12 = (bf16[272,768]{1,0:T(8,128)(2,1)S(1)}, bf16[272,768]{1,0:T(8,128)(2,1)}, u32[]{:S(2)}, u32[]{:S(2)}) collective-permute-start(bf16[272,768]{1,0:T(8,128)(2,1)S(1)} %collective-permute-done.1.refs_2_), channel_id=1, source_target_pairs={{0,1},{1,0},{2,3},{3,2},{4,5},{5,4},{6,7},{7,6},{8,9},{9,8},{10,11... | collective-permute-start | bytes 1253384 | tf_op jit(solution)/shard_map/ppermute | solution.py:235
  42.7 0.8 copy-start.3
  42.7 2.1 %collective-permute-start.17 = (bf16[272,768]{1,0:T(8,128)(2,1)S(1)}, bf16[272,768]{1,0:T(8,128)(2,1)}, u32[]{:S(2)}, u32[]{:S(2)}) collective-permute-start(bf16[272,768]{1,0:T(8,128)(2,1)S(1)} %collective-permute-done.6.refs_7_), channel_id=1, source_target_pairs={{0,1},{1,0},{2,3},{3,2},{4,5},{5,4},{6,7},{7,6},{8,9},{9,8},{10,11... | collective-permute-start | bytes 1253384 | tf_op jit(solution)/shard_map/ppermute | solution.py:235
  42.8 0.8 copy-start.5
  42.8 2.6 %collective-permute-start.20 = (bf16[272,768]{1,0:T(8,128)(2,1)S(1)}, bf16[272,768]{1,0:T(8,128)(2,1)}, u32[]{:S(2)}, u32[]{:S(2)}) collective-permute-start(bf16[272,768]{1,0:T(8,128)(2,1)S(1)} %collective-permute-done.9.refs_10_), channel_id=1, source_target_pairs={{0,1},{1,0},{2,3},{3,2},{4,5},{5,4},{6,7},{7,6},{8,9},{9,8},{10,11... | collective-permute-start | bytes 1253384 | tf_op jit(solution)/shard_map/ppermute | solution.py:235
  43.6 2.2 %copy-start.11 = (s32[10]{0:T(128)S(1)}, s32[10]{0:T(128)}, u32[]{:S(2)}) copy-start(s32[10]{0:T(128)} %constant.49.clone) | copy-start | bytes 124
  43.6 2.2 %copy-start.12 = (s32[10]{0:T(128)S(1)}, s32[10]{0:T(128)}, u32[]{:S(2)}) copy-start(s32[10]{0:T(128)} %constant.50.clone) | copy-start | bytes 124
  43.6 2.9 %collective-permute-start.14 = (bf16[272,768]{1,0:T(8,128)(2,1)S(1)}, bf16[272,768]{1,0:T(8,128)(2,1)}, u32[]{:S(2)}, u32[]{:S(2)}) collective-permute-start(bf16[272,768]{1,0:T(8,128)(2,1)S(1)} %collective-permute-done.3.refs_4_), channel_id=1, source_target_pairs={{0,1},{1,0},{2,3},{3,2},{4,5},{5,4},{6,7},{7,6},{8,9},{9,8},{10,11... | collective-permute-start | bytes 1253384 | tf_op jit(solution)/shard_map/ppermute | solution.py:235
  44.3 2.9 %collective-permute-start.15 = (bf16[272,768]{1,0:T(8,128)(2,1)S(1)}, bf16[272,768]{1,0:T(8,128)(2,1)}, u32[]{:S(2)}, u32[]{:S(2)}) collective-permute-start(bf16[272,768]{1,0:T(8,128)(2,1)S(1)} %collective-permute-done.4.refs_5_), channel_id=1, source_target_pairs={{0,1},{1,0},{2,3},{3,2},{4,5},{5,4},{6,7},{7,6},{8,9},{9,8},{10,11... | collective-permute-start | bytes 1253384 | tf_op jit(solution)/shard_map/ppermute | solution.py:235
  44.4 3.0 %collective-permute-start.16 = (bf16[272,768]{1,0:T(8,128)(2,1)}, bf16[272,768]{1,0:T(8,128)(2,1)}, u32[]{:S(2)}, u32[]{:S(2)}) collective-permute-start(bf16[272,768]{1,0:T(8,128)(2,1)} %copy-done.1), channel_id=1, source_target_pairs={{0,1},{1,0},{2,3},{3,2},{4,5},{5,4},{6,7},{7,6},{8,9},{9,8},{10,11... | collective-permute-start | bytes 1253384 | tf_op jit(solution)/shard_map/ppermute | solution.py:235
  44.8 3.2 %collective-permute-start.19 = (bf16[272,768]{1,0:T(8,128)(2,1)}, bf16[272,768]{1,0:T(8,128)(2,1)}, u32[]{:S(2)}, u32[]{:S(2)}) collective-permute-start(bf16[272,768]{1,0:T(8,128)(2,1)} %copy-done.3), channel_id=1, source_target_pairs={{0,1},{1,0},{2,3},{3,2},{4,5},{5,4},{6,7},{7,6},{8,9},{9,8},{10,11... | collective-permute-start | bytes 1253384 | tf_op jit(solution)/shard_map/ppermute | solution.py:235
  45.4 3.2 %collective-permute-start.18 = (bf16[272,768]{1,0:T(8,128)(2,1)}, bf16[272,768]{1,0:T(8,128)(2,1)}, u32[]{:S(2)}, u32[]{:S(2)}) collective-permute-start(bf16[272,768]{1,0:T(8,128)(2,1)} %copy-done.5), channel_id=1, source_target_pairs={{0,1},{1,0},{2,3},{3,2},{4,5},{5,4},{6,7},{7,6},{8,9},{9,8},{10,11... | collective-permute-start | bytes 1253384 | tf_op jit(solution)/shard_map/ppermute | solution.py:235
  45.8 2.8 %copy-start.7 = (s32[1344]{0:T(1024)S(1)}, s32[1344]{0:T(1024)}, u32[]{:S(2)}) copy-start(s32[1344]{0:T(1024)} %constant.45.clone.wide_ref) | copy-start | bytes 16132
  45.8 0.7 copy-start.9
  45.8 0.7 copy-start.10
  46.5 2.1 %copy-start.8 = (s32[224]{0:T(256)S(1)}, s32[224]{0:T(256)}, u32[]{:S(2)}) copy-start(s32[224]{0:T(256)} %constant.46.clone.narrow_ref) | copy-start | bytes 2692
  48.6 1.0 %copy-start = (bf16[272,768]{1,0:T(8,128)(2,1)S(1)}, bf16[272,768]{1,0:T(8,128)(2,1)}, u32[]{:S(2)}) copy-start(bf16[272,768]{1,0:T(8,128)(2,1)} %pack.1.refs_0_) | copy-start | bytes 1253380
  49.6 1.0 %copy-start.2 = (bf16[272,768]{1,0:T(8,128)(2,1)S(1)}, bf16[272,768]{1,0:T(8,128)(2,1)}, u32[]{:S(2)}) copy-start(bf16[272,768]{1,0:T(8,128)(2,1)} %copy-done.1) | copy-start | bytes 1253380
  50.6 1.0 %copy-start.4 = (bf16[272,768]{1,0:T(8,128)(2,1)S(1)}, bf16[272,768]{1,0:T(8,128)(2,1)}, u32[]{:S(2)}) copy-start(bf16[272,768]{1,0:T(8,128)(2,1)} %copy-done.3) | copy-start | bytes 1253380
  51.6 1.0 %copy-start.6 = (bf16[272,768]{1,0:T(8,128)(2,1)S(1)}, bf16[272,768]{1,0:T(8,128)(2,1)}, u32[]{:S(2)}) copy-start(bf16[272,768]{1,0:T(8,128)(2,1)} %copy-done.5) | copy-start | bytes 1253380
  76.0 1.6 %collective-permute-start.21 = (f32[10,256]{1,0:T(8,128)S(1)}, f32[10,256]{1,0:T(8,128)S(1)}, u32[]{:S(2)}, u32[]{:S(2)}) collective-permute-start(f32[10,256]{1,0:T(8,128)S(1)} %broadcast_select_fusion), channel_id=1, source_target_pairs={{0,1},{1,0},{2,3},{3,2},{4,5},{5,4},{6,7},{7,6},{8,9},{9,8},{10,11... | collective-permute-start | bytes 30728 | tf_op jit(solution)/shard_map/ppermute | solution.py:252
  77.7 11.3 %collective-permute-start.22 = (f32[1,512]{1,0:T(1,128)S(1)}, f32[1,512]{1,0:T(1,128)S(1)}, u32[]{:S(2)}, u32[]{:S(2)}) collective-permute-start(f32[1,512]{1,0:T(1,128)S(1)} %bitcast.35), channel_id=1, source_target_pairs={{0,2},{1,7},{2,4},{3,1},{4,6},{5,3},{6,0},{7,5},{8,10},{9,15},{10,... | collective-permute-start | bytes 6152 | tf_op jit(solution)/shard_map/ppermute | solution.py:256
  81.0 8.0 %collective-permute-start.23 = (f32[1,512]{1,0:T(1,128)S(1)}, f32[1,512]{1,0:T(1,128)S(1)}, u32[]{:S(2)}, u32[]{:S(2)}) collective-permute-start(f32[1,512]{1,0:T(1,128)S(1)} %bitcast.36), channel_id=1, source_target_pairs={{0,8},{1,11},{2,10},{3,13},{4,12},{5,15},{6,14},{7,9},{8,16},{9,19... | collective-permute-start | bytes 6152 | tf_op jit(solution)/shard_map/ppermute | solution.py:256
  81.0 8.0 %collective-permute-start.24 = (f32[1,512]{1,0:T(1,128)S(1)}, f32[1,512]{1,0:T(1,128)S(1)}, u32[]{:S(2)}, u32[]{:S(2)}) collective-permute-start(f32[1,512]{1,0:T(1,128)S(1)} %bitcast.37), channel_id=1, source_target_pairs={{0,18},{1,57},{2,20},{3,59},{4,22},{5,61},{6,16},{7,63},{8,26},{9,... | collective-permute-start | bytes 6152 | tf_op jit(solution)/shard_map/ppermute | solution.py:256
  83.3 5.7 %collective-permute-start.25 = (f32[1,512]{1,0:T(1,128)S(1)}, f32[1,512]{1,0:T(1,128)S(1)}, u32[]{:S(2)}, u32[]{:S(2)}) collective-permute-start(f32[1,512]{1,0:T(1,128)S(1)} %bitcast.38), channel_id=1, source_target_pairs={{0,70},{1,89},{2,64},{3,91},{4,66},{5,93},{6,68},{7,95},{8,78},{9,... | collective-permute-start | bytes 6152 | tf_op jit(solution)/shard_map/ppermute | solution.py:256
  84.4 5.3 %collective-permute-start.26 = (f32[1,512]{1,0:T(1,128)S(1)}, f32[1,512]{1,0:T(1,128)S(1)}, u32[]{:S(2)}, u32[]{:S(2)}) collective-permute-start(f32[1,512]{1,0:T(1,128)S(1)} %bitcast.39), channel_id=1, source_target_pairs={{0,102},{1,127},{2,96},{3,121},{4,98},{5,123},{6,100},{7,125},{8,1... | collective-permute-start | bytes 6152 | tf_op jit(solution)/shard_map/ppermute | solution.py:256
  89.8 2.5 %collective-permute-start.27 = (f32[256]{0:T(256)S(1)}, f32[256]{0:T(256)S(1)}, u32[]{:S(2)}, u32[]{:S(2)}) collective-permute-start(f32[256]{0:T(256)S(1)} %broadcast_select_fusion.5), channel_id=1, source_target_pairs={{0,1},{1,0},{2,3},{3,2},{4,5},{5,4},{6,7},{7,6},{8,9},{9,8},{10,11... | collective-permute-start | bytes 3080 | tf_op jit(solution)/shard_map/ppermute | solution.py:260

commit v2 on v0

v2 whole, which is shorter than its diff:
```python
import functools
import math

import jax
import jax.numpy as jnp
import numpy as np
from jax import lax
from jax.experimental import pallas as pl
from jax.experimental.pallas import tpu as pltpu
from jax.sharding import PartitionSpec as P

sharpness = 30.0
EXP2_SCALE = sharpness * math.log2(math.e)
ROWS, WIDTH, LABEL_ROWS, LANES = 256, 768, 16, 128
BOTH = ("cluster", "member")
CLUSTER_SHIFT = 5

PLAN = ((0, 5), (0, 60), (0, 17), (0, 3), (2, 3), (3, 12), (4, 16), (1, 48), (4, 4), (3, 4))
SWAPPED = 7
BLOCKS = len(PLAN) + 1
PHASES = ((5, 5), (BLOCKS, SWAPPED))


def shift(place, by):
    return sum(((place >> s) + (by >> s) & 3) << s for s in (0, 2, 4))


def minus(place):
    return sum((-(place >> s) & 3) << s for s in (0, 2, 4))


def mirror(place, core=1):
    return place & 3 | (place >> 4) << 2 | (place >> 2 & 3) << 4 if core else place


def device(place, core):
    x, y, z = place & 3, place >> 2 & 3, place >> 4
    return ((z * 4 + y) * 4 + x) * 2 + core


def fetch(jumps):
    return [(device(shift(p, jumps[c]), c), device(p, c)) for p in range(64) for c in (0, 1)]


def give(jumps):
    return [(b, a) for a, b in fetch(jumps)]


CORE_SWAP = [(d, d ^ 1) for d in range(128)]


def held_offsets():
    held = [0]
    for source, jump in PLAN:
        held.append(shift(held[source], jump))
    return held


HELD = held_offsets()
assert len(set(HELD)) == BLOCKS and {mirror(o) for o in HELD} == set(HELD)


def units():
    lists, seen = [], set()
    for mine, other in PHASES:
        found = [("self", 0, True, 0, None)] if not lists else []
        for b in range(mine):
            for a in range(b):
                d = shift(HELD[a], minus(HELD[b]))
                if (0, d) not in seen:
                    seen.update({(0, d), (0, minus(d))})
                    axis = next((i for i in range(3) if d >> (2 * i) & 3 == 2), None)
                    found.append(("full" if d != minus(d) else "half", a, True, b, axis))
        for b in range(other):
            for a in range(mine):
                d = shift(HELD[a], minus(mirror(HELD[b])))
                if (1, d) not in seen:
                    seen.update({(1, d), (1, minus(mirror(d)))})
                    found.append(("full" if d != minus(mirror(d)) else "half", a, False, b, None))
        lists.append(sorted(found, key=lambda unit: unit[1]))
    assert len(seen) == 63 + 64
    return lists


UNITS = units()


def pack_body(rows_ref, target_ref, out_ref):
    vectors = rows_ref[...].astype(jnp.float32)
    norms = jnp.sum(vectors * vectors, axis=1, keepdims=True)
    out_ref[0:ROWS, :] = (vectors * lax.rsqrt(norms + 1e-06)).astype(jnp.bfloat16)
    labels = (target_ref[...] >> CLUSTER_SHIFT).astype(jnp.float32)
    out_ref[ROWS:, 0:ROWS] = jnp.broadcast_to(labels, (LABEL_ROWS, ROWS)).astype(jnp.bfloat16)
    out_ref[ROWS:, ROWS:] = jnp.zeros((LABEL_ROWS, WIDTH - ROWS), jnp.bfloat16)


def pack(embeddings, destination):
    return pl.pallas_call(
        pack_body,
        out_shape=jax.ShapeDtypeStruct((ROWS + LABEL_ROWS, WIDTH), jnp.bfloat16),
        name="pack",
    )(embeddings, destination.reshape(1, ROWS))


def parts(start=0):
    return [slice(start + s, start + s + LANES) for s in range(0, ROWS - start, LANES)]


def pairs_body(work, mine_used, other_used, earlier, place_ref, *refs):
    count = len(mine_used) + len(other_used)
    mine = dict(zip(mine_used, refs))
    other = dict(zip(other_used, refs[len(mine_used) : count]))
    before_ref = refs[count] if earlier else None
    out_ref, labels_ref, row_sums, column_sums = refs[count + earlier :]
    firsts = sorted({a for _, a, *_ in work})
    at = {a: n for n, a in enumerate(firsts)}
    row_sums[...] = jnp.zeros_like(row_sums)
    column_sums[...] = jnp.zeros_like(column_sums)

    def row_labels(ref):
        return ref[ROWS:, 0:ROWS].astype(jnp.float32)[0:1]

    for a in firsts:
        labels = row_labels(mine[a])
        for part in parts():
            labels_ref[at[a], part, :] = jnp.broadcast_to(labels[:, part], (LANES, LANES)).T

    def weights(a, a_rows, b_ref, b_rows, b_labels):
        scores = lax.dot_general(
            mine[a][a_rows], b_ref[b_rows], (((1,), (1,)), ((), ())), preferred_element_type=jnp.float32
        )
        left = labels_ref[at[a], a_rows, :]
        return [
            jnp.where(left == right, jnp.exp2(scores[:, n * LANES : (n + 1) * LANES] * EXP2_SCALE), 0.0)
            for n, right in enumerate(b_labels)
        ]

    def down(value):
        return jnp.sum(value.reshape(-1, 8, LANES), axis=0)

    for kind, a, is_mine, b, axis in work:
        b_ref = mine[b] if is_mine else other[b]
        slot = b if is_mine else BLOCKS + b
        labels = row_labels(b_ref)
        everything = slice(0, ROWS)
        if kind == "half":
            low, high = parts()
            (value,) = weights(a, low, b_ref, high, [labels[:, high]])
            row_sums[at[a], low, :] += value
            column_sums[slot, :, high] += down(value)
            which = place_ref[0] if axis is None else place_ref[1 + axis]
            same = pl.ds(pl.multiple_of(which * LANES, LANES), LANES)
            chosen = jnp.where(which == 0, labels[:, low], labels[:, high])
            (value,) = weights(a, same, b_ref, same, [chosen])
            row_sums[at[a], same, :] += value
            column_sums[slot, :, same] += down(value)
            continue
        values = weights(a, everything, b_ref, everything, [labels[:, part] for part in parts()])
        if kind == "self":
            rows = lax.broadcasted_iota(jnp.int32, (ROWS, LANES), 0)
            lanes = lax.broadcasted_iota(jnp.int32, (ROWS, LANES), 1)
            values = [jnp.where(rows == lanes + n * LANES, 0.0, value) for n, value in enumerate(values)]
        else:
            for part, value in zip(parts(), values):
                column_sums[slot, :, part] += down(value)
        row_sums[at[a]] += values[0] + values[1]

    for slot in range(2 * BLOCKS):
        for part in parts():
            total = jnp.sum(column_sums[slot, :, part], axis=0, keepdims=True)
            if slot in at:
                total += jnp.sum(row_sums[at[slot], part, :].T, axis=0, keepdims=True)
            if earlier:
                total += before_ref[slot : slot + 1, part]
            out_ref[slot : slot + 1, part] = total


def pair_sums(phase, place, mine, other, before):
    work = UNITS[phase]
    mine_used = sorted({a for _, a, *_ in work} | {b for _, _, is_mine, b, _ in work if is_mine})
    other_used = sorted({b for _, _, is_mine, b, _ in work if not is_mine})
    blocks = [mine[k] for k in mine_used] + [other[k] for k in other_used]
    blocks = [pltpu.with_memory_space_constraint(block, pltpu.VMEM) for block in blocks]
    before = [] if before is None else [before]
    smem, vmem = pl.BlockSpec(memory_space=pltpu.SMEM), pl.BlockSpec(memory_space=pltpu.VMEM)
    firsts = len({a for _, a, *_ in work})
    area = sum(ROWS * ROWS // (2 if kind == "half" else 1) for kind, *_ in work)
    return pl.pallas_call(
        functools.partial(pairs_body, work, mine_used, other_used, len(before)),
        out_shape=jax.ShapeDtypeStruct((2 * BLOCKS, ROWS), jnp.float32),
        in_specs=[smem] + [vmem] * (len(blocks) + len(before)),
        out_specs=vmem,
        scratch_shapes=[
            pltpu.VMEM((firsts, ROWS, LANES), jnp.float32),
            pltpu.VMEM((firsts, ROWS, LANES), jnp.float32),
            pltpu.VMEM((2 * BLOCKS, 8, ROWS), jnp.float32),
        ],
        compiler_params=pltpu.CompilerParams(vmem_limit_bytes=24 * 1024 * 1024),
        cost_estimate=pl.CostEstimate(flops=2 * area * WIDTH, bytes_accessed=0, transcendentals=area),
        name=f"pair_sums_{phase}",
    )(place, *blocks, *before)


def shards(embeddings, destination):
    member = lax.axis_index("member")
    core = member & 1
    chip = (member >> 1) + 16 * lax.axis_index("cluster")
    x, y, z = (chip >> s & 1 for s in (1, 3, 5))
    place = jnp.stack([core, x, jnp.where(core == 0, y, z), jnp.where(core == 0, z, y)]).astype(jnp.int32)

    mine = [pack(embeddings, destination)]
    for source, jump in PLAN:
        mine.append(lax.ppermute(mine[source], BOTH, fetch((jump, mirror(jump)))))
    other = [lax.ppermute(block, BOTH, CORE_SWAP) for block in mine[:SWAPPED]]
    sums = None
    for phase in range(len(PHASES)):
        sums = pair_sums(phase, place, mine, other, sums)

    offsets = sorted(HELD)[1:]
    shares = [offsets[0::2], offsets[1::2]]

    def rows_of(share_of):
        by_core = []
        for c in (0, 1):
            places = [(mirror(o, c), mirror(o, 1 - c)) for o in share_of(c)]
            slots = [(HELD.index(a), BLOCKS + HELD.index(b)) for a, b in places]
            by_core.append(np.array([pair[::-1] if c else pair for pair in slots], np.int32).reshape(-1))
        index = jnp.where(core == 0, jnp.asarray(by_core[0]), jnp.asarray(by_core[1]))
        return jnp.take(sums, index, axis=0)

    kept = rows_of(lambda c: shares[c])
    given = rows_of(lambda c: shares[1 - c])
    kept = (kept + lax.ppermute(given, BOTH, CORE_SWAP)).reshape(-1, 2 * ROWS)
    total = jnp.where(core == 0, jnp.stack([sums[0], sums[BLOCKS]]), jnp.stack([sums[BLOCKS], sums[0]])).reshape(-1)
    for k in range(len(shares[0])):
        total += lax.ppermute(kept[k : k + 1], BOTH, give((shares[0][k], shares[1][k])))[0]
    total = total.reshape(2, ROWS)
    own = jnp.where(core == 0, total[0], total[1])
    rest = jnp.where(core == 0, total[1], total[0])
    density = own + lax.ppermute(rest, BOTH, CORE_SWAP)
    return jnp.log1p(density)


def solution(mesh):
    in_specs = (P(BOTH, None), P(BOTH, None))
    return jax.shard_map(shards, mesh=mesh, in_specs=in_specs, out_specs=P(BOTH), check_vma=False)
```

time: 195 us -> 75.3 us (0.39)
  blocking collectives: 67.3 us -> 0 us
  starting transfers between devices: 4.42 us -> 43.4 us
  waiting for transfers between devices: 49.3 us -> 14.3 us
  local copies, waits for them, and re-layouts: 31.3 us -> 2.82 us
  matrix products: 24.2 us -> 0 us
  Pallas kernels: 0 us -> 13.6 us
  between operations: 13.5 us -> 0.18 us
  other arithmetic: 4.55 us -> 0.85 us
    all_to_all x2 -> x0, blocking collectives: 44.5 us -> none  [the longest x1 27.8 us: shards(): lax.all_to_all(send_units, ('cluster', 'member'), split_axis=0, concat_ax...]
    ppermute x0 -> x24, starting transfers between devices: none -> 43.4 us  [the longest x10 18 us: shards(): mine.append(lax.ppermute(mine[source], BOTH, fetch((jump, mirror(jump)))))]
    all_gather x1 -> x0, waiting for transfers between devices: 39.4 us -> none  [shards(): piece_units = lax.all_gather(local_units, 'member', axis=0, tiled=True)]
    scatter x2 -> x0, local copies, waits for them, and re-layouts: 25.6 us -> none  [the longest x1 14.2 us: shards(): send_units = jnp.zeros((device_count, capacity, features), jnp.bfloat16)....]
    dot_general x1 -> x0, matrix products: 24.2 us -> none  [pair_weights(): lax.dot_general(left_units, right_units, (((1,), (1,)), ((), ())), prefer...]
    all_gather x1 -> x0, blocking collectives: 22.8 us -> none  [shards(): piece_labels = lax.all_gather(wire_labels, 'member', axis=0, tiled=True)]
    ppermute x0 -> x24, waiting for transfers between devices: none -> 14.3 us  [the longest x10 12.2 us: shards(): mine.append(lax.ppermute(mine[source], BOTH, fetch((jump, mirror(jump)))))]
    pallas_call x0 -> x3, Pallas kernels: none -> 13.6 us  [the longest x2 11.6 us: pair_sums(): pl.pallas_call(functools.partial(pairs_body, work, mine_used, other_used,...]
  transfers between devices with their start and end apart: 2 -> 24, of which waited for: 2 -> 8; matrix products, arithmetic and copies ran while one was open for 7% -> 1% of each run, Pallas kernels for 0% -> 5%
where the time goes in v2:
time: 75.3 us; the launch traced here: 75.1 us
  starting transfers between devices  43.4 us (58%)
  waiting for transfers between devices  14.3 us (19%)
  Pallas kernels  13.6 us (18%)
  local copies, waits for them, and re-layouts  2.82 us (4%)
  other arithmetic  0.85 us (1%)
    ppermute x10, starting transfers between devices, shards(): mine.append(lax.ppermute(mine[source], BOTH, fetch((jump, mirror(jump)))))  18 us
    ppermute x5, starting transfers between devices, shards(): lax.ppermute(kept[k:k + 1], BOTH, give((shares[0][k], shares[1][k])))[0]  12.3 us
    ppermute x10, waiting for transfers between devices, shards(): mine.append(lax.ppermute(mine[source], BOTH, fetch((jump, mirror(jump)))))  12.2 us
    pallas_call x2, Pallas kernels, pair_sums(): pl.pallas_call(functools.partial(pairs_body, work, mine_used, other_used,...  11.6 us
    ppermute x7, starting transfers between devices, shards(): other = [lax.ppermute(block, BOTH, CORE_SWAP) for block in mine[:SWAPPED]]  11 us
    ppermute x1, starting transfers between devices, shards(): kept = (kept + lax.ppermute(given, BOTH, CORE_SWAP)).reshape(-1, 2 * ROWS)  2.08 us
    pallas_call x1, Pallas kernels, pack(): pl.pallas_call(pack_body, out_shape=jax.ShapeDtypeStruct((ROWS + LABEL_RO...  1.91 us
    unnamed x19, local copies, waits for them, and re-layouts  1.69 us
  transfers between devices with their start and end apart: 24, of which 8 were waited for; matrix products, arithmetic and copies ran while one was open for 1% of the time, Pallas kernels for 5%

profile of v2, /device:TPU:1, one launch (start us, length us, event | category | flops | bytes accessed | tf_op | source)
XLA Modules:
  0.0 75.1 jit_solution(4587590699194801943)
XLA Ops:
  0.0 1.9 %pack.1.refs_0_ = bf16[272,768]{1,0:T(8,128)(2,1)} custom-call(bf16[256,768]{1,0:T(8,128)(2,1)} %rows_ref.1, s32[1,256]{1,0:T(1,128)} %bitcast.44), custom_call_target="tpu_custom_call" | custom-call | tf_op jit(solution)/shard_map/pack/pallas_call | solution.py:98
  1.9 5.8 %collective-permute-start.2 = (bf16[272,768]{1,0:T(8,128)(2,1)}, bf16[272,768]{1,0:T(8,128)(2,1)S(1)}, u32[]{:S(2)}, u32[]{:S(2)}) collective-permute-start(bf16[272,768]{1,0:T(8,128)(2,1)} %pack.1.refs_0_), channel_id=1, source_target_pairs={{34,0},{11,1},{36,2},{13,3},{38,4},{15,5},{32,6},{9,7},{42,8},{19,... | collective-permute-start | bytes 1253384 | tf_op jit(solution)/shard_map/ppermute | solution.py:213
  7.7 4.0 %collective-permute-start = (bf16[272,768]{1,0:T(8,128)(2,1)}, bf16[272,768]{1,0:T(8,128)(2,1)S(1)}, u32[]{:S(2)}, u32[]{:S(2)}) collective-permute-start(bf16[272,768]{1,0:T(8,128)(2,1)} %pack.1.refs_0_), channel_id=1, source_target_pairs={{10,0},{35,1},{12,2},{37,3},{14,4},{39,5},{8,6},{33,7},{18,8},{43,... | collective-permute-start | bytes 1253384 | tf_op jit(solution)/shard_map/ppermute | solution.py:213
  11.7 0.0 collective-permute-start.1
  11.7 0.9 %collective-permute-start.3 = (bf16[272,768]{1,0:T(8,128)(2,1)}, bf16[272,768]{1,0:T(8,128)(2,1)S(1)}, u32[]{:S(2)}, u32[]{:S(2)}) collective-permute-start(bf16[272,768]{1,0:T(8,128)(2,1)} %pack.1.refs_0_), channel_id=1, source_target_pairs={{6,0},{7,1},{0,2},{1,3},{2,4},{3,5},{4,6},{5,7},{14,8},{15,9},{8,1... | collective-permute-start | bytes 1253384 | tf_op jit(solution)/shard_map/ppermute | solution.py:213
  12.6 1.5 %collective-permute-start.10 = (bf16[272,768]{1,0:T(8,128)(2,1)}, bf16[272,768]{1,0:T(8,128)(2,1)S(1)}, u32[]{:S(2)}, u32[]{:S(2)}) collective-permute-start(bf16[272,768]{1,0:T(8,128)(2,1)} %pack.1.refs_0_), channel_id=1, source_target_pairs={{0,1},{1,0},{2,3},{3,2},{4,5},{5,4},{6,7},{7,6},{8,9},{9,8},{10,11... | collective-permute-start | bytes 1253384 | tf_op jit(solution)/shard_map/ppermute | solution.py:214
  14.1 1.1 %collective-permute-done.2.refs_3_ = bf16[272,768]{1,0:T(8,128)(2,1)S(1)} collective-permute-done((bf16[272,768]{1,0:T(8,128)(2,1)}, bf16[272,768]{1,0:T(8,128)(2,1)S(1)}, u32[]{:S(2)}, u32[]{:S(2)}) %collective-permute-start.2) | collective-permute-done | bytes 417824 | tf_op jit(solution)/shard_map/ppermute | solution.py:213
  15.2 4.8 %collective-permute-start.13 = (bf16[272,768]{1,0:T(8,128)(2,1)S(1)}, bf16[272,768]{1,0:T(8,128)(2,1)S(1)}, u32[]{:S(2)}, u32[]{:S(2)}) collective-permute-start(bf16[272,768]{1,0:T(8,128)(2,1)S(1)} %collective-permute-done.2.refs_3_), channel_id=1, source_target_pairs={{0,1},{1,0},{2,3},{3,2},{4,5},{5,4},{6,7},{7,6},{8,9},{9,8},{10,11... | collective-permute-start | bytes 1253384 | tf_op jit(solution)/shard_map/ppermute | solution.py:214
  20.1 5.5 %collective-permute-done.refs_1_ = bf16[272,768]{1,0:T(8,128)(2,1)S(1)} collective-permute-done((bf16[272,768]{1,0:T(8,128)(2,1)}, bf16[272,768]{1,0:T(8,128)(2,1)S(1)}, u32[]{:S(2)}, u32[]{:S(2)}) %collective-permute-start) | collective-permute-done | bytes 417824 | tf_op jit(solution)/shard_map/ppermute | solution.py:213
  25.5 1.3 %collective-permute-start.11 = (bf16[272,768]{1,0:T(8,128)(2,1)S(1)}, bf16[272,768]{1,0:T(8,128)(2,1)S(1)}, u32[]{:S(2)}, u32[]{:S(2)}) collective-permute-start(bf16[272,768]{1,0:T(8,128)(2,1)S(1)} %collective-permute-done.refs_1_), channel_id=1, source_target_pairs={{0,1},{1,0},{2,3},{3,2},{4,5},{5,4},{6,7},{7,6},{8,9},{9,8},{10,11... | collective-permute-start | bytes 1253384 | tf_op jit(solution)/shard_map/ppermute | solution.py:214
  26.8 0.0 collective-permute-done.1.refs_2_
  26.8 0.2 collective-permute-start.5
  27.0 0.3 collective-permute-start.12
  27.3 0.0 collective-permute-done.10.refs_5_.refs_11_
  27.3 1.0 %collective-permute-start.4 = (bf16[272,768]{1,0:T(8,128)(2,1)S(1)}, bf16[272,768]{1,0:T(8,128)(2,1)}, u32[]{:S(2)}, u32[]{:S(2)}) collective-permute-start(bf16[272,768]{1,0:T(8,128)(2,1)S(1)} %collective-permute-done.1.refs_2_), channel_id=1, source_target_pairs={{6,0},{7,1},{0,2},{1,3},{2,4},{3,5},{4,6},{5,7},{14,8},{15,9},{8,1... | collective-permute-start | bytes 1253384 | tf_op jit(solution)/shard_map/ppermute | solution.py:213
  28.3 0.7 collective-permute-start.14
  29.0 2.5 %collective-permute-start.6 = (bf16[272,768]{1,0:T(8,128)(2,1)S(1)}, bf16[272,768]{1,0:T(8,128)(2,1)}, u32[]{:S(2)}, u32[]{:S(2)}) collective-permute-start(bf16[272,768]{1,0:T(8,128)(2,1)S(1)} %collective-permute-done.3.refs_4_), channel_id=1, source_target_pairs={{32,0},{9,1},{34,2},{11,3},{36,4},{13,5},{38,6},{15,7},{40,8},{17,... | collective-permute-start | bytes 1253384 | tf_op jit(solution)/shard_map/ppermute | solution.py:213
  31.6 0.0 copy-start.2
  31.6 0.0 copy-start.3
  31.6 0.6 copy-done.2
  32.2 0.0 copy-done.3
  32.3 2.1 %collective-permute-start.8 = (bf16[272,768]{1,0:T(8,128)(2,1)S(1)}, bf16[272,768]{1,0:T(8,128)(2,1)S(1)}, u32[]{:S(2)}, u32[]{:S(2)}) collective-permute-start(bf16[272,768]{1,0:T(8,128)(2,1)S(1)} %collective-permute-done.3.refs_4_), channel_id=1, source_target_pairs={{8,0},{33,1},{10,2},{35,3},{12,4},{37,5},{14,6},{39,7},{16,8},{41,... | collective-permute-start | bytes 1253384 | tf_op jit(solution)/shard_map/ppermute | solution.py:213
  34.3 1.0 %collective-permute-done.5.refs_6_ = bf16[272,768]{1,0:T(8,128)(2,1)S(1)} collective-permute-done((bf16[272,768]{1,0:T(8,128)(2,1)S(1)}, bf16[272,768]{1,0:T(8,128)(2,1)S(1)}, u32[]{:S(2)}, u32[]{:S(2)}) %collective-permute-start.5) | collective-permute-done | bytes 417824 | tf_op jit(solution)/shard_map/ppermute | solution.py:213
  35.3 0.8 collective-permute-start.9
  36.1 4.5 %collective-permute-done.4.refs_5_ = bf16[272,768]{1,0:T(8,128)(2,1)} collective-permute-done((bf16[272,768]{1,0:T(8,128)(2,1)S(1)}, bf16[272,768]{1,0:T(8,128)(2,1)}, u32[]{:S(2)}, u32[]{:S(2)}) %collective-permute-start.4) | collective-permute-done | bytes 417824 | tf_op jit(solution)/shard_map/ppermute | solution.py:213
  40.5 0.8 %collective-permute-start.7 = (bf16[272,768]{1,0:T(8,128)(2,1)S(1)}, bf16[272,768]{1,0:T(8,128)(2,1)S(1)}, u32[]{:S(2)}, u32[]{:S(2)}) collective-permute-start(bf16[272,768]{1,0:T(8,128)(2,1)S(1)} %collective-permute-done.refs_1_), channel_id=1, source_target_pairs={{96,0},{25,1},{98,2},{27,3},{100,4},{29,5},{102,6},{31,7},{104,8},... | collective-permute-start | bytes 1253384 | tf_op jit(solution)/shard_map/ppermute | solution.py:213
  41.3 2.1 %collective-permute-start.16 = (bf16[272,768]{1,0:T(8,128)(2,1)S(1)}, bf16[272,768]{1,0:T(8,128)(2,1)S(1)}, u32[]{:S(2)}, u32[]{:S(2)}) collective-permute-start(bf16[272,768]{1,0:T(8,128)(2,1)S(1)} %collective-permute-done.5.refs_6_), channel_id=1, source_target_pairs={{0,1},{1,0},{2,3},{3,2},{4,5},{5,4},{6,7},{7,6},{8,9},{9,8},{10,11... | collective-permute-start | bytes 1253384 | tf_op jit(solution)/shard_map/ppermute | solution.py:214
  43.4 0.3 collective-permute-start.15
  43.7 0.1 pad_add_fusion.place_ref
  43.8 1.0 %copy-done = bf16[272,768]{1,0:T(8,128)(2,1)S(1)} copy-done((bf16[272,768]{1,0:T(8,128)(2,1)S(1)}, bf16[272,768]{1,0:T(8,128)(2,1)}, u32[]{:S(2)}) %copy-start) | copy-done | bytes 417816
  44.8 4.0 %pair_sums_0.1.refs_18_ = f32[22,256]{1,0:T(8,128)S(1)} custom-call(s32[4]{0:T(128)S(1)} %pad_add_fusion.place_ref, bf16[272,768]{1,0:T(8,128)(2,1)S(1)} %copy-done, bf16[272,768]{1,0:T(8,128)(2,1)S(1)} %collective-permute-done.refs_1_, bf16[272,768]{1,0:T(8,128)(2,1)S(1)} %collective-permute-done.1.refs_2_, ...), custom_call_target="tpu_custom_call" | custom-call | flops 2164260864 | tf_op jit(solution)/shard_map/pair_sums_0/pallas_call | solution.py:188
  48.8 0.1 collective-permute-done.7.refs_8_
  49.0 7.6 %pair_sums_1.1 = f32[22,256]{1,0:T(8,128)S(1)} custom-call(s32[4]{0:T(128)S(1)} %pad_add_fusion.place_ref, bf16[272,768]{1,0:T(8,128)(2,1)S(1)} %copy-done.1, bf16[272,768]{1,0:T(8,128)(2,1)S(1)} %collective-permute-done.refs_1_, bf16[272,768]{1,0:T(8,128)(2,1)S(1)} %collective-permute-done.1.refs_2_, bf16[272,768]{1,0:T(8,128)(2,1)S(1)} %collective-permute-done.2.refs_3_, ...), custom_call_target="tpu_custom_call" | custom-call | flops 4328521728 | tf_op jit(solution)/shard_map/pair_sums_1/pallas_call | solution.py:188
  56.6 0.6 gather_fusion.1
  57.2 0.1 broadcast_select_fusion
  57.2 2.1 %collective-permute-start.17 = (f32[10,256]{1,0:T(8,128)S(1)}, f32[10,256]{1,0:T(8,128)S(1)}, u32[]{:S(2)}, u32[]{:S(2)}) collective-permute-start(f32[10,256]{1,0:T(8,128)S(1)} %broadcast_select_fusion), channel_id=1, source_target_pairs={{0,1},{1,0},{2,3},{3,2},{4,5},{5,4},{6,7},{7,6},{8,9},{9,8},{10,11... | collective-permute-start | bytes 30728 | tf_op jit(solution)/shard_map/ppermute | solution.py:233
  59.3 0.6 gather_fusion
  59.9 0.3 collective-permute-done.17
  60.1 0.1 select_add_fusion
  60.2 0.1 collective-permute-start.18
  60.3 0.6 collective-permute-start.19
  60.9 4.2 %collective-permute-start.20 = (f32[1,512]{1,0:T(1,128)S(1)}, f32[1,512]{1,0:T(1,128)S(1)}, u32[]{:S(2)}, u32[]{:S(2)}) collective-permute-start(f32[1,512]{1,0:T(1,128)S(1)} %bitcast.41), channel_id=1, source_target_pairs={{0,38},{1,43},{2,32},{3,45},{4,34},{5,47},{6,36},{7,41},{8,46},{9,... | collective-permute-start | bytes 6152 | tf_op jit(solution)/shard_map/ppermute | solution.py:236
  65.1 2.4 %collective-permute-start.21 = (f32[1,512]{1,0:T(1,128)S(1)}, f32[1,512]{1,0:T(1,128)S(1)}, u32[]{:S(2)}, u32[]{:S(2)}) collective-permute-start(f32[1,512]{1,0:T(1,128)S(1)} %bitcast.42), channel_id=1, source_target_pairs={{0,58},{1,107},{2,60},{3,109},{4,62},{5,111},{6,56},{7,105},{8,34}... | collective-permute-start | bytes 6152 | tf_op jit(solution)/shard_map/ppermute | solution.py:236
  67.6 5.0 %collective-permute-start.22 = (f32[1,512]{1,0:T(1,128)S(1)}, f32[1,512]{1,0:T(1,128)S(1)}, u32[]{:S(2)}, u32[]{:S(2)}) collective-permute-start(f32[1,512]{1,0:T(1,128)S(1)} %bitcast.43), channel_id=1, source_target_pairs={{0,120},{1,127},{2,122},{3,121},{4,124},{5,123},{6,126},{7,125},{8... | collective-permute-start | bytes 6152 | tf_op jit(solution)/shard_map/ppermute | solution.py:236
  72.6 0.7 collective-permute-done.22
  73.3 0.1 collective-permute-start.23
  73.4 1.1 %collective-permute-done.23 = f32[256]{0:T(256)S(1)} collective-permute-done((f32[256]{0:T(256)S(1)}, f32[256]{0:T(256)S(1)}, u32[]{:S(2)}, u32[]{:S(2)}) %collective-permute-start.23) | collective-permute-done | bytes 1056 | tf_op jit(solution)/shard_map/ppermute | solution.py:240
  74.5 0.6 add_log-plus-one_fusion
  (36 shorter events, 0.1 us)
Async XLA Ops:
  1.9 13.3 %collective-permute-start.2 = (bf16[272,768]{1,0:T(8,128)(2,1)}, bf16[272,768]{1,0:T(8,128)(2,1)S(1)}, u32[]{:S(2)}, u32[]{:S(2)}) collective-permute-start(bf16[272,768]{1,0:T(8,128)(2,1)} %pack.1.refs_0_), channel_id=1, source_target_pairs={{34,0},{11,1},{36,2},{13,3},{38,4},{15,5},{32,6},{9,7},{42,8},{19,... | collective-permute-start | bytes 1253384 | tf_op jit(solution)/shard_map/ppermute | solution.py:213
  7.7 17.9 %collective-permute-start = (bf16[272,768]{1,0:T(8,128)(2,1)}, bf16[272,768]{1,0:T(8,128)(2,1)S(1)}, u32[]{:S(2)}, u32[]{:S(2)}) collective-permute-start(bf16[272,768]{1,0:T(8,128)(2,1)} %pack.1.refs_0_), channel_id=1, source_target_pairs={{10,0},{35,1},{12,2},{37,3},{14,4},{39,5},{8,6},{33,7},{18,8},{43,... | collective-permute-start | bytes 1253384 | tf_op jit(solution)/shard_map/ppermute | solution.py:213
  11.7 15.1 %collective-permute-start.1 = (bf16[272,768]{1,0:T(8,128)(2,1)}, bf16[272,768]{1,0:T(8,128)(2,1)S(1)}, u32[]{:S(2)}, u32[]{:S(2)}) collective-permute-start(bf16[272,768]{1,0:T(8,128)(2,1)} %pack.1.refs_0_), channel_id=1, source_target_pairs={{120,0},{121,1},{122,2},{123,3},{124,4},{125,5},{126,6},{127,7},{9... | collective-permute-start | bytes 1253384 | tf_op jit(solution)/shard_map/ppermute | solution.py:213
  11.7 15.3 %collective-permute-start.3 = (bf16[272,768]{1,0:T(8,128)(2,1)}, bf16[272,768]{1,0:T(8,128)(2,1)S(1)}, u32[]{:S(2)}, u32[]{:S(2)}) collective-permute-start(bf16[272,768]{1,0:T(8,128)(2,1)} %pack.1.refs_0_), channel_id=1, source_target_pairs={{6,0},{7,1},{0,2},{1,3},{2,4},{3,5},{4,6},{5,7},{14,8},{15,9},{8,1... | collective-permute-start | bytes 1253384 | tf_op jit(solution)/shard_map/ppermute | solution.py:213
  12.6 14.7 %collective-permute-start.10 = (bf16[272,768]{1,0:T(8,128)(2,1)}, bf16[272,768]{1,0:T(8,128)(2,1)S(1)}, u32[]{:S(2)}, u32[]{:S(2)}) collective-permute-start(bf16[272,768]{1,0:T(8,128)(2,1)} %pack.1.refs_0_), channel_id=1, source_target_pairs={{0,1},{1,0},{2,3},{3,2},{4,5},{5,4},{6,7},{7,6},{8,9},{9,8},{10,11... | collective-permute-start | bytes 1253384 | tf_op jit(solution)/shard_map/ppermute | solution.py:214
  15.2 13.1 %collective-permute-start.13 = (bf16[272,768]{1,0:T(8,128)(2,1)S(1)}, bf16[272,768]{1,0:T(8,128)(2,1)S(1)}, u32[]{:S(2)}, u32[]{:S(2)}) collective-permute-start(bf16[272,768]{1,0:T(8,128)(2,1)S(1)} %collective-permute-done.2.refs_3_), channel_id=1, source_target_pairs={{0,1},{1,0},{2,3},{3,2},{4,5},{5,4},{6,7},{7,6},{8,9},{9,8},{10,11... | collective-permute-start | bytes 1253384 | tf_op jit(solution)/shard_map/ppermute | solution.py:214
  25.5 3.5 %collective-permute-start.11 = (bf16[272,768]{1,0:T(8,128)(2,1)S(1)}, bf16[272,768]{1,0:T(8,128)(2,1)S(1)}, u32[]{:S(2)}, u32[]{:S(2)}) collective-permute-start(bf16[272,768]{1,0:T(8,128)(2,1)S(1)} %collective-permute-done.refs_1_), channel_id=1, source_target_pairs={{0,1},{1,0},{2,3},{3,2},{4,5},{5,4},{6,7},{7,6},{8,9},{9,8},{10,11... | collective-permute-start | bytes 1253384 | tf_op jit(solution)/shard_map/ppermute | solution.py:214
  26.8 4.7 %copy-start.4 = (s32[10]{0:T(128)S(1)}, s32[10]{0:T(128)}, u32[]{:S(2)}) copy-start(s32[10]{0:T(128)} %constant.39.clone) | copy-start | bytes 124
  26.8 4.7 %copy-start.5 = (s32[10]{0:T(128)S(1)}, s32[10]{0:T(128)}, u32[]{:S(2)}) copy-start(s32[10]{0:T(128)} %constant.40.clone) | copy-start | bytes 124
  26.8 8.5 %collective-permute-start.5 = (bf16[272,768]{1,0:T(8,128)(2,1)S(1)}, bf16[272,768]{1,0:T(8,128)(2,1)S(1)}, u32[]{:S(2)}, u32[]{:S(2)}) collective-permute-start(bf16[272,768]{1,0:T(8,128)(2,1)S(1)} %collective-permute-done.2.refs_3_), channel_id=1, source_target_pairs={{24,0},{97,1},{26,2},{99,3},{28,4},{101,5},{30,6},{103,7},{0,8},{1... | collective-permute-start | bytes 1253384 | tf_op jit(solution)/shard_map/ppermute | solution.py:213
  27.0 5.2 %collective-permute-start.12 = (bf16[272,768]{1,0:T(8,128)(2,1)S(1)}, bf16[272,768]{1,0:T(8,128)(2,1)}, u32[]{:S(2)}, u32[]{:S(2)}) collective-permute-start(bf16[272,768]{1,0:T(8,128)(2,1)S(1)} %collective-permute-done.1.refs_2_), channel_id=1, source_target_pairs={{0,1},{1,0},{2,3},{3,2},{4,5},{5,4},{6,7},{7,6},{8,9},{9,8},{10,11... | collective-permute-start | bytes 1253384 | tf_op jit(solution)/shard_map/ppermute | solution.py:214
  27.3 13.3 %collective-permute-start.4 = (bf16[272,768]{1,0:T(8,128)(2,1)S(1)}, bf16[272,768]{1,0:T(8,128)(2,1)}, u32[]{:S(2)}, u32[]{:S(2)}) collective-permute-start(bf16[272,768]{1,0:T(8,128)(2,1)S(1)} %collective-permute-done.1.refs_2_), channel_id=1, source_target_pairs={{6,0},{7,1},{0,2},{1,3},{2,4},{3,5},{4,6},{5,7},{14,8},{15,9},{8,1... | collective-permute-start | bytes 1253384 | tf_op jit(solution)/shard_map/ppermute | solution.py:213
  28.3 13.0 %collective-permute-start.14 = (bf16[272,768]{1,0:T(8,128)(2,1)S(1)}, bf16[272,768]{1,0:T(8,128)(2,1)}, u32[]{:S(2)}, u32[]{:S(2)}) collective-permute-start(bf16[272,768]{1,0:T(8,128)(2,1)S(1)} %collective-permute-done.3.refs_4_), channel_id=1, source_target_pairs={{0,1},{1,0},{2,3},{3,2},{4,5},{5,4},{6,7},{7,6},{8,9},{9,8},{10,11... | collective-permute-start | bytes 1253384 | tf_op jit(solution)/shard_map/ppermute | solution.py:214
  29.0 14.4 %collective-permute-start.6 = (bf16[272,768]{1,0:T(8,128)(2,1)S(1)}, bf16[272,768]{1,0:T(8,128)(2,1)}, u32[]{:S(2)}, u32[]{:S(2)}) collective-permute-start(bf16[272,768]{1,0:T(8,128)(2,1)S(1)} %collective-permute-done.3.refs_4_), channel_id=1, source_target_pairs={{32,0},{9,1},{34,2},{11,3},{36,4},{13,5},{38,6},{15,7},{40,8},{17,... | collective-permute-start | bytes 1253384 | tf_op jit(solution)/shard_map/ppermute | solution.py:213
  31.6 0.7 copy-start.2
  31.6 0.7 copy-start.3
  32.3 16.6 %collective-permute-start.8 = (bf16[272,768]{1,0:T(8,128)(2,1)S(1)}, bf16[272,768]{1,0:T(8,128)(2,1)S(1)}, u32[]{:S(2)}, u32[]{:S(2)}) collective-permute-start(bf16[272,768]{1,0:T(8,128)(2,1)S(1)} %collective-permute-done.3.refs_4_), channel_id=1, source_target_pairs={{8,0},{33,1},{10,2},{35,3},{12,4},{37,5},{14,6},{39,7},{16,8},{41,... | collective-permute-start | bytes 1253384 | tf_op jit(solution)/shard_map/ppermute | solution.py:213
  35.3 13.5 %collective-permute-start.9 = (bf16[272,768]{1,0:T(8,128)(2,1)S(1)}, bf16[272,768]{1,0:T(8,128)(2,1)S(1)}, u32[]{:S(2)}, u32[]{:S(2)}) collective-permute-start(bf16[272,768]{1,0:T(8,128)(2,1)S(1)} %collective-permute-done.2.refs_3_), channel_id=1, source_target_pairs={{8,0},{33,1},{10,2},{35,3},{12,4},{37,5},{14,6},{39,7},{16,8},{41,... | collective-permute-start | bytes 1253384 | tf_op jit(solution)/shard_map/ppermute | solution.py:213
  40.5 8.4 %collective-permute-start.7 = (bf16[272,768]{1,0:T(8,128)(2,1)S(1)}, bf16[272,768]{1,0:T(8,128)(2,1)S(1)}, u32[]{:S(2)}, u32[]{:S(2)}) collective-permute-start(bf16[272,768]{1,0:T(8,128)(2,1)S(1)} %collective-permute-done.refs_1_), channel_id=1, source_target_pairs={{96,0},{25,1},{98,2},{27,3},{100,4},{29,5},{102,6},{31,7},{104,8},... | collective-permute-start | bytes 1253384 | tf_op jit(solution)/shard_map/ppermute | solution.py:213
  41.3 7.6 %collective-permute-start.16 = (bf16[272,768]{1,0:T(8,128)(2,1)S(1)}, bf16[272,768]{1,0:T(8,128)(2,1)S(1)}, u32[]{:S(2)}, u32[]{:S(2)}) collective-permute-start(bf16[272,768]{1,0:T(8,128)(2,1)S(1)} %collective-permute-done.5.refs_6_), channel_id=1, source_target_pairs={{0,1},{1,0},{2,3},{3,2},{4,5},{5,4},{6,7},{7,6},{8,9},{9,8},{10,11... | collective-permute-start | bytes 1253384 | tf_op jit(solution)/shard_map/ppermute | solution.py:214
  43.4 5.5 %collective-permute-start.15 = (bf16[272,768]{1,0:T(8,128)(2,1)}, bf16[272,768]{1,0:T(8,128)(2,1)S(1)}, u32[]{:S(2)}, u32[]{:S(2)}) collective-permute-start(bf16[272,768]{1,0:T(8,128)(2,1)} %collective-permute-done.4.refs_5_), channel_id=1, source_target_pairs={{0,1},{1,0},{2,3},{3,2},{4,5},{5,4},{6,7},{7,6},{8,9},{9,8},{10,11... | collective-permute-start | bytes 1253384 | tf_op jit(solution)/shard_map/ppermute | solution.py:214
  43.8 1.0 %copy-start = (bf16[272,768]{1,0:T(8,128)(2,1)S(1)}, bf16[272,768]{1,0:T(8,128)(2,1)}, u32[]{:S(2)}) copy-start(bf16[272,768]{1,0:T(8,128)(2,1)} %pack.1.refs_0_) | copy-start | bytes 1253380
  44.8 4.2 %copy-start.1 = (bf16[272,768]{1,0:T(8,128)(2,1)S(1)}, bf16[272,768]{1,0:T(8,128)(2,1)}, u32[]{:S(2)}) copy-start(bf16[272,768]{1,0:T(8,128)(2,1)} %pack.1.refs_0_) | copy-start | bytes 1253380
  57.2 2.9 %collective-permute-start.17 = (f32[10,256]{1,0:T(8,128)S(1)}, f32[10,256]{1,0:T(8,128)S(1)}, u32[]{:S(2)}, u32[]{:S(2)}) collective-permute-start(f32[10,256]{1,0:T(8,128)S(1)} %broadcast_select_fusion), channel_id=1, source_target_pairs={{0,1},{1,0},{2,3},{3,2},{4,5},{5,4},{6,7},{7,6},{8,9},{9,8},{10,11... | collective-permute-start | bytes 30728 | tf_op jit(solution)/shard_map/ppermute | solution.py:233
  60.2 12.3 %collective-permute-start.18 = (f32[1,512]{1,0:T(1,128)S(1)}, f32[1,512]{1,0:T(1,128)S(1)}, u32[]{:S(2)}, u32[]{:S(2)}) collective-permute-start(f32[1,512]{1,0:T(1,128)S(1)} %bitcast.39), channel_id=1, source_target_pairs={{0,6},{1,11},{2,0},{3,13},{4,2},{5,15},{6,4},{7,9},{8,14},{9,19},{... | collective-permute-start | bytes 6152 | tf_op jit(solution)/shard_map/ppermute | solution.py:236
  60.3 12.2 %collective-permute-start.19 = (f32[1,512]{1,0:T(1,128)S(1)}, f32[1,512]{1,0:T(1,128)S(1)}, u32[]{:S(2)}, u32[]{:S(2)}) collective-permute-start(f32[1,512]{1,0:T(1,128)S(1)} %bitcast.40), channel_id=1, source_target_pairs={{0,14},{1,35},{2,8},{3,37},{4,10},{5,39},{6,12},{7,33},{8,22},{9,4... | collective-permute-start | bytes 6152 | tf_op jit(solution)/shard_map/ppermute | solution.py:236
  60.9 11.7 %collective-permute-start.20 = (f32[1,512]{1,0:T(1,128)S(1)}, f32[1,512]{1,0:T(1,128)S(1)}, u32[]{:S(2)}, u32[]{:S(2)}) collective-permute-start(f32[1,512]{1,0:T(1,128)S(1)} %bitcast.41), channel_id=1, source_target_pairs={{0,38},{1,43},{2,32},{3,45},{4,34},{5,47},{6,36},{7,41},{8,46},{9,... | collective-permute-start | bytes 6152 | tf_op jit(solution)/shard_map/ppermute | solution.py:236
  65.1 7.5 %collective-permute-start.21 = (f32[1,512]{1,0:T(1,128)S(1)}, f32[1,512]{1,0:T(1,128)S(1)}, u32[]{:S(2)}, u32[]{:S(2)}) collective-permute-start(f32[1,512]{1,0:T(1,128)S(1)} %bitcast.42), channel_id=1, source_target_pairs={{0,58},{1,107},{2,60},{3,109},{4,62},{5,111},{6,56},{7,105},{8,34}... | collective-permute-start | bytes 6152 | tf_op jit(solution)/shard_map/ppermute | solution.py:236
  67.6 5.7 %collective-permute-start.22 = (f32[1,512]{1,0:T(1,128)S(1)}, f32[1,512]{1,0:T(1,128)S(1)}, u32[]{:S(2)}, u32[]{:S(2)}) collective-permute-start(f32[1,512]{1,0:T(1,128)S(1)} %bitcast.43), channel_id=1, source_target_pairs={{0,120},{1,127},{2,122},{3,121},{4,124},{5,123},{6,126},{7,125},{8... | collective-permute-start | bytes 6152 | tf_op jit(solution)/shard_map/ppermute | solution.py:236
  73.3 1.2 %collective-permute-start.23 = (f32[256]{0:T(256)S(1)}, f32[256]{0:T(256)S(1)}, u32[]{:S(2)}, u32[]{:S(2)}) collective-permute-start(f32[256]{0:T(256)S(1)} %broadcast_select_fusion.3), channel_id=1, source_target_pairs={{0,1},{1,0},{2,3},{3,2},{4,5},{5,4},{6,7},{7,6},{8,9},{9,8},{10,11... | collective-permute-start | bytes 3080 | tf_op jit(solution)/shard_map/ppermute | solution.py:240

commit v3 on v2

--- a/solution.py
+++ b/solution.py
@@ -15,10 +15,10 @@
 BOTH = ("cluster", "member")
 CLUSTER_SHIFT = 5
 
-PLAN = ((0, 5), (0, 60), (0, 17), (0, 3), (2, 3), (3, 12), (4, 16), (1, 48), (4, 4), (3, 4))
+PLAN = ((0, 13), (0, 20), (0, 3), (0, 49), (1, 48), (1, 16), (2, 3), (3, 48), (4, 4), (3, 12))
 SWAPPED = 7
 BLOCKS = len(PLAN) + 1
-PHASES = ((5, 5), (BLOCKS, SWAPPED))
+PHASES = ((5, 5), (7, 7), (BLOCKS, SWAPPED))
 
 
 def shift(place, by):
@@ -58,6 +58,25 @@
 
 HELD = held_offsets()
 assert len(set(HELD)) == BLOCKS and {mirror(o) for o in HELD} == set(HELD)
+
+
+def distance(place):
+    return sum(min(place >> s & 3, -(place >> s) & 3) for s in (0, 2, 4))
+
+
+AFAR = sorted(sorted(HELD)[1:], key=distance, reverse=True)
+SHARES = (AFAR[0::2], AFAR[1::2])
+SHARE = len(SHARES[0])
+GIVEN, HOME = 16, 32
+
+
+def table_row(core, slot):
+    kind = core if slot < BLOCKS else 1 - core
+    offset = mirror(HELD[slot % BLOCKS], kind)
+    if offset == 0:
+        return HOME + kind
+    own = offset in SHARES[core]
+    return 2 * SHARES[core if own else 1 - core].index(offset) + kind + (0 if own else GIVEN)
 
 
 def units():
@@ -106,12 +125,12 @@
     return [slice(start + s, start + s + LANES) for s in range(0, ROWS - start, LANES)]
 
 
-def pairs_body(work, mine_used, other_used, earlier, place_ref, *refs):
+def pairs_body(work, mine_used, other_used, earlier, last, place_ref, *refs):
     count = len(mine_used) + len(other_used)
     mine = dict(zip(mine_used, refs))
     other = dict(zip(other_used, refs[len(mine_used) : count]))
     before_ref = refs[count] if earlier else None
-    out_ref, labels_ref, row_sums, column_sums = refs[count + earlier :]
+    outs, (labels_ref, row_sums, column_sums, table) = refs[count + earlier : -4], refs[-4:]
     firsts = sorted({a for _, a, *_ in work})
     at = {a: n for n, a in enumerate(firsts)}
     row_sums[...] = jnp.zeros_like(row_sums)
@@ -166,13 +185,23 @@
         row_sums[at[a]] += values[0] + values[1]
 
     for slot in range(2 * BLOCKS):
+        if last:
+            rows = [table_row(core, slot) for core in (0, 1)]
+            row = jnp.where(place_ref[0] == 0, rows[0], rows[1])
         for part in parts():
             total = jnp.sum(column_sums[slot, :, part], axis=0, keepdims=True)
             if slot in at:
                 total += jnp.sum(row_sums[at[slot], part, :].T, axis=0, keepdims=True)
             if earlier:
-                total += before_ref[slot : slot + 1, part]
-            out_ref[slot : slot + 1, part] = total
+                total += before_ref[slot, :, part]
+            if last:
+                table[row, :, part] = total
+            else:
+                outs[0][slot, :, part] = total
+    if last:
+        outs[0][...] = table[0 : 2 * SHARE]
+        outs[1][...] = table[GIVEN : GIVEN + 2 * SHARE]
+        outs[2][...] = table[HOME : HOME + 2]
 
 
 def pair_sums(phase, place, mine, other, before):
@@ -182,18 +211,21 @@
     blocks = [mine[k] for k in mine_used] + [other[k] for k in other_used]
     blocks = [pltpu.with_memory_space_constraint(block, pltpu.VMEM) for block in blocks]
     before = [] if before is None else [before]
+    last = phase == len(PHASES) - 1
+    outs = (2 * SHARE, 2 * SHARE, 2) if last else (2 * BLOCKS,)
     smem, vmem = pl.BlockSpec(memory_space=pltpu.SMEM), pl.BlockSpec(memory_space=pltpu.VMEM)
     firsts = len({a for _, a, *_ in work})
     area = sum(ROWS * ROWS // (2 if kind == "half" else 1) for kind, *_ in work)
     return pl.pallas_call(
-        functools.partial(pairs_body, work, mine_used, other_used, len(before)),
-        out_shape=jax.ShapeDtypeStruct((2 * BLOCKS, ROWS), jnp.float32),
+        functools.partial(pairs_body, work, mine_used, other_used, len(before), last),
+        out_shape=[jax.ShapeDtypeStruct((n, 1, ROWS), jnp.float32) for n in outs],
         in_specs=[smem] + [vmem] * (len(blocks) + len(before)),
-        out_specs=vmem,
+        out_specs=[vmem] * len(outs),
         scratch_shapes=[
             pltpu.VMEM((firsts, ROWS, LANES), jnp.float32),
             pltpu.VMEM((firsts, ROWS, LANES), jnp.float32),
             pltpu.VMEM((2 * BLOCKS, 8, ROWS), jnp.float32),
+            pltpu.VMEM((HOME + 2, 1, ROWS), jnp.float32),
         ],
         compiler_params=pltpu.CompilerParams(vmem_limit_bytes=24 * 1024 * 1024),
         cost_estimate=pl.CostEstimate(flops=2 * area * WIDTH, bytes_accessed=0, transcendentals=area),
@@ -209,36 +241,26 @@
     place = jnp.stack([core, x, jnp.where(core == 0, y, z), jnp.where(core == 0, z, y)]).astype(jnp.int32)
 
     mine = [pack(embeddings, destination)]
-    for source, jump in PLAN:
+    other = [lax.ppermute(mine[0], BOTH, CORE_SWAP)]
+    for source, jump in PLAN[:-1]:
         mine.append(lax.ppermute(mine[source], BOTH, fetch((jump, mirror(jump)))))
-    other = [lax.ppermute(block, BOTH, CORE_SWAP) for block in mine[:SWAPPED]]
-    sums = None
-    for phase in range(len(PHASES)):
-        sums = pair_sums(phase, place, mine, other, sums)
-
-    offsets = sorted(HELD)[1:]
-    shares = [offsets[0::2], offsets[1::2]]
-
-    def rows_of(share_of):
-        by_core = []
-        for c in (0, 1):
-            places = [(mirror(o, c), mirror(o, 1 - c)) for o in share_of(c)]
-            slots = [(HELD.index(a), BLOCKS + HELD.index(b)) for a, b in places]
-            by_core.append(np.array([pair[::-1] if c else pair for pair in slots], np.int32).reshape(-1))
-        index = jnp.where(core == 0, jnp.asarray(by_core[0]), jnp.asarray(by_core[1]))
-        return jnp.take(sums, index, axis=0)
-
-    kept = rows_of(lambda c: shares[c])
-    given = rows_of(lambda c: shares[1 - c])
-    kept = (kept + lax.ppermute(given, BOTH, CORE_SWAP)).reshape(-1, 2 * ROWS)
-    total = jnp.where(core == 0, jnp.stack([sums[0], sums[BLOCKS]]), jnp.stack([sums[BLOCKS], sums[0]])).reshape(-1)
-    for k in range(len(shares[0])):
-        total += lax.ppermute(kept[k : k + 1], BOTH, give((shares[0][k], shares[1][k])))[0]
-    total = total.reshape(2, ROWS)
-    own = jnp.where(core == 0, total[0], total[1])
-    rest = jnp.where(core == 0, total[1], total[0])
-    density = own + lax.ppermute(rest, BOTH, CORE_SWAP)
-    return jnp.log1p(density)
+    other += [lax.ppermute(block, BOTH, CORE_SWAP) for block in mine[1 : PHASES[0][1]]]
+    (sums,) = pair_sums(0, place, mine, other, None)
+
+    source, jump = PLAN[-1]
+    source, later, sums = lax.optimization_barrier((mine[source], mine[PHASES[0][1] : SWAPPED], sums))
+    mine.append(lax.ppermute(source, BOTH, fetch((jump, mirror(jump)))))
+    other += [lax.ppermute(block, BOTH, CORE_SWAP) for block in later]
+    (sums,) = pair_sums(1, place, mine, other, sums)
+    kept, given, home = pair_sums(2, place, mine, other, sums)
+
+    kept += lax.ppermute(given, BOTH, CORE_SWAP)
+    for n in range(SHARE):
+        jumps = [SHARES[c][n] for c in (0, 1)]
+        home += lax.ppermute(kept[2 * n : 2 * n + 2], BOTH, give(jumps))
+    home = home.reshape(2, ROWS)
+    own, rest = jnp.where(core == 0, home[0], home[1]), jnp.where(core == 0, home[1], home[0])
+    return jnp.log1p(own + lax.ppermute(rest, BOTH, CORE_SWAP))
 
 
 def solution(mesh):

time: 75.3 us -> 75.2 us (level)
  waiting for transfers between devices: 14.3 us -> 17.1 us
  starting transfers between devices: 43.4 us -> 41 us
  local copies, waits for them, and re-layouts: 2.82 us -> 1.01 us
  Pallas kernels: 13.6 us -> 15.1 us
    ppermute x14 -> x15, waiting for transfers between devices: 2.1 us -> 5.11 us  [the longest x1 1.79 us: shards(): mine.append(lax.ppermute(source, BOTH, fetch((jump, mirror(jump)))))]
    pallas_call x2 -> x3, Pallas kernels: 11.6 us -> 13.2 us  [pair_sums(): pl.pallas_call(functools.partial(pairs_body, work, mine_used, other_used,...]
    ppermute x14 -> x15, starting transfers between devices: 25.4 us -> 24 us  [the longest x5 11 us: shards(): home += lax.ppermute(kept[2 * n:2 * n + 2], BOTH, give(jumps))]
    gather x2 -> x0, local copies, waits for them, and re-layouts: 1.13 us -> none  [rows_of(): return jnp.take(sums, index, axis=0)]
    ppermute x10 -> x9, starting transfers between devices: 18 us -> 17 us  [shards(): mine.append(lax.ppermute(mine[source], BOTH, fetch((jump, mirror(jump)))))]
    unnamed x19 -> x4, local copies, waits for them, and re-layouts: 1.69 us -> 1 us
    ppermute x10 -> x9, waiting for transfers between devices: 12.2 us -> 12 us  [shards(): mine.append(lax.ppermute(mine[source], BOTH, fetch((jump, mirror(jump)))))]
  transfers between devices with their start and end apart: 24 -> 24, of which waited for: 8 -> 10; matrix products, arithmetic and copies ran while one was open for 1% -> 0% of each run, Pallas kernels for 5% -> 11%
where the time goes in v3:
time: 75.2 us; the launch traced here: 75 us
  starting transfers between devices  41 us (55%)
  waiting for transfers between devices  17.1 us (23%)
  Pallas kernels  15.1 us (20%)
  local copies, waits for them, and re-layouts  1.01 us (1%)
    ppermute x9, starting transfers between devices, shards(): mine.append(lax.ppermute(mine[source], BOTH, fetch((jump, mirror(jump)))))  17 us
    pallas_call x3, Pallas kernels, pair_sums(): pl.pallas_call(functools.partial(pairs_body, work, mine_used, other_used,...  13.2 us
    ppermute x9, waiting for transfers between devices, shards(): mine.append(lax.ppermute(mine[source], BOTH, fetch((jump, mirror(jump)))))  12 us
    ppermute x5, starting transfers between devices, shards(): home += lax.ppermute(kept[2 * n:2 * n + 2], BOTH, give(jumps))  11 us
    ppermute x4, starting transfers between devices, shards(): lax.ppermute(block, BOTH, CORE_SWAP)  6.96 us
    ppermute x1, starting transfers between devices, shards(): return jnp.log1p(own + lax.ppermute(rest, BOTH, CORE_SWAP))  2.84 us
    pallas_call x1, Pallas kernels, pack(): pl.pallas_call(pack_body, out_shape=jax.ShapeDtypeStruct((ROWS + LABEL_RO...  1.94 us
    ppermute x1, starting transfers between devices, shards(): other = [lax.ppermute(mine[0], BOTH, CORE_SWAP)]  1.79 us
  transfers between devices with their start and end apart: 24, of which 10 were waited for; matrix products, arithmetic and copies ran while one was open for 0% of the time, Pallas kernels for 11%

profile of v3, /device:TPU:1, one launch (start us, length us, event | category | flops | bytes accessed | tf_op | source)
XLA Modules:
  0.0 75.0 jit_solution(11537442934449242215)
XLA Ops:
  0.0 1.9 %pack.1.refs_0_ = bf16[272,768]{1,0:T(8,128)(2,1)} custom-call(bf16[256,768]{1,0:T(8,128)(2,1)} %rows_ref.1, s32[1,256]{1,0:T(1,128)} %bitcast.8), custom_call_target="tpu_custom_call" | custom-call | tf_op jit(solution)/shard_map/pack/pallas_call | solution.py:117
  1.9 4.7 %collective-permute-start = (bf16[272,768]{1,0:T(8,128)(2,1)}, bf16[272,768]{1,0:T(8,128)(2,1)S(1)}, u32[]{:S(2)}, u32[]{:S(2)}) collective-permute-start(bf16[272,768]{1,0:T(8,128)(2,1)} %pack.1.refs_0_), channel_id=1, source_target_pairs={{26,0},{99,1},{28,2},{101,3},{30,4},{103,5},{24,6},{97,7},{2,8},{1... | collective-permute-start | bytes 1253384 | tf_op jit(solution)/shard_map/ppermute | solution.py:246
  6.6 3.5 %collective-permute-start.1 = (bf16[272,768]{1,0:T(8,128)(2,1)}, bf16[272,768]{1,0:T(8,128)(2,1)S(1)}, u32[]{:S(2)}, u32[]{:S(2)}) collective-permute-start(bf16[272,768]{1,0:T(8,128)(2,1)} %pack.1.refs_0_), channel_id=1, source_target_pairs={{40,0},{41,1},{42,2},{43,3},{44,4},{45,5},{46,6},{47,7},{48,8},{49... | collective-permute-start | bytes 1253384 | tf_op jit(solution)/shard_map/ppermute | solution.py:246
  10.1 0.1 collective-permute-start.6
  10.2 1.0 %collective-permute-start.2 = (bf16[272,768]{1,0:T(8,128)(2,1)}, bf16[272,768]{1,0:T(8,128)(2,1)S(1)}, u32[]{:S(2)}, u32[]{:S(2)}) collective-permute-start(bf16[272,768]{1,0:T(8,128)(2,1)} %pack.1.refs_0_), channel_id=1, source_target_pairs={{98,0},{27,1},{100,2},{29,3},{102,4},{31,5},{96,6},{25,7},{106,8},... | collective-permute-start | bytes 1253384 | tf_op jit(solution)/shard_map/ppermute | solution.py:246
  11.2 1.8 %collective-permute-start.9 = (bf16[272,768]{1,0:T(8,128)(2,1)}, bf16[272,768]{1,0:T(8,128)(2,1)S(1)}, u32[]{:S(2)}, u32[]{:S(2)}) collective-permute-start(bf16[272,768]{1,0:T(8,128)(2,1)} %pack.1.refs_0_), channel_id=1, source_target_pairs={{0,1},{1,0},{2,3},{3,2},{4,5},{5,4},{6,7},{7,6},{8,9},{9,8},{10,11... | collective-permute-start | bytes 1253384 | tf_op jit(solution)/shard_map/ppermute | solution.py:244
  13.0 2.6 %collective-permute-done.refs_1_ = bf16[272,768]{1,0:T(8,128)(2,1)S(1)} collective-permute-done((bf16[272,768]{1,0:T(8,128)(2,1)}, bf16[272,768]{1,0:T(8,128)(2,1)S(1)}, u32[]{:S(2)}, u32[]{:S(2)}) %collective-permute-start) | collective-permute-done | bytes 417824 | tf_op jit(solution)/shard_map/ppermute | solution.py:246
  15.6 2.0 %collective-permute-start.10 = (bf16[272,768]{1,0:T(8,128)(2,1)S(1)}, bf16[272,768]{1,0:T(8,128)(2,1)S(1)}, u32[]{:S(2)}, u32[]{:S(2)}) collective-permute-start(bf16[272,768]{1,0:T(8,128)(2,1)S(1)} %collective-permute-done.refs_1_), channel_id=1, source_target_pairs={{0,1},{1,0},{2,3},{3,2},{4,5},{5,4},{6,7},{7,6},{8,9},{9,8},{10,11... | collective-permute-start | bytes 1253384 | tf_op jit(solution)/shard_map/ppermute | solution.py:247
  17.6 1.3 %collective-permute-done.1.refs_2_ = bf16[272,768]{1,0:T(8,128)(2,1)S(1)} collective-permute-done((bf16[272,768]{1,0:T(8,128)(2,1)}, bf16[272,768]{1,0:T(8,128)(2,1)S(1)}, u32[]{:S(2)}, u32[]{:S(2)}) %collective-permute-start.1) | collective-permute-done | bytes 417824 | tf_op jit(solution)/shard_map/ppermute | solution.py:246
  18.9 1.3 %collective-permute-start.11 = (bf16[272,768]{1,0:T(8,128)(2,1)S(1)}, bf16[272,768]{1,0:T(8,128)(2,1)S(1)}, u32[]{:S(2)}, u32[]{:S(2)}) collective-permute-start(bf16[272,768]{1,0:T(8,128)(2,1)S(1)} %collective-permute-done.1.refs_2_), channel_id=1, source_target_pairs={{0,1},{1,0},{2,3},{3,2},{4,5},{5,4},{6,7},{7,6},{8,9},{9,8},{10,11... | collective-permute-start | bytes 1253384 | tf_op jit(solution)/shard_map/ppermute | solution.py:247
  20.3 0.1 collective-permute-done.6.refs_3_
  20.4 3.2 %collective-permute-start.12 = (bf16[272,768]{1,0:T(8,128)(2,1)S(1)}, bf16[272,768]{1,0:T(8,128)(2,1)S(1)}, u32[]{:S(2)}, u32[]{:S(2)}) collective-permute-start(bf16[272,768]{1,0:T(8,128)(2,1)S(1)} %collective-permute-done.6.refs_3_), channel_id=1, source_target_pairs={{0,1},{1,0},{2,3},{3,2},{4,5},{5,4},{6,7},{7,6},{8,9},{9,8},{10,11... | collective-permute-start | bytes 1253384 | tf_op jit(solution)/shard_map/ppermute | solution.py:247
  23.6 3.2 %collective-permute-done.2.refs_4_.refs_3_ = bf16[272,768]{1,0:T(8,128)(2,1)S(1)} collective-permute-done((bf16[272,768]{1,0:T(8,128)(2,1)}, bf16[272,768]{1,0:T(8,128)(2,1)S(1)}, u32[]{:S(2)}, u32[]{:S(2)}) %collective-permute-start.2) | collective-permute-done | bytes 417824 | tf_op jit(solution)/shard_map/ppermute | solution.py:246
  26.8 0.5 collective-permute-start.13
  27.2 0.0 collective-permute-done.9.refs_5_.refs_7_.refs_10_
  27.2 1.3 %collective-permute-start.3 = (bf16[272,768]{1,0:T(8,128)(2,1)S(1)}, bf16[272,768]{1,0:T(8,128)(2,1)}, u32[]{:S(2)}, u32[]{:S(2)}) collective-permute-start(bf16[272,768]{1,0:T(8,128)(2,1)S(1)} %collective-permute-done.refs_1_), channel_id=1, source_target_pairs={{96,0},{25,1},{98,2},{27,3},{100,4},{29,5},{102,6},{31,7},{104,8},... | collective-permute-start | bytes 1253384 | tf_op jit(solution)/shard_map/ppermute | solution.py:246
  28.5 0.0 collective-permute-done.10.refs_6_.refs_8_.refs_11_
  28.5 1.5 %collective-permute-start.4 = (bf16[272,768]{1,0:T(8,128)(2,1)S(1)}, bf16[272,768]{1,0:T(8,128)(2,1)}, u32[]{:S(2)}, u32[]{:S(2)}) collective-permute-start(bf16[272,768]{1,0:T(8,128)(2,1)S(1)} %collective-permute-done.refs_1_), channel_id=1, source_target_pairs={{32,0},{9,1},{34,2},{11,3},{36,4},{13,5},{38,6},{15,7},{40,8},{17,... | collective-permute-start | bytes 1253384 | tf_op jit(solution)/shard_map/ppermute | solution.py:246
  30.0 0.1 pad_add_fusion.place_ref
  30.1 0.0 collective-permute-done.11.refs_7_.refs_9_.refs_12_
  30.1 1.0 %copy-done = bf16[272,768]{1,0:T(8,128)(2,1)S(1)} copy-done((bf16[272,768]{1,0:T(8,128)(2,1)S(1)}, bf16[272,768]{1,0:T(8,128)(2,1)}, u32[]{:S(2)}) %copy-start) | copy-done | bytes 417816
  31.1 4.1 %pair_sums_0.1.refs_14_ = f32[22,1,256]{2,1,0:T(1,128)S(1)} custom-call(s32[4]{0:T(128)S(1)} %pad_add_fusion.place_ref, bf16[272,768]{1,0:T(8,128)(2,1)S(1)} %copy-done, bf16[272,768]{1,0:T(8,128)(2,1)S(1)} %collective-permute-done.refs_1_, bf16[272,768]{1,0:T(8,128)(2,1)S(1)} %collective-permute-done.1.refs_2_, ...), custom_call_target="tpu_custom_call" | custom-call | flops 2164260864 | tf_op jit(solution)/shard_map/pair_sums_0/pallas_call | solution.py:219
  35.2 0.5 collective-permute-done.3.refs_5_.refs_4_
  35.8 0.0 collective-permute-done.4.refs_6_.refs_5_
  35.8 1.3 %collective-permute-start.15 = (bf16[272,768]{1,0:T(8,128)(2,1)}, bf16[272,768]{1,0:T(8,128)(2,1)S(1)}, u32[]{:S(2)}, u32[]{:S(2)}) collective-permute-start(bf16[272,768]{1,0:T(8,128)(2,1)} %collective-permute-done.3.refs_5_.refs_4_), channel_id=1, source_target_pairs={{0,1},{1,0},{2,3},{3,2},{4,5},{5,4},{6,7},{7,6},{8,9},{9,8},{10,11... | collective-permute-start | bytes 1253384 | tf_op jit(solution)/shard_map/ppermute | solution.py:253
  37.1 0.0 collective-permute-start.16
  37.1 1.2 %collective-permute-start.5 = (bf16[272,768]{1,0:T(8,128)(2,1)S(1)}, bf16[272,768]{1,0:T(8,128)(2,1)S(1)}, u32[]{:S(2)}, u32[]{:S(2)}) collective-permute-start(bf16[272,768]{1,0:T(8,128)(2,1)S(1)} %collective-permute-done.1.refs_2_), channel_id=1, source_target_pairs={{6,0},{7,1},{0,2},{1,3},{2,4},{3,5},{4,6},{5,7},{14,8},{15,9},{8,1... | collective-permute-start | bytes 1253384 | tf_op jit(solution)/shard_map/ppermute | solution.py:246
  38.3 0.7 collective-permute-start.7
  39.1 3.0 %collective-permute-start.8 = (bf16[272,768]{1,0:T(8,128)(2,1)S(1)}, bf16[272,768]{1,0:T(8,128)(2,1)S(1)}, u32[]{:S(2)}, u32[]{:S(2)}) collective-permute-start(bf16[272,768]{1,0:T(8,128)(2,1)S(1)} %collective-permute-done.2.refs_4_.refs_3_), channel_id=1, source_target_pairs={{8,0},{33,1},{10,2},{35,3},{12,4},{37,5},{14,6},{39,7},{16,8},{41,... | collective-permute-start | bytes 1253384 | tf_op jit(solution)/shard_map/ppermute | solution.py:246
  42.0 0.0 collective-permute-start.14
  42.1 0.0 collective-permute-done.16.refs_13_.refs_16_
  42.1 4.1 %pair_sums_1.1.refs_17_ = f32[22,1,256]{2,1,0:T(1,128)S(1)} custom-call(s32[4]{0:T(128)S(1)} %pad_add_fusion.place_ref, bf16[272,768]{1,0:T(8,128)(2,1)S(1)} %copy-done.1, bf16[272,768]{1,0:T(8,128)(2,1)S(1)} %collective-permute-done.refs_1_, bf16[272,768]{1,0:T(8,128)(2,1)S(1)} %collective-permute-done.1.refs_2_, ...), custom_call_target="tpu_custom_call" | custom-call | flops 1962934272 | tf_op jit(solution)/shard_map/pair_sums_1/pallas_call | solution.py:219
  46.2 4.1 %collective-permute-done.5.refs_6_ = bf16[272,768]{1,0:T(8,128)(2,1)S(1)} collective-permute-done((bf16[272,768]{1,0:T(8,128)(2,1)S(1)}, bf16[272,768]{1,0:T(8,128)(2,1)S(1)}, u32[]{:S(2)}, u32[]{:S(2)}) %collective-permute-start.5) | collective-permute-done | bytes 417824 | tf_op jit(solution)/shard_map/ppermute | solution.py:246
  50.4 0.0 collective-permute-done.7.refs_7_
  50.4 0.0 collective-permute-done.8.refs_8_
  50.4 1.8 %collective-permute-done.14.refs_9_ = bf16[272,768]{1,0:T(8,128)(2,1)S(1)} collective-permute-done((bf16[272,768]{1,0:T(8,128)(2,1)S(1)}, bf16[272,768]{1,0:T(8,128)(2,1)S(1)}, u32[]{:S(2)}, u32[]{:S(2)}) %collective-permute-start.14) | collective-permute-done | bytes 417824 | tf_op jit(solution)/shard_map/ppermute | solution.py:252
  52.2 5.0 %pair_sums_2.1 = (f32[10,1,256]{2,1,0:T(1,128)S(1)}, f32[10,1,256]{2,1,0:T(1,128)S(1)}, f32[2,1,256]{2,1,0:T(1,128)S(1)}) custom-call(s32[4]{0:T(128)S(1)} %pad_add_fusion.place_ref, bf16[272,768]{1,0:T(8,128)(2,1)S(1)} %copy-done.1, bf16[272,768]{1,0:T(8,128)(2,1)S(1)} %collective-permute-done.refs_1_, bf16[272,768]{1,0:T(8,128)(2,1)S(1)} %collective-permute-done.1.refs_2_, ...), custom_call_target="tpu_custom_call" | custom-call | flops 2365587456 | tf_op jit(solution)/shard_map/pair_sums_2/pallas_call | solution.py:219
  57.1 0.1 collective-permute-start.17
  57.2 1.2 %collective-permute-done.17 = f32[10,1,256]{2,1,0:T(1,128)S(1)} collective-permute-done((f32[10,1,256]{2,1,0:T(1,128)S(1)}, f32[10,1,256]{2,1,0:T(1,128)S(1)}, u32[]{:S(2)}, u32[]{:S(2)}) %collective-permute-start.17) | collective-permute-done | bytes 10272 | tf_op jit(solution)/shard_map/ppermute | solution.py:257
  58.4 1.5 %collective-permute-start.18 = (f32[2,1,256]{2,1,0:T(1,128)S(1)}, f32[2,1,256]{2,1,0:T(1,128)S(1)}, u32[]{:S(2)}, u32[]{:S(2)}) collective-permute-start(f32[2,1,256]{2,1,0:T(1,128)S(1)} %get-tuple-element.19), channel_id=1, source_target_pairs={{0,46},{1,59},{2,40},{3,61},{4,42},{5,63},{6,44},{7,57},{8,54},{9,... | collective-permute-start | bytes 6152 | tf_op jit(solution)/shard_map/ppermute | solution.py:260
  59.9 5.0 %collective-permute-start.19 = (f32[2,1,256]{2,1,0:T(1,128)S(1)}, f32[2,1,256]{2,1,0:T(1,128)S(1)}, u32[]{:S(2)}, u32[]{:S(2)}) collective-permute-start(f32[2,1,256]{2,1,0:T(1,128)S(1)} %get-tuple-element.23), channel_id=1, source_target_pairs={{0,106},{1,123},{2,108},{3,125},{4,110},{5,127},{6,104},{7,121},{8... | collective-permute-start | bytes 6152 | tf_op jit(solution)/shard_map/ppermute | solution.py:260
  64.9 1.3 %collective-permute-start.20 = (f32[2,1,256]{2,1,0:T(1,128)S(1)}, f32[2,1,256]{2,1,0:T(1,128)S(1)}, u32[]{:S(2)}, u32[]{:S(2)}) collective-permute-start(f32[2,1,256]{2,1,0:T(1,128)S(1)} %get-tuple-element.22), channel_id=1, source_target_pairs={{0,26},{1,31},{2,28},{3,25},{4,30},{5,27},{6,24},{7,29},{8,2},{9,7... | collective-permute-start | bytes 6152 | tf_op jit(solution)/shard_map/ppermute | solution.py:260
  66.1 0.5 collective-permute-start.21
  66.7 2.7 %collective-permute-start.22 = (f32[2,1,256]{2,1,0:T(1,128)S(1)}, f32[2,1,256]{2,1,0:T(1,128)S(1)}, u32[]{:S(2)}, u32[]{:S(2)}) collective-permute-start(f32[2,1,256]{2,1,0:T(1,128)S(1)} %get-tuple-element.20), channel_id=1, source_target_pairs={{0,102},{1,7},{2,96},{3,1},{4,98},{5,3},{6,100},{7,5},{8,110},{9,1... | collective-permute-start | bytes 6152 | tf_op jit(solution)/shard_map/ppermute | solution.py:260
  69.4 1.3 %collective-permute-done.21 = f32[2,1,256]{2,1,0:T(1,128)S(1)} collective-permute-done((f32[2,1,256]{2,1,0:T(1,128)S(1)}, f32[2,1,256]{2,1,0:T(1,128)S(1)}, u32[]{:S(2)}, u32[]{:S(2)}) %collective-permute-start.21) | collective-permute-done | bytes 2080 | tf_op jit(solution)/shard_map/ppermute | solution.py:260
  70.7 2.8 %collective-permute-start.23 = (f32[256]{0:T(256)S(1)}, f32[256]{0:T(256)S(1)}, u32[]{:S(2)}, u32[]{:S(2)}) collective-permute-start(f32[256]{0:T(256)S(1)} %bitcast.9), channel_id=1, source_target_pairs={{0,1},{1,0},{2,3},{3,2},{4,5},{5,4},{6,7},{7,6},{8,9},{9,8},{10,11... | collective-permute-start | bytes 3080 | tf_op jit(solution)/shard_map/ppermute | solution.py:263
  73.6 0.8 %collective-permute-done.23 = f32[256]{0:T(256)S(1)} collective-permute-done((f32[256]{0:T(256)S(1)}, f32[256]{0:T(256)S(1)}, u32[]{:S(2)}, u32[]{:S(2)}) %collective-permute-start.23) | collective-permute-done | bytes 1056 | tf_op jit(solution)/shard_map/ppermute | solution.py:263
  74.4 0.6 add_log-plus-one_fusion
  (14 shorter events, 0.1 us)
Async XLA Ops:
  1.9 13.7 %collective-permute-start = (bf16[272,768]{1,0:T(8,128)(2,1)}, bf16[272,768]{1,0:T(8,128)(2,1)S(1)}, u32[]{:S(2)}, u32[]{:S(2)}) collective-permute-start(bf16[272,768]{1,0:T(8,128)(2,1)} %pack.1.refs_0_), channel_id=1, source_target_pairs={{26,0},{99,1},{28,2},{101,3},{30,4},{103,5},{24,6},{97,7},{2,8},{1... | collective-permute-start | bytes 1253384 | tf_op jit(solution)/shard_map/ppermute | solution.py:246
  6.6 12.3 %collective-permute-start.1 = (bf16[272,768]{1,0:T(8,128)(2,1)}, bf16[272,768]{1,0:T(8,128)(2,1)S(1)}, u32[]{:S(2)}, u32[]{:S(2)}) collective-permute-start(bf16[272,768]{1,0:T(8,128)(2,1)} %pack.1.refs_0_), channel_id=1, source_target_pairs={{40,0},{41,1},{42,2},{43,3},{44,4},{45,5},{46,6},{47,7},{48,8},{49... | collective-permute-start | bytes 1253384 | tf_op jit(solution)/shard_map/ppermute | solution.py:246
  10.1 10.3 %collective-permute-start.6 = (bf16[272,768]{1,0:T(8,128)(2,1)}, bf16[272,768]{1,0:T(8,128)(2,1)S(1)}, u32[]{:S(2)}, u32[]{:S(2)}) collective-permute-start(bf16[272,768]{1,0:T(8,128)(2,1)} %pack.1.refs_0_), channel_id=1, source_target_pairs={{6,0},{7,1},{0,2},{1,3},{2,4},{3,5},{4,6},{5,7},{14,8},{15,9},{8,1... | collective-permute-start | bytes 1253384 | tf_op jit(solution)/shard_map/ppermute | solution.py:246
  10.2 16.6 %collective-permute-start.2 = (bf16[272,768]{1,0:T(8,128)(2,1)}, bf16[272,768]{1,0:T(8,128)(2,1)S(1)}, u32[]{:S(2)}, u32[]{:S(2)}) collective-permute-start(bf16[272,768]{1,0:T(8,128)(2,1)} %pack.1.refs_0_), channel_id=1, source_target_pairs={{98,0},{27,1},{100,2},{29,3},{102,4},{31,5},{96,6},{25,7},{106,8},... | collective-permute-start | bytes 1253384 | tf_op jit(solution)/shard_map/ppermute | solution.py:246
  11.2 16.0 %collective-permute-start.9 = (bf16[272,768]{1,0:T(8,128)(2,1)}, bf16[272,768]{1,0:T(8,128)(2,1)S(1)}, u32[]{:S(2)}, u32[]{:S(2)}) collective-permute-start(bf16[272,768]{1,0:T(8,128)(2,1)} %pack.1.refs_0_), channel_id=1, source_target_pairs={{0,1},{1,0},{2,3},{3,2},{4,5},{5,4},{6,7},{7,6},{8,9},{9,8},{10,11... | collective-permute-start | bytes 1253384 | tf_op jit(solution)/shard_map/ppermute | solution.py:244
  15.6 12.9 %collective-permute-start.10 = (bf16[272,768]{1,0:T(8,128)(2,1)S(1)}, bf16[272,768]{1,0:T(8,128)(2,1)S(1)}, u32[]{:S(2)}, u32[]{:S(2)}) collective-permute-start(bf16[272,768]{1,0:T(8,128)(2,1)S(1)} %collective-permute-done.refs_1_), channel_id=1, source_target_pairs={{0,1},{1,0},{2,3},{3,2},{4,5},{5,4},{6,7},{7,6},{8,9},{9,8},{10,11... | collective-permute-start | bytes 1253384 | tf_op jit(solution)/shard_map/ppermute | solution.py:247
  18.9 11.2 %collective-permute-start.11 = (bf16[272,768]{1,0:T(8,128)(2,1)S(1)}, bf16[272,768]{1,0:T(8,128)(2,1)S(1)}, u32[]{:S(2)}, u32[]{:S(2)}) collective-permute-start(bf16[272,768]{1,0:T(8,128)(2,1)S(1)} %collective-permute-done.1.refs_2_), channel_id=1, source_target_pairs={{0,1},{1,0},{2,3},{3,2},{4,5},{5,4},{6,7},{7,6},{8,9},{9,8},{10,11... | collective-permute-start | bytes 1253384 | tf_op jit(solution)/shard_map/ppermute | solution.py:247
  20.4 9.7 %collective-permute-start.12 = (bf16[272,768]{1,0:T(8,128)(2,1)S(1)}, bf16[272,768]{1,0:T(8,128)(2,1)S(1)}, u32[]{:S(2)}, u32[]{:S(2)}) collective-permute-start(bf16[272,768]{1,0:T(8,128)(2,1)S(1)} %collective-permute-done.6.refs_3_), channel_id=1, source_target_pairs={{0,1},{1,0},{2,3},{3,2},{4,5},{5,4},{6,7},{7,6},{8,9},{9,8},{10,11... | collective-permute-start | bytes 1253384 | tf_op jit(solution)/shard_map/ppermute | solution.py:247
  26.8 3.4 %collective-permute-start.13 = (bf16[272,768]{1,0:T(8,128)(2,1)S(1)}, bf16[272,768]{1,0:T(8,128)(2,1)}, u32[]{:S(2)}, u32[]{:S(2)}) collective-permute-start(bf16[272,768]{1,0:T(8,128)(2,1)S(1)} %collective-permute-done.2.refs_4_.refs_3_), channel_id=1, source_target_pairs={{0,1},{1,0},{2,3},{3,2},{4,5},{5,4},{6,7},{7,6},{8,9},{9,8},{10,11... | collective-permute-start | bytes 1253384 | tf_op jit(solution)/shard_map/ppermute | solution.py:247
  27.2 8.6 %collective-permute-start.3 = (bf16[272,768]{1,0:T(8,128)(2,1)S(1)}, bf16[272,768]{1,0:T(8,128)(2,1)}, u32[]{:S(2)}, u32[]{:S(2)}) collective-permute-start(bf16[272,768]{1,0:T(8,128)(2,1)S(1)} %collective-permute-done.refs_1_), channel_id=1, source_target_pairs={{96,0},{25,1},{98,2},{27,3},{100,4},{29,5},{102,6},{31,7},{104,8},... | collective-permute-start | bytes 1253384 | tf_op jit(solution)/shard_map/ppermute | solution.py:246
  28.5 7.3 %collective-permute-start.4 = (bf16[272,768]{1,0:T(8,128)(2,1)S(1)}, bf16[272,768]{1,0:T(8,128)(2,1)}, u32[]{:S(2)}, u32[]{:S(2)}) collective-permute-start(bf16[272,768]{1,0:T(8,128)(2,1)S(1)} %collective-permute-done.refs_1_), channel_id=1, source_target_pairs={{32,0},{9,1},{34,2},{11,3},{36,4},{13,5},{38,6},{15,7},{40,8},{17,... | collective-permute-start | bytes 1253384 | tf_op jit(solution)/shard_map/ppermute | solution.py:246
  30.1 1.0 %copy-start = (bf16[272,768]{1,0:T(8,128)(2,1)S(1)}, bf16[272,768]{1,0:T(8,128)(2,1)}, u32[]{:S(2)}) copy-start(bf16[272,768]{1,0:T(8,128)(2,1)} %pack.1.refs_0_) | copy-start | bytes 1253380
  31.1 10.9 %copy-start.1 = (bf16[272,768]{1,0:T(8,128)(2,1)S(1)}, bf16[272,768]{1,0:T(8,128)(2,1)}, u32[]{:S(2)}) copy-start(bf16[272,768]{1,0:T(8,128)(2,1)} %pack.1.refs_0_) | copy-start | bytes 1253380
  35.8 6.2 %collective-permute-start.15 = (bf16[272,768]{1,0:T(8,128)(2,1)}, bf16[272,768]{1,0:T(8,128)(2,1)S(1)}, u32[]{:S(2)}, u32[]{:S(2)}) collective-permute-start(bf16[272,768]{1,0:T(8,128)(2,1)} %collective-permute-done.3.refs_5_.refs_4_), channel_id=1, source_target_pairs={{0,1},{1,0},{2,3},{3,2},{4,5},{5,4},{6,7},{7,6},{8,9},{9,8},{10,11... | collective-permute-start | bytes 1253384 | tf_op jit(solution)/shard_map/ppermute | solution.py:253
  37.1 4.9 %collective-permute-start.16 = (bf16[272,768]{1,0:T(8,128)(2,1)}, bf16[272,768]{1,0:T(8,128)(2,1)S(1)}, u32[]{:S(2)}, u32[]{:S(2)}) collective-permute-start(bf16[272,768]{1,0:T(8,128)(2,1)} %collective-permute-done.4.refs_6_.refs_5_), channel_id=1, source_target_pairs={{0,1},{1,0},{2,3},{3,2},{4,5},{5,4},{6,7},{7,6},{8,9},{9,8},{10,11... | collective-permute-start | bytes 1253384 | tf_op jit(solution)/shard_map/ppermute | solution.py:253
  37.1 13.2 %collective-permute-start.5 = (bf16[272,768]{1,0:T(8,128)(2,1)S(1)}, bf16[272,768]{1,0:T(8,128)(2,1)S(1)}, u32[]{:S(2)}, u32[]{:S(2)}) collective-permute-start(bf16[272,768]{1,0:T(8,128)(2,1)S(1)} %collective-permute-done.1.refs_2_), channel_id=1, source_target_pairs={{6,0},{7,1},{0,2},{1,3},{2,4},{3,5},{4,6},{5,7},{14,8},{15,9},{8,1... | collective-permute-start | bytes 1253384 | tf_op jit(solution)/shard_map/ppermute | solution.py:246
  38.3 12.0 %collective-permute-start.7 = (bf16[272,768]{1,0:T(8,128)(2,1)S(1)}, bf16[272,768]{1,0:T(8,128)(2,1)S(1)}, u32[]{:S(2)}, u32[]{:S(2)}) collective-permute-start(bf16[272,768]{1,0:T(8,128)(2,1)S(1)} %collective-permute-done.6.refs_3_), channel_id=1, source_target_pairs={{96,0},{25,1},{98,2},{27,3},{100,4},{29,5},{102,6},{31,7},{104,8},... | collective-permute-start | bytes 1253384 | tf_op jit(solution)/shard_map/ppermute | solution.py:246
  39.1 11.3 %collective-permute-start.8 = (bf16[272,768]{1,0:T(8,128)(2,1)S(1)}, bf16[272,768]{1,0:T(8,128)(2,1)S(1)}, u32[]{:S(2)}, u32[]{:S(2)}) collective-permute-start(bf16[272,768]{1,0:T(8,128)(2,1)S(1)} %collective-permute-done.2.refs_4_.refs_3_), channel_id=1, source_target_pairs={{8,0},{33,1},{10,2},{35,3},{12,4},{37,5},{14,6},{39,7},{16,8},{41,... | collective-permute-start | bytes 1253384 | tf_op jit(solution)/shard_map/ppermute | solution.py:246
  42.0 10.1 %collective-permute-start.14 = (bf16[272,768]{1,0:T(8,128)(2,1)S(1)}, bf16[272,768]{1,0:T(8,128)(2,1)S(1)}, u32[]{:S(2)}, u32[]{:S(2)}) collective-permute-start(bf16[272,768]{1,0:T(8,128)(2,1)S(1)} %collective-permute-done.6.refs_3_), channel_id=1, source_target_pairs={{24,0},{97,1},{26,2},{99,3},{28,4},{101,5},{30,6},{103,7},{0,8},{1... | collective-permute-start | bytes 1253384 | tf_op jit(solution)/shard_map/ppermute | solution.py:252
  57.1 1.3 %collective-permute-start.17 = (f32[10,1,256]{2,1,0:T(1,128)S(1)}, f32[10,1,256]{2,1,0:T(1,128)S(1)}, u32[]{:S(2)}, u32[]{:S(2)}) collective-permute-start(f32[10,1,256]{2,1,0:T(1,128)S(1)} %get-tuple-element.18), channel_id=1, source_target_pairs={{0,1},{1,0},{2,3},{3,2},{4,5},{5,4},{6,7},{7,6},{8,9},{9,8},{10,11... | collective-permute-start | bytes 30728 | tf_op jit(solution)/shard_map/ppermute | solution.py:257
  58.4 11.0 %collective-permute-start.18 = (f32[2,1,256]{2,1,0:T(1,128)S(1)}, f32[2,1,256]{2,1,0:T(1,128)S(1)}, u32[]{:S(2)}, u32[]{:S(2)}) collective-permute-start(f32[2,1,256]{2,1,0:T(1,128)S(1)} %get-tuple-element.19), channel_id=1, source_target_pairs={{0,46},{1,59},{2,40},{3,61},{4,42},{5,63},{6,44},{7,57},{8,54},{9,... | collective-permute-start | bytes 6152 | tf_op jit(solution)/shard_map/ppermute | solution.py:260
  59.9 9.5 %collective-permute-start.19 = (f32[2,1,256]{2,1,0:T(1,128)S(1)}, f32[2,1,256]{2,1,0:T(1,128)S(1)}, u32[]{:S(2)}, u32[]{:S(2)}) collective-permute-start(f32[2,1,256]{2,1,0:T(1,128)S(1)} %get-tuple-element.23), channel_id=1, source_target_pairs={{0,106},{1,123},{2,108},{3,125},{4,110},{5,127},{6,104},{7,121},{8... | collective-permute-start | bytes 6152 | tf_op jit(solution)/shard_map/ppermute | solution.py:260
  64.9 4.5 %collective-permute-start.20 = (f32[2,1,256]{2,1,0:T(1,128)S(1)}, f32[2,1,256]{2,1,0:T(1,128)S(1)}, u32[]{:S(2)}, u32[]{:S(2)}) collective-permute-start(f32[2,1,256]{2,1,0:T(1,128)S(1)} %get-tuple-element.22), channel_id=1, source_target_pairs={{0,26},{1,31},{2,28},{3,25},{4,30},{5,27},{6,24},{7,29},{8,2},{9,7... | collective-permute-start | bytes 6152 | tf_op jit(solution)/shard_map/ppermute | solution.py:260
  66.1 4.5 %collective-permute-start.21 = (f32[2,1,256]{2,1,0:T(1,128)S(1)}, f32[2,1,256]{2,1,0:T(1,128)S(1)}, u32[]{:S(2)}, u32[]{:S(2)}) collective-permute-start(f32[2,1,256]{2,1,0:T(1,128)S(1)} %get-tuple-element.21), channel_id=1, source_target_pairs={{0,40},{1,99},{2,42},{3,101},{4,44},{5,103},{6,46},{7,97},{8,48},{... | collective-permute-start | bytes 6152 | tf_op jit(solution)/shard_map/ppermute | solution.py:260
  66.7 4.0 %collective-permute-start.22 = (f32[2,1,256]{2,1,0:T(1,128)S(1)}, f32[2,1,256]{2,1,0:T(1,128)S(1)}, u32[]{:S(2)}, u32[]{:S(2)}) collective-permute-start(f32[2,1,256]{2,1,0:T(1,128)S(1)} %get-tuple-element.20), channel_id=1, source_target_pairs={{0,102},{1,7},{2,96},{3,1},{4,98},{5,3},{6,100},{7,5},{8,110},{9,1... | collective-permute-start | bytes 6152 | tf_op jit(solution)/shard_map/ppermute | solution.py:260
  70.7 3.7 %collective-permute-start.23 = (f32[256]{0:T(256)S(1)}, f32[256]{0:T(256)S(1)}, u32[]{:S(2)}, u32[]{:S(2)}) collective-permute-start(f32[256]{0:T(256)S(1)} %bitcast.9), channel_id=1, source_target_pairs={{0,1},{1,0},{2,3},{3,2},{4,5},{5,4},{6,7},{7,6},{8,9},{9,8},{10,11... | collective-permute-start | bytes 3080 | tf_op jit(solution)/shard_map/ppermute | solution.py:263

commit v4 on v3

--- a/solution.py
+++ b/solution.py
@@ -18,7 +18,7 @@
 PLAN = ((0, 13), (0, 20), (0, 3), (0, 49), (1, 48), (1, 16), (2, 3), (3, 48), (4, 4), (3, 12))
 SWAPPED = 7
 BLOCKS = len(PLAN) + 1
-PHASES = ((5, 5), (7, 7), (BLOCKS, SWAPPED))
+PHASES = ((4, 4), (7, 4), (BLOCKS, 4), (BLOCKS, SWAPPED))
 
 
 def shift(place, by):
@@ -116,7 +116,7 @@
 def pack(embeddings, destination):
     return pl.pallas_call(
         pack_body,
-        out_shape=jax.ShapeDtypeStruct((ROWS + LABEL_ROWS, WIDTH), jnp.bfloat16),
+        out_shape=pltpu.VMEM((ROWS + LABEL_ROWS, WIDTH), jnp.bfloat16),
         name="pack",
     )(embeddings, destination.reshape(1, ROWS))
 
@@ -241,18 +241,18 @@
     place = jnp.stack([core, x, jnp.where(core == 0, y, z), jnp.where(core == 0, z, y)]).astype(jnp.int32)
 
     mine = [pack(embeddings, destination)]
-    other = [lax.ppermute(mine[0], BOTH, CORE_SWAP)]
-    for source, jump in PLAN[:-1]:
+    for source, jump in PLAN[:8]:
         mine.append(lax.ppermute(mine[source], BOTH, fetch((jump, mirror(jump)))))
-    other += [lax.ppermute(block, BOTH, CORE_SWAP) for block in mine[1 : PHASES[0][1]]]
+    other = [lax.ppermute(block, BOTH, CORE_SWAP) for block in mine[0:4]]
     (sums,) = pair_sums(0, place, mine, other, None)
-
-    source, jump = PLAN[-1]
-    source, later, sums = lax.optimization_barrier((mine[source], mine[PHASES[0][1] : SWAPPED], sums))
-    mine.append(lax.ppermute(source, BOTH, fetch((jump, mirror(jump)))))
+    held, sums = lax.optimization_barrier((mine[4], sums))
+    for source, jump in PLAN[8:]:
+        mine.append(lax.ppermute(held if source == 4 else mine[source], BOTH, fetch((jump, mirror(jump)))))
+    (sums,) = pair_sums(1, place, mine, other, sums)
+    later, sums = lax.optimization_barrier((mine[4:SWAPPED], sums))
     other += [lax.ppermute(block, BOTH, CORE_SWAP) for block in later]
-    (sums,) = pair_sums(1, place, mine, other, sums)
-    kept, given, home = pair_sums(2, place, mine, other, sums)
+    (sums,) = pair_sums(2, place, mine, other, sums)
+    kept, given, home = pair_sums(3, place, mine, other, sums)
 
     kept += lax.ppermute(given, BOTH, CORE_SWAP)
     for n in range(SHARE):

time: 75.2 us -> 66.4 us (0.88)
  waiting for transfers between devices: 17.1 us -> 9.36 us
  local copies, waits for them, and re-layouts: 1.01 us -> 0.01 us
    ppermute x9 -> x8, waiting for transfers between devices: 12 us -> 5.31 us  [shards(): mine.append(lax.ppermute(mine[source], BOTH, fetch((jump, mirror(jump)))))]
    ppermute x5, starting transfers between devices: 11 us -> 9.77 us  [shards(): home += lax.ppermute(kept[2 * n:2 * n + 2], BOTH, give(jumps))]
    ppermute x2 -> x3, starting transfers between devices: 1.32 us -> 2.5 us  [shards(): other += [lax.ppermute(block, BOTH, CORE_SWAP) for block in later]]
    unnamed x4 -> x0, local copies, waits for them, and re-layouts: 1 us -> none
    pallas_call x3 -> x4, Pallas kernels: 13.2 us -> 14 us  [pair_sums(): pl.pallas_call(functools.partial(pairs_body, work, mine_used, other_used,...]
    pallas_call x1, Pallas kernels: 1.94 us -> 1.16 us  [pack(): pl.pallas_call(pack_body, out_shape=pltpu.VMEM((ROWS + LABEL_ROWS, WIDTH)...]
    ppermute x9 -> x8, starting transfers between devices: 17 us -> 16.5 us  [shards(): mine.append(lax.ppermute(mine[source], BOTH, fetch((jump, mirror(jump)))))]
  transfers between devices with their start and end apart: 24 -> 24, of which waited for: 10 -> 8; matrix products, arithmetic and copies ran while one was open for 0% -> 0% of each run, Pallas kernels for 11% -> 19%
where the time goes in v4:
time: 66.4 us; the launch traced here: 66.2 us
  starting transfers between devices  40.9 us (62%)
  Pallas kernels  15.2 us (23%)
  waiting for transfers between devices  9.36 us (14%)
  other arithmetic  0.68 us (1%)
    ppermute x8, starting transfers between devices, shards(): mine.append(lax.ppermute(mine[source], BOTH, fetch((jump, mirror(jump)))))  16.5 us
    pallas_call x4, Pallas kernels, pair_sums(): pl.pallas_call(functools.partial(pairs_body, work, mine_used, other_used,...  14 us
    ppermute x5, starting transfers between devices, shards(): home += lax.ppermute(kept[2 * n:2 * n + 2], BOTH, give(jumps))  9.77 us
    ppermute x4, starting transfers between devices, shards(): other = [lax.ppermute(block, BOTH, CORE_SWAP) for block in mine[0:4]]  5.89 us
    ppermute x8, waiting for transfers between devices, shards(): mine.append(lax.ppermute(mine[source], BOTH, fetch((jump, mirror(jump)))))  5.31 us
    ppermute x1, starting transfers between devices, shards(): return jnp.log1p(own + lax.ppermute(rest, BOTH, CORE_SWAP))  3.38 us
    ppermute x2, starting transfers between devices, shards(): lax.ppermute(held if source == 4 else mine[source], BOTH, fetch((jump, mi...  2.73 us
    ppermute x3, starting transfers between devices, shards(): other += [lax.ppermute(block, BOTH, CORE_SWAP) for block in later]  2.5 us
  transfers between devices with their start and end apart: 24, of which 8 were waited for; matrix products, arithmetic and copies ran while one was open for 0% of the time, Pallas kernels for 19%

profile of v4, /device:TPU:1, one launch (start us, length us, event | category | flops | bytes accessed | tf_op | source)
XLA Modules:
  0.0 66.2 jit_solution(10700551462901843926)
XLA Ops:
  0.0 1.2 %pack.1.refs_0_ = bf16[272,768]{1,0:T(8,128)(2,1)S(1)} custom-call(bf16[256,768]{1,0:T(8,128)(2,1)} %rows_ref.1, s32[1,256]{1,0:T(1,128)} %bitcast.8), custom_call_target="tpu_custom_call" | custom-call | tf_op jit(solution)/shard_map/pack/pallas_call | solution.py:117
  1.2 4.7 %collective-permute-start.1 = (bf16[272,768]{1,0:T(8,128)(2,1)S(1)}, bf16[272,768]{1,0:T(8,128)(2,1)S(1)}, u32[]{:S(2)}, u32[]{:S(2)}) collective-permute-start(bf16[272,768]{1,0:T(8,128)(2,1)S(1)} %pack.1.refs_0_), channel_id=1, source_target_pairs={{26,0},{99,1},{28,2},{101,3},{30,4},{103,5},{24,6},{97,7},{2,8},{1... | collective-permute-start | bytes 1253384 | tf_op jit(solution)/shard_map/ppermute | solution.py:245
  5.9 3.5 %collective-permute-start.3 = (bf16[272,768]{1,0:T(8,128)(2,1)S(1)}, bf16[272,768]{1,0:T(8,128)(2,1)S(1)}, u32[]{:S(2)}, u32[]{:S(2)}) collective-permute-start(bf16[272,768]{1,0:T(8,128)(2,1)S(1)} %pack.1.refs_0_), channel_id=1, source_target_pairs={{40,0},{41,1},{42,2},{43,3},{44,4},{45,5},{46,6},{47,7},{48,8},{49... | collective-permute-start | bytes 1253384 | tf_op jit(solution)/shard_map/ppermute | solution.py:245
  9.4 0.2 collective-permute-start.5
  9.6 2.1 %collective-permute-start.6 = (bf16[272,768]{1,0:T(8,128)(2,1)S(1)}, bf16[272,768]{1,0:T(8,128)(2,1)S(1)}, u32[]{:S(2)}, u32[]{:S(2)}) collective-permute-start(bf16[272,768]{1,0:T(8,128)(2,1)S(1)} %pack.1.refs_0_), channel_id=1, source_target_pairs={{0,1},{1,0},{2,3},{3,2},{4,5},{5,4},{6,7},{7,6},{8,9},{9,8},{10,11... | collective-permute-start | bytes 1253384 | tf_op jit(solution)/shard_map/ppermute | solution.py:246
  11.6 2.8 %collective-permute-start = (bf16[272,768]{1,0:T(8,128)(2,1)S(1)}, bf16[272,768]{1,0:T(8,128)(2,1)S(1)}, u32[]{:S(2)}, u32[]{:S(2)}) collective-permute-start(bf16[272,768]{1,0:T(8,128)(2,1)S(1)} %pack.1.refs_0_), channel_id=1, source_target_pairs={{98,0},{27,1},{100,2},{29,3},{102,4},{31,5},{96,6},{25,7},{106,8},... | collective-permute-start | bytes 1253384 | tf_op jit(solution)/shard_map/ppermute | solution.py:245
  14.4 0.2 collective-permute-done.1.refs_1_
  14.6 2.1 %collective-permute-start.7 = (bf16[272,768]{1,0:T(8,128)(2,1)S(1)}, bf16[272,768]{1,0:T(8,128)(2,1)S(1)}, u32[]{:S(2)}, u32[]{:S(2)}) collective-permute-start(bf16[272,768]{1,0:T(8,128)(2,1)S(1)} %collective-permute-done.1.refs_1_), channel_id=1, source_target_pairs={{0,1},{1,0},{2,3},{3,2},{4,5},{5,4},{6,7},{7,6},{8,9},{9,8},{10,11... | collective-permute-start | bytes 1253384 | tf_op jit(solution)/shard_map/ppermute | solution.py:246
  16.7 1.3 %collective-permute-done.3.refs_2_ = bf16[272,768]{1,0:T(8,128)(2,1)S(1)} collective-permute-done((bf16[272,768]{1,0:T(8,128)(2,1)S(1)}, bf16[272,768]{1,0:T(8,128)(2,1)S(1)}, u32[]{:S(2)}, u32[]{:S(2)}) %collective-permute-start.3) | collective-permute-done | bytes 417824 | tf_op jit(solution)/shard_map/ppermute | solution.py:245
  18.0 1.3 %collective-permute-start.8 = (bf16[272,768]{1,0:T(8,128)(2,1)S(1)}, bf16[272,768]{1,0:T(8,128)(2,1)}, u32[]{:S(2)}, u32[]{:S(2)}) collective-permute-start(bf16[272,768]{1,0:T(8,128)(2,1)S(1)} %collective-permute-done.3.refs_2_), channel_id=1, source_target_pairs={{0,1},{1,0},{2,3},{3,2},{4,5},{5,4},{6,7},{7,6},{8,9},{9,8},{10,11... | collective-permute-start | bytes 1253384 | tf_op jit(solution)/shard_map/ppermute | solution.py:246
  19.2 0.2 collective-permute-done.5.refs_3_
  19.5 2.8 %collective-permute-start.2 = (bf16[272,768]{1,0:T(8,128)(2,1)S(1)}, bf16[272,768]{1,0:T(8,128)(2,1)S(1)}, u32[]{:S(2)}, u32[]{:S(2)}) collective-permute-start(bf16[272,768]{1,0:T(8,128)(2,1)S(1)} %collective-permute-done.1.refs_1_), channel_id=1, source_target_pairs={{32,0},{9,1},{34,2},{11,3},{36,4},{13,5},{38,6},{15,7},{40,8},{17,... | collective-permute-start | bytes 1253384 | tf_op jit(solution)/shard_map/ppermute | solution.py:245
  22.2 0.0 collective-permute-done.6.refs_4_.refs_7_.refs_10_
  22.2 0.0 collective-permute-start.10
  22.2 3.6 %collective-permute-done.refs_4_.refs_3_.refs_0_ = bf16[272,768]{1,0:T(8,128)(2,1)S(1)} collective-permute-done((bf16[272,768]{1,0:T(8,128)(2,1)S(1)}, bf16[272,768]{1,0:T(8,128)(2,1)S(1)}, u32[]{:S(2)}, u32[]{:S(2)}) %collective-permute-start) | collective-permute-done | bytes 417824 | tf_op jit(solution)/shard_map/ppermute | solution.py:245
  25.8 0.5 collective-permute-start.11
  26.3 1.2 %collective-permute-start.4 = (bf16[272,768]{1,0:T(8,128)(2,1)S(1)}, bf16[272,768]{1,0:T(8,128)(2,1)S(1)}, u32[]{:S(2)}, u32[]{:S(2)}) collective-permute-start(bf16[272,768]{1,0:T(8,128)(2,1)S(1)} %collective-permute-done.3.refs_2_), channel_id=1, source_target_pairs={{6,0},{7,1},{0,2},{1,3},{2,4},{3,5},{4,6},{5,7},{14,8},{15,9},{8,1... | collective-permute-start | bytes 1253384 | tf_op jit(solution)/shard_map/ppermute | solution.py:245
  27.5 1.4 %collective-permute-start.15 = (bf16[272,768]{1,0:T(8,128)(2,1)S(1)}, bf16[272,768]{1,0:T(8,128)(2,1)S(1)}, u32[]{:S(2)}, u32[]{:S(2)}) collective-permute-start(bf16[272,768]{1,0:T(8,128)(2,1)S(1)} %collective-permute-done.5.refs_3_), channel_id=1, source_target_pairs={{96,0},{25,1},{98,2},{27,3},{100,4},{29,5},{102,6},{31,7},{104,8},... | collective-permute-start | bytes 1253384 | tf_op jit(solution)/shard_map/ppermute | solution.py:245
  28.9 0.1 pad_add_fusion.place_ref
  29.0 3.1 %pair_sums_0.1.refs_11_ = f32[22,1,256]{2,1,0:T(1,128)S(1)} custom-call(s32[4]{0:T(128)S(1)} %pad_add_fusion.place_ref, bf16[272,768]{1,0:T(8,128)(2,1)S(1)} %pack.1.refs_0_, bf16[272,768]{1,0:T(8,128)(2,1)S(1)} %collective-permute-done.1.refs_1_, bf16[272,768]{1,0:T(8,128)(2,1)S(1)} %collective-permute-done.3.refs_2_, ...), custom_call_target="tpu_custom_call" | custom-call | flops 1409286144 | tf_op jit(solution)/shard_map/pair_sums_0/pallas_call | solution.py:219
  32.0 0.0 collective-permute-done.2.refs_6_.refs_5_.refs_1_
  32.0 0.1 collective-permute-start.16
  32.1 2.7 %collective-permute-start.9 = (bf16[272,768]{1,0:T(8,128)(2,1)S(1)}, bf16[272,768]{1,0:T(8,128)(2,1)S(1)}, u32[]{:S(2)}, u32[]{:S(2)}) collective-permute-start(bf16[272,768]{1,0:T(8,128)(2,1)S(1)} %collective-permute-done.refs_4_.refs_3_.refs_0_), channel_id=1, source_target_pairs={{8,0},{33,1},{10,2},{35,3},{12,4},{37,5},{14,6},{39,7},{16,8},{41,... | collective-permute-start | bytes 1253384 | tf_op jit(solution)/shard_map/ppermute | solution.py:250
  34.8 0.0 collective-permute-done.11.refs_10_.refs_13_
  34.8 4.6 %pair_sums_1.1.refs_14_ = f32[22,1,256]{2,1,0:T(1,128)S(1)} custom-call(s32[4]{0:T(128)S(1)} %pad_add_fusion.place_ref, bf16[272,768]{1,0:T(8,128)(2,1)S(1)} %pack.1.refs_0_, bf16[272,768]{1,0:T(8,128)(2,1)S(1)} %collective-permute-done.1.refs_1_, bf16[272,768]{1,0:T(8,128)(2,1)S(1)} %collective-permute-done.3.refs_2_, ...), custom_call_target="tpu_custom_call" | custom-call | flops 2415919104 | tf_op jit(solution)/shard_map/pair_sums_1/pallas_call | solution.py:219
  39.4 1.4 %collective-permute-start.12 = (bf16[272,768]{1,0:T(8,128)(2,1)S(1)}, bf16[272,768]{1,0:T(8,128)(2,1)S(1)}, u32[]{:S(2)}, u32[]{:S(2)}) collective-permute-start(bf16[272,768]{1,0:T(8,128)(2,1)S(1)} %collective-permute-done.refs_4_.refs_3_.refs_0_), channel_id=1, source_target_pairs={{0,1},{1,0},{2,3},{3,2},{4,5},{5,4},{6,7},{7,6},{8,9},{9,8},{10,11... | collective-permute-start | bytes 1253384 | tf_op jit(solution)/shard_map/ppermute | solution.py:253
  40.8 0.1 collective-permute-start.13
  40.9 1.0 %collective-permute-start.14 = (bf16[272,768]{1,0:T(8,128)(2,1)S(1)}, bf16[272,768]{1,0:T(8,128)(2,1)S(1)}, u32[]{:S(2)}, u32[]{:S(2)}) collective-permute-start(bf16[272,768]{1,0:T(8,128)(2,1)S(1)} %collective-permute-done.2.refs_6_.refs_5_.refs_1_), channel_id=1, source_target_pairs={{0,1},{1,0},{2,3},{3,2},{4,5},{5,4},{6,7},{7,6},{8,9},{9,8},{10,11... | collective-permute-start | bytes 1253384 | tf_op jit(solution)/shard_map/ppermute | solution.py:253
  41.9 1.1 %collective-permute-done.16.refs_9_ = bf16[272,768]{1,0:T(8,128)(2,1)S(1)} collective-permute-done((bf16[272,768]{1,0:T(8,128)(2,1)S(1)}, bf16[272,768]{1,0:T(8,128)(2,1)S(1)}, u32[]{:S(2)}, u32[]{:S(2)}) %collective-permute-start.16) | collective-permute-done | bytes 417824 | tf_op jit(solution)/shard_map/ppermute | solution.py:250
  43.0 4.7 %pair_sums_2.1.refs_7_ = f32[22,1,256]{2,1,0:T(1,128)S(1)} custom-call(s32[4]{0:T(128)S(1)} %pad_add_fusion.place_ref, bf16[272,768]{1,0:T(8,128)(2,1)S(1)} %pack.1.refs_0_, bf16[272,768]{1,0:T(8,128)(2,1)S(1)} %collective-permute-done.1.refs_1_, bf16[272,768]{1,0:T(8,128)(2,1)S(1)} %collective-permute-done.3.refs_2_, ...), custom_call_target="tpu_custom_call" | custom-call | flops 2113929216 | tf_op jit(solution)/shard_map/pair_sums_2/pallas_call | solution.py:219
  47.7 0.0 collective-permute-done.12.refs_4_
  47.7 0.0 collective-permute-done.13.refs_5_
  47.7 1.7 %pair_sums_3.1 = (f32[10,1,256]{2,1,0:T(1,128)S(1)}, f32[10,1,256]{2,1,0:T(1,128)S(1)}, f32[2,1,256]{2,1,0:T(1,128)S(1)}) custom-call(s32[4]{0:T(128)S(1)} %pad_add_fusion.place_ref, bf16[272,768]{1,0:T(8,128)(2,1)S(1)} %collective-permute-done.refs_4_.refs_3_.refs_0_, bf16[272,768]{1,0:T(8,128)(2,1)S(1)} %collective-permute-done.2.refs_6_.refs_5_.refs_1_, ...), custom_call_target="tpu_custom_call" | custom-call | flops 553648128 | tf_op jit(solution)/shard_map/pair_sums_3/pallas_call | solution.py:219
  49.4 0.1 collective-permute-start.17
  49.5 1.2 %collective-permute-done.17 = f32[10,1,256]{2,1,0:T(1,128)S(1)} collective-permute-done((f32[10,1,256]{2,1,0:T(1,128)S(1)}, f32[10,1,256]{2,1,0:T(1,128)S(1)}, u32[]{:S(2)}, u32[]{:S(2)}) %collective-permute-start.17) | collective-permute-done | bytes 10272 | tf_op jit(solution)/shard_map/ppermute | solution.py:257
  50.7 4.1 %collective-permute-start.18 = (f32[2,1,256]{2,1,0:T(1,128)S(1)}, f32[2,1,256]{2,1,0:T(1,128)S(1)}, u32[]{:S(2)}, u32[]{:S(2)}) collective-permute-start(f32[2,1,256]{2,1,0:T(1,128)S(1)} %get-tuple-element.23), channel_id=1, source_target_pairs={{0,46},{1,59},{2,40},{3,61},{4,42},{5,63},{6,44},{7,57},{8,54},{9,... | collective-permute-start | bytes 6152 | tf_op jit(solution)/shard_map/ppermute | solution.py:260
  54.8 1.1 %collective-permute-start.19 = (f32[2,1,256]{2,1,0:T(1,128)S(1)}, f32[2,1,256]{2,1,0:T(1,128)S(1)}, u32[]{:S(2)}, u32[]{:S(2)}) collective-permute-start(f32[2,1,256]{2,1,0:T(1,128)S(1)} %get-tuple-element.27), channel_id=1, source_target_pairs={{0,106},{1,123},{2,108},{3,125},{4,110},{5,127},{6,104},{7,121},{8... | collective-permute-start | bytes 6152 | tf_op jit(solution)/shard_map/ppermute | solution.py:260
  55.9 1.0 %collective-permute-start.20 = (f32[2,1,256]{2,1,0:T(1,128)S(1)}, f32[2,1,256]{2,1,0:T(1,128)S(1)}, u32[]{:S(2)}, u32[]{:S(2)}) collective-permute-start(f32[2,1,256]{2,1,0:T(1,128)S(1)} %get-tuple-element.26), channel_id=1, source_target_pairs={{0,26},{1,31},{2,28},{3,25},{4,30},{5,27},{6,24},{7,29},{8,2},{9,7... | collective-permute-start | bytes 6152 | tf_op jit(solution)/shard_map/ppermute | solution.py:260
  56.9 1.0 %collective-permute-start.21 = (f32[2,1,256]{2,1,0:T(1,128)S(1)}, f32[2,1,256]{2,1,0:T(1,128)S(1)}, u32[]{:S(2)}, u32[]{:S(2)}) collective-permute-start(f32[2,1,256]{2,1,0:T(1,128)S(1)} %get-tuple-element.25), channel_id=1, source_target_pairs={{0,40},{1,99},{2,42},{3,101},{4,44},{5,103},{6,46},{7,97},{8,48},{... | collective-permute-start | bytes 6152 | tf_op jit(solution)/shard_map/ppermute | solution.py:260
  57.9 2.5 %collective-permute-start.22 = (f32[2,1,256]{2,1,0:T(1,128)S(1)}, f32[2,1,256]{2,1,0:T(1,128)S(1)}, u32[]{:S(2)}, u32[]{:S(2)}) collective-permute-start(f32[2,1,256]{2,1,0:T(1,128)S(1)} %get-tuple-element.24), channel_id=1, source_target_pairs={{0,102},{1,7},{2,96},{3,1},{4,98},{5,3},{6,100},{7,5},{8,110},{9,1... | collective-permute-start | bytes 6152 | tf_op jit(solution)/shard_map/ppermute | solution.py:260
  60.4 0.0 collective-permute-done.18
  60.4 0.0 collective-permute-done.19
  60.4 0.0 collective-permute-done.20
  60.5 1.0 %collective-permute-done.21 = f32[2,1,256]{2,1,0:T(1,128)S(1)} collective-permute-done((f32[2,1,256]{2,1,0:T(1,128)S(1)}, f32[2,1,256]{2,1,0:T(1,128)S(1)}, u32[]{:S(2)}, u32[]{:S(2)}) %collective-permute-start.21) | collective-permute-done | bytes 2080 | tf_op jit(solution)/shard_map/ppermute | solution.py:260
  61.4 0.0 collective-permute-done.22
  61.4 3.4 %collective-permute-start.23 = (f32[256]{0:T(256)S(1)}, f32[256]{0:T(256)S(1)}, u32[]{:S(2)}, u32[]{:S(2)}) collective-permute-start(f32[256]{0:T(256)S(1)} %bitcast.9), channel_id=1, source_target_pairs={{0,1},{1,0},{2,3},{3,2},{4,5},{5,4},{6,7},{7,6},{8,9},{9,8},{10,11... | collective-permute-start | bytes 3080 | tf_op jit(solution)/shard_map/ppermute | solution.py:263
  64.8 0.8 %collective-permute-done.23 = f32[256]{0:T(256)S(1)} collective-permute-done((f32[256]{0:T(256)S(1)}, f32[256]{0:T(256)S(1)}, u32[]{:S(2)}, u32[]{:S(2)}) %collective-permute-start.23) | collective-permute-done | bytes 1056 | tf_op jit(solution)/shard_map/ppermute | solution.py:263
  65.6 0.6 add_log-plus-one_fusion
  (11 shorter events, 0.1 us)
Async XLA Ops:
  1.2 13.4 %collective-permute-start.1 = (bf16[272,768]{1,0:T(8,128)(2,1)S(1)}, bf16[272,768]{1,0:T(8,128)(2,1)S(1)}, u32[]{:S(2)}, u32[]{:S(2)}) collective-permute-start(bf16[272,768]{1,0:T(8,128)(2,1)S(1)} %pack.1.refs_0_), channel_id=1, source_target_pairs={{26,0},{99,1},{28,2},{101,3},{30,4},{103,5},{24,6},{97,7},{2,8},{1... | collective-permute-start | bytes 1253384 | tf_op jit(solution)/shard_map/ppermute | solution.py:245
  5.9 12.1 %collective-permute-start.3 = (bf16[272,768]{1,0:T(8,128)(2,1)S(1)}, bf16[272,768]{1,0:T(8,128)(2,1)S(1)}, u32[]{:S(2)}, u32[]{:S(2)}) collective-permute-start(bf16[272,768]{1,0:T(8,128)(2,1)S(1)} %pack.1.refs_0_), channel_id=1, source_target_pairs={{40,0},{41,1},{42,2},{43,3},{44,4},{45,5},{46,6},{47,7},{48,8},{49... | collective-permute-start | bytes 1253384 | tf_op jit(solution)/shard_map/ppermute | solution.py:245
  9.4 10.1 %collective-permute-start.5 = (bf16[272,768]{1,0:T(8,128)(2,1)S(1)}, bf16[272,768]{1,0:T(8,128)(2,1)S(1)}, u32[]{:S(2)}, u32[]{:S(2)}) collective-permute-start(bf16[272,768]{1,0:T(8,128)(2,1)S(1)} %pack.1.refs_0_), channel_id=1, source_target_pairs={{6,0},{7,1},{0,2},{1,3},{2,4},{3,5},{4,6},{5,7},{14,8},{15,9},{8,1... | collective-permute-start | bytes 1253384 | tf_op jit(solution)/shard_map/ppermute | solution.py:245
  9.6 12.7 %collective-permute-start.6 = (bf16[272,768]{1,0:T(8,128)(2,1)S(1)}, bf16[272,768]{1,0:T(8,128)(2,1)S(1)}, u32[]{:S(2)}, u32[]{:S(2)}) collective-permute-start(bf16[272,768]{1,0:T(8,128)(2,1)S(1)} %pack.1.refs_0_), channel_id=1, source_target_pairs={{0,1},{1,0},{2,3},{3,2},{4,5},{5,4},{6,7},{7,6},{8,9},{9,8},{10,11... | collective-permute-start | bytes 1253384 | tf_op jit(solution)/shard_map/ppermute | solution.py:246
  11.6 14.2 %collective-permute-start = (bf16[272,768]{1,0:T(8,128)(2,1)S(1)}, bf16[272,768]{1,0:T(8,128)(2,1)S(1)}, u32[]{:S(2)}, u32[]{:S(2)}) collective-permute-start(bf16[272,768]{1,0:T(8,128)(2,1)S(1)} %pack.1.refs_0_), channel_id=1, source_target_pairs={{98,0},{27,1},{100,2},{29,3},{102,4},{31,5},{96,6},{25,7},{106,8},... | collective-permute-start | bytes 1253384 | tf_op jit(solution)/shard_map/ppermute | solution.py:245
  14.6 11.7 %collective-permute-start.7 = (bf16[272,768]{1,0:T(8,128)(2,1)S(1)}, bf16[272,768]{1,0:T(8,128)(2,1)S(1)}, u32[]{:S(2)}, u32[]{:S(2)}) collective-permute-start(bf16[272,768]{1,0:T(8,128)(2,1)S(1)} %collective-permute-done.1.refs_1_), channel_id=1, source_target_pairs={{0,1},{1,0},{2,3},{3,2},{4,5},{5,4},{6,7},{7,6},{8,9},{9,8},{10,11... | collective-permute-start | bytes 1253384 | tf_op jit(solution)/shard_map/ppermute | solution.py:246
  18.0 9.5 %collective-permute-start.8 = (bf16[272,768]{1,0:T(8,128)(2,1)S(1)}, bf16[272,768]{1,0:T(8,128)(2,1)}, u32[]{:S(2)}, u32[]{:S(2)}) collective-permute-start(bf16[272,768]{1,0:T(8,128)(2,1)S(1)} %collective-permute-done.3.refs_2_), channel_id=1, source_target_pairs={{0,1},{1,0},{2,3},{3,2},{4,5},{5,4},{6,7},{7,6},{8,9},{9,8},{10,11... | collective-permute-start | bytes 1253384 | tf_op jit(solution)/shard_map/ppermute | solution.py:246
  19.5 12.6 %collective-permute-start.2 = (bf16[272,768]{1,0:T(8,128)(2,1)S(1)}, bf16[272,768]{1,0:T(8,128)(2,1)S(1)}, u32[]{:S(2)}, u32[]{:S(2)}) collective-permute-start(bf16[272,768]{1,0:T(8,128)(2,1)S(1)} %collective-permute-done.1.refs_1_), channel_id=1, source_target_pairs={{32,0},{9,1},{34,2},{11,3},{36,4},{13,5},{38,6},{15,7},{40,8},{17,... | collective-permute-start | bytes 1253384 | tf_op jit(solution)/shard_map/ppermute | solution.py:245
  22.2 9.9 %collective-permute-start.10 = (bf16[272,768]{1,0:T(8,128)(2,1)S(1)}, bf16[272,768]{1,0:T(8,128)(2,1)}, u32[]{:S(2)}, u32[]{:S(2)}) collective-permute-start(bf16[272,768]{1,0:T(8,128)(2,1)S(1)} %collective-permute-done.1.refs_1_), channel_id=1, source_target_pairs={{96,0},{25,1},{98,2},{27,3},{100,4},{29,5},{102,6},{31,7},{104,8},... | collective-permute-start | bytes 1253384 | tf_op jit(solution)/shard_map/ppermute | solution.py:245
  25.8 9.0 %collective-permute-start.11 = (bf16[272,768]{1,0:T(8,128)(2,1)S(1)}, bf16[272,768]{1,0:T(8,128)(2,1)}, u32[]{:S(2)}, u32[]{:S(2)}) collective-permute-start(bf16[272,768]{1,0:T(8,128)(2,1)S(1)} %collective-permute-done.5.refs_3_), channel_id=1, source_target_pairs={{0,1},{1,0},{2,3},{3,2},{4,5},{5,4},{6,7},{7,6},{8,9},{9,8},{10,11... | collective-permute-start | bytes 1253384 | tf_op jit(solution)/shard_map/ppermute | solution.py:246
  26.3 14.5 %collective-permute-start.4 = (bf16[272,768]{1,0:T(8,128)(2,1)S(1)}, bf16[272,768]{1,0:T(8,128)(2,1)S(1)}, u32[]{:S(2)}, u32[]{:S(2)}) collective-permute-start(bf16[272,768]{1,0:T(8,128)(2,1)S(1)} %collective-permute-done.3.refs_2_), channel_id=1, source_target_pairs={{6,0},{7,1},{0,2},{1,3},{2,4},{3,5},{4,6},{5,7},{14,8},{15,9},{8,1... | collective-permute-start | bytes 1253384 | tf_op jit(solution)/shard_map/ppermute | solution.py:245
  27.5 13.4 %collective-permute-start.15 = (bf16[272,768]{1,0:T(8,128)(2,1)S(1)}, bf16[272,768]{1,0:T(8,128)(2,1)S(1)}, u32[]{:S(2)}, u32[]{:S(2)}) collective-permute-start(bf16[272,768]{1,0:T(8,128)(2,1)S(1)} %collective-permute-done.5.refs_3_), channel_id=1, source_target_pairs={{96,0},{25,1},{98,2},{27,3},{100,4},{29,5},{102,6},{31,7},{104,8},... | collective-permute-start | bytes 1253384 | tf_op jit(solution)/shard_map/ppermute | solution.py:245
  32.0 11.0 %collective-permute-start.16 = (bf16[272,768]{1,0:T(8,128)(2,1)S(1)}, bf16[272,768]{1,0:T(8,128)(2,1)S(1)}, u32[]{:S(2)}, u32[]{:S(2)}) collective-permute-start(bf16[272,768]{1,0:T(8,128)(2,1)S(1)} %collective-permute-done.5.refs_3_), channel_id=1, source_target_pairs={{24,0},{97,1},{26,2},{99,3},{28,4},{101,5},{30,6},{103,7},{0,8},{1... | collective-permute-start | bytes 1253384 | tf_op jit(solution)/shard_map/ppermute | solution.py:250
  32.1 10.9 %collective-permute-start.9 = (bf16[272,768]{1,0:T(8,128)(2,1)S(1)}, bf16[272,768]{1,0:T(8,128)(2,1)S(1)}, u32[]{:S(2)}, u32[]{:S(2)}) collective-permute-start(bf16[272,768]{1,0:T(8,128)(2,1)S(1)} %collective-permute-done.refs_4_.refs_3_.refs_0_), channel_id=1, source_target_pairs={{8,0},{33,1},{10,2},{35,3},{12,4},{37,5},{14,6},{39,7},{16,8},{41,... | collective-permute-start | bytes 1253384 | tf_op jit(solution)/shard_map/ppermute | solution.py:250
  39.4 8.3 %collective-permute-start.12 = (bf16[272,768]{1,0:T(8,128)(2,1)S(1)}, bf16[272,768]{1,0:T(8,128)(2,1)S(1)}, u32[]{:S(2)}, u32[]{:S(2)}) collective-permute-start(bf16[272,768]{1,0:T(8,128)(2,1)S(1)} %collective-permute-done.refs_4_.refs_3_.refs_0_), channel_id=1, source_target_pairs={{0,1},{1,0},{2,3},{3,2},{4,5},{5,4},{6,7},{7,6},{8,9},{9,8},{10,11... | collective-permute-start | bytes 1253384 | tf_op jit(solution)/shard_map/ppermute | solution.py:253
  40.8 6.9 %collective-permute-start.13 = (bf16[272,768]{1,0:T(8,128)(2,1)}, bf16[272,768]{1,0:T(8,128)(2,1)S(1)}, u32[]{:S(2)}, u32[]{:S(2)}) collective-permute-start(bf16[272,768]{1,0:T(8,128)(2,1)} %collective-permute-done.10.refs_5_.refs_4_), channel_id=1, source_target_pairs={{0,1},{1,0},{2,3},{3,2},{4,5},{5,4},{6,7},{7,6},{8,9},{9,8},{10,11... | collective-permute-start | bytes 1253384 | tf_op jit(solution)/shard_map/ppermute | solution.py:253
  40.9 6.8 %collective-permute-start.14 = (bf16[272,768]{1,0:T(8,128)(2,1)S(1)}, bf16[272,768]{1,0:T(8,128)(2,1)S(1)}, u32[]{:S(2)}, u32[]{:S(2)}) collective-permute-start(bf16[272,768]{1,0:T(8,128)(2,1)S(1)} %collective-permute-done.2.refs_6_.refs_5_.refs_1_), channel_id=1, source_target_pairs={{0,1},{1,0},{2,3},{3,2},{4,5},{5,4},{6,7},{7,6},{8,9},{9,8},{10,11... | collective-permute-start | bytes 1253384 | tf_op jit(solution)/shard_map/ppermute | solution.py:253
  49.4 1.3 %collective-permute-start.17 = (f32[10,1,256]{2,1,0:T(1,128)S(1)}, f32[10,1,256]{2,1,0:T(1,128)S(1)}, u32[]{:S(2)}, u32[]{:S(2)}) collective-permute-start(f32[10,1,256]{2,1,0:T(1,128)S(1)} %get-tuple-element.22), channel_id=1, source_target_pairs={{0,1},{1,0},{2,3},{3,2},{4,5},{5,4},{6,7},{7,6},{8,9},{9,8},{10,11... | collective-permute-start | bytes 30728 | tf_op jit(solution)/shard_map/ppermute | solution.py:257
  50.7 9.8 %collective-permute-start.18 = (f32[2,1,256]{2,1,0:T(1,128)S(1)}, f32[2,1,256]{2,1,0:T(1,128)S(1)}, u32[]{:S(2)}, u32[]{:S(2)}) collective-permute-start(f32[2,1,256]{2,1,0:T(1,128)S(1)} %get-tuple-element.23), channel_id=1, source_target_pairs={{0,46},{1,59},{2,40},{3,61},{4,42},{5,63},{6,44},{7,57},{8,54},{9,... | collective-permute-start | bytes 6152 | tf_op jit(solution)/shard_map/ppermute | solution.py:260
  54.8 5.7 %collective-permute-start.19 = (f32[2,1,256]{2,1,0:T(1,128)S(1)}, f32[2,1,256]{2,1,0:T(1,128)S(1)}, u32[]{:S(2)}, u32[]{:S(2)}) collective-permute-start(f32[2,1,256]{2,1,0:T(1,128)S(1)} %get-tuple-element.27), channel_id=1, source_target_pairs={{0,106},{1,123},{2,108},{3,125},{4,110},{5,127},{6,104},{7,121},{8... | collective-permute-start | bytes 6152 | tf_op jit(solution)/shard_map/ppermute | solution.py:260
  55.9 4.6 %collective-permute-start.20 = (f32[2,1,256]{2,1,0:T(1,128)S(1)}, f32[2,1,256]{2,1,0:T(1,128)S(1)}, u32[]{:S(2)}, u32[]{:S(2)}) collective-permute-start(f32[2,1,256]{2,1,0:T(1,128)S(1)} %get-tuple-element.26), channel_id=1, source_target_pairs={{0,26},{1,31},{2,28},{3,25},{4,30},{5,27},{6,24},{7,29},{8,2},{9,7... | collective-permute-start | bytes 6152 | tf_op jit(solution)/shard_map/ppermute | solution.py:260
  56.9 4.5 %collective-permute-start.21 = (f32[2,1,256]{2,1,0:T(1,128)S(1)}, f32[2,1,256]{2,1,0:T(1,128)S(1)}, u32[]{:S(2)}, u32[]{:S(2)}) collective-permute-start(f32[2,1,256]{2,1,0:T(1,128)S(1)} %get-tuple-element.25), channel_id=1, source_target_pairs={{0,40},{1,99},{2,42},{3,101},{4,44},{5,103},{6,46},{7,97},{8,48},{... | collective-permute-start | bytes 6152 | tf_op jit(solution)/shard_map/ppermute | solution.py:260
  57.9 3.5 %collective-permute-start.22 = (f32[2,1,256]{2,1,0:T(1,128)S(1)}, f32[2,1,256]{2,1,0:T(1,128)S(1)}, u32[]{:S(2)}, u32[]{:S(2)}) collective-permute-start(f32[2,1,256]{2,1,0:T(1,128)S(1)} %get-tuple-element.24), channel_id=1, source_target_pairs={{0,102},{1,7},{2,96},{3,1},{4,98},{5,3},{6,100},{7,5},{8,110},{9,1... | collective-permute-start | bytes 6152 | tf_op jit(solution)/shard_map/ppermute | solution.py:260
  61.4 4.2 %collective-permute-start.23 = (f32[256]{0:T(256)S(1)}, f32[256]{0:T(256)S(1)}, u32[]{:S(2)}, u32[]{:S(2)}) collective-permute-start(f32[256]{0:T(256)S(1)} %bitcast.9), channel_id=1, source_target_pairs={{0,1},{1,0},{2,3},{3,2},{4,5},{5,4},{6,7},{7,6},{8,9},{9,8},{10,11... | collective-permute-start | bytes 3080 | tf_op jit(solution)/shard_map/ppermute | solution.py:263

commit v5 on v4

--- a/solution.py
+++ b/solution.py
@@ -16,9 +16,9 @@
 CLUSTER_SHIFT = 5
 
 PLAN = ((0, 13), (0, 20), (0, 3), (0, 49), (1, 48), (1, 16), (2, 3), (3, 48), (4, 4), (3, 12))
-SWAPPED = 7
 BLOCKS = len(PLAN) + 1
-PHASES = ((4, 4), (7, 4), (BLOCKS, 4), (BLOCKS, SWAPPED))
+EARLY, LATE = (0, 1, 2, 3), (4, 5, 6)
+PHASES = ((4, EARLY), (7, EARLY), (BLOCKS, EARLY), (BLOCKS, EARLY + LATE))
 
 
 def shift(place, by):
@@ -90,7 +90,7 @@
                     seen.update({(0, d), (0, minus(d))})
                     axis = next((i for i in range(3) if d >> (2 * i) & 3 == 2), None)
                     found.append(("full" if d != minus(d) else "half", a, True, b, axis))
-        for b in range(other):
+        for b in other:
             for a in range(mine):
                 d = shift(HELD[a], minus(mirror(HELD[b])))
                 if (1, d) not in seen:
@@ -125,7 +125,8 @@
     return [slice(start + s, start + s + LANES) for s in range(0, ROWS - start, LANES)]
 
 
-def pairs_body(work, mine_used, other_used, earlier, last, place_ref, *refs):
+def pairs_body(work, mine_used, other_used, earlier, last, *refs):
+    core, bits = core_index(), high_bits()
     count = len(mine_used) + len(other_used)
     mine = dict(zip(mine_used, refs))
     other = dict(zip(other_used, refs[len(mine_used) : count]))
@@ -167,7 +168,7 @@
             (value,) = weights(a, low, b_ref, high, [labels[:, high]])
             row_sums[at[a], low, :] += value
             column_sums[slot, :, high] += down(value)
-            which = place_ref[0] if axis is None else place_ref[1 + axis]
+            which = core if axis is None else bits[axis]
             same = pl.ds(pl.multiple_of(which * LANES, LANES), LANES)
             chosen = jnp.where(which == 0, labels[:, low], labels[:, high])
             (value,) = weights(a, same, b_ref, same, [chosen])
@@ -186,8 +187,8 @@
 
     for slot in range(2 * BLOCKS):
         if last:
-            rows = [table_row(core, slot) for core in (0, 1)]
-            row = jnp.where(place_ref[0] == 0, rows[0], rows[1])
+            rows = [table_row(c, slot) for c in (0, 1)]
+            row = jnp.where(core == 0, rows[0], rows[1])
         for part in parts():
             total = jnp.sum(column_sums[slot, :, part], axis=0, keepdims=True)
             if slot in at:
@@ -204,22 +205,22 @@
         outs[2][...] = table[HOME : HOME + 2]
 
 
-def pair_sums(phase, place, mine, other, before):
+def pair_sums(phase, mine, other, before):
     work = UNITS[phase]
     mine_used = sorted({a for _, a, *_ in work} | {b for _, _, is_mine, b, _ in work if is_mine})
     other_used = sorted({b for _, _, is_mine, b, _ in work if not is_mine})
     blocks = [mine[k] for k in mine_used] + [other[k] for k in other_used]
     blocks = [pltpu.with_memory_space_constraint(block, pltpu.VMEM) for block in blocks]
-    before = [] if before is None else [before]
+    before = [] if before is None else [pltpu.with_memory_space_constraint(before, pltpu.VMEM)]
     last = phase == len(PHASES) - 1
     outs = (2 * SHARE, 2 * SHARE, 2) if last else (2 * BLOCKS,)
-    smem, vmem = pl.BlockSpec(memory_space=pltpu.SMEM), pl.BlockSpec(memory_space=pltpu.VMEM)
+    vmem = pl.BlockSpec(memory_space=pltpu.VMEM)
     firsts = len({a for _, a, *_ in work})
     area = sum(ROWS * ROWS // (2 if kind == "half" else 1) for kind, *_ in work)
     return pl.pallas_call(
         functools.partial(pairs_body, work, mine_used, other_used, len(before), last),
-        out_shape=[jax.ShapeDtypeStruct((n, 1, ROWS), jnp.float32) for n in outs],
-        in_specs=[smem] + [vmem] * (len(blocks) + len(before)),
+        out_shape=[pltpu.VMEM((n, 1, ROWS), jnp.float32) for n in outs],
+        in_specs=[vmem] * (len(blocks) + len(before)),
         out_specs=[vmem] * len(outs),
         scratch_shapes=[
             pltpu.VMEM((firsts, ROWS, LANES), jnp.float32),
@@ -230,29 +231,34 @@
         compiler_params=pltpu.CompilerParams(vmem_limit_bytes=24 * 1024 * 1024),
         cost_estimate=pl.CostEstimate(flops=2 * area * WIDTH, bytes_accessed=0, transcendentals=area),
         name=f"pair_sums_{phase}",
-    )(place, *blocks, *before)
+    )(*blocks, *before)
+
+
+def core_index():
+    return lax.axis_index("member") & 1
+
+
+def high_bits():
+    member, core = lax.axis_index("member"), core_index()
+    x, y, z = member >> 2 & 1, member >> 4 & 1, lax.axis_index("cluster") >> 1
+    return x, jnp.where(core == 0, y, z), jnp.where(core == 0, z, y)
 
 
 def shards(embeddings, destination):
-    member = lax.axis_index("member")
-    core = member & 1
-    chip = (member >> 1) + 16 * lax.axis_index("cluster")
-    x, y, z = (chip >> s & 1 for s in (1, 3, 5))
-    place = jnp.stack([core, x, jnp.where(core == 0, y, z), jnp.where(core == 0, z, y)]).astype(jnp.int32)
-
+    core = core_index()
     mine = [pack(embeddings, destination)]
     for source, jump in PLAN[:8]:
         mine.append(lax.ppermute(mine[source], BOTH, fetch((jump, mirror(jump)))))
-    other = [lax.ppermute(block, BOTH, CORE_SWAP) for block in mine[0:4]]
-    (sums,) = pair_sums(0, place, mine, other, None)
+    other = {k: lax.ppermute(mine[k], BOTH, CORE_SWAP) for k in EARLY}
+    (sums,) = pair_sums(0, mine, other, None)
     held, sums = lax.optimization_barrier((mine[4], sums))
     for source, jump in PLAN[8:]:
         mine.append(lax.ppermute(held if source == 4 else mine[source], BOTH, fetch((jump, mirror(jump)))))
-    (sums,) = pair_sums(1, place, mine, other, sums)
-    later, sums = lax.optimization_barrier((mine[4:SWAPPED], sums))
-    other += [lax.ppermute(block, BOTH, CORE_SWAP) for block in later]
-    (sums,) = pair_sums(2, place, mine, other, sums)
-    kept, given, home = pair_sums(3, place, mine, other, sums)
+    (sums,) = pair_sums(1, mine, other, sums)
+    later, sums = lax.optimization_barrier(([mine[k] for k in LATE], sums))
+    other.update({k: lax.ppermute(block, BOTH, CORE_SWAP) for k, block in zip(LATE, later)})
+    (sums,) = pair_sums(2, mine, other, sums)
+    kept, given, home = pair_sums(3, mine, other, sums)
 
     kept += lax.ppermute(given, BOTH, CORE_SWAP)
     for n in range(SHARE):

time: 66.4 us -> 64.1 us (0.965)
  Pallas kernels: 15.2 us -> 11.2 us
  starting transfers between devices: 40.9 us -> 42.6 us
    pallas_call x4, Pallas kernels: 14 us -> 10 us  [pair_sums(): pl.pallas_call(functools.partial(pairs_body, work, mine_used, other_used,...]
    ppermute x7, starting transfers between devices: 8.39 us -> 11.7 us  [the longest x4 5.89 us: shards(): other = {k: lax.ppermute(mine[k], BOTH, CORE_SWAP) for k in EARLY}]
    ppermute x5, waiting for transfers between devices: 0.98 us -> 2.03 us  [shards(): home += lax.ppermute(kept[2 * n:2 * n + 2], BOTH, give(jumps))]
    ppermute x5, starting transfers between devices: 9.77 us -> 8.72 us  [shards(): home += lax.ppermute(kept[2 * n:2 * n + 2], BOTH, give(jumps))]
    ppermute x2, waiting for transfers between devices: 1.07 us -> 0.02 us  [shards(): lax.ppermute(held if source == 4 else mine[source], BOTH, fetch((jump, mi...]
  transfers between devices with their start and end apart: 24 -> 24, of which waited for: 8 -> 8; matrix products, arithmetic and copies ran while one was open for 0% -> 0% of each run, Pallas kernels for 19% -> 14%
where the time goes in v5:
time: 64.1 us; the launch traced here: 64 us
  starting transfers between devices  42.6 us (66%)
  Pallas kernels  11.2 us (17%)
  waiting for transfers between devices  9.56 us (15%)
    ppermute x8, starting transfers between devices, shards(): mine.append(lax.ppermute(mine[source], BOTH, fetch((jump, mirror(jump)))))  16.5 us
    pallas_call x4, Pallas kernels, pair_sums(): pl.pallas_call(functools.partial(pairs_body, work, mine_used, other_used,...  10 us
    ppermute x5, starting transfers between devices, shards(): home += lax.ppermute(kept[2 * n:2 * n + 2], BOTH, give(jumps))  8.72 us
    ppermute x4, starting transfers between devices, shards(): other = {k: lax.ppermute(mine[k], BOTH, CORE_SWAP) for k in EARLY}  5.89 us
    ppermute x3, starting transfers between devices, shards(): lax.ppermute(block, BOTH, CORE_SWAP)  5.79 us
    ppermute x8, waiting for transfers between devices, shards(): mine.append(lax.ppermute(mine[source], BOTH, fetch((jump, mirror(jump)))))  5.5 us
    ppermute x1, starting transfers between devices, shards(): return jnp.log1p(own + lax.ppermute(rest, BOTH, CORE_SWAP))  2.84 us
    ppermute x2, starting transfers between devices, shards(): lax.ppermute(held if source == 4 else mine[source], BOTH, fetch((jump, mi...  2.73 us
  transfers between devices with their start and end apart: 24, of which 8 were waited for; matrix products, arithmetic and copies ran while one was open for 0% of the time, Pallas kernels for 14%

profile of v5, /device:TPU:1, one launch (start us, length us, event | category | flops | bytes accessed | tf_op | source)
XLA Modules:
  0.0 64.0 jit_solution(8112158380344807768)
XLA Ops:
  0.0 1.2 %pack.1.refs_0_ = bf16[272,768]{1,0:T(8,128)(2,1)S(1)} custom-call(bf16[256,768]{1,0:T(8,128)(2,1)} %rows_ref.1, s32[1,256]{1,0:T(1,128)} %bitcast.4), custom_call_target="tpu_custom_call" | custom-call | tf_op jit(solution)/shard_map/pack/pallas_call | solution.py:117
  1.2 4.7 %collective-permute-start.1 = (bf16[272,768]{1,0:T(8,128)(2,1)S(1)}, bf16[272,768]{1,0:T(8,128)(2,1)S(1)}, u32[]{:S(2)}, u32[]{:S(2)}) collective-permute-start(bf16[272,768]{1,0:T(8,128)(2,1)S(1)} %pack.1.refs_0_), channel_id=1, source_target_pairs={{26,0},{99,1},{28,2},{101,3},{30,4},{103,5},{24,6},{97,7},{2,8},{1... | collective-permute-start | bytes 1253384 | tf_op jit(solution)/shard_map/ppermute | solution.py:251
  5.9 3.5 %collective-permute-start.3 = (bf16[272,768]{1,0:T(8,128)(2,1)S(1)}, bf16[272,768]{1,0:T(8,128)(2,1)S(1)}, u32[]{:S(2)}, u32[]{:S(2)}) collective-permute-start(bf16[272,768]{1,0:T(8,128)(2,1)S(1)} %pack.1.refs_0_), channel_id=1, source_target_pairs={{40,0},{41,1},{42,2},{43,3},{44,4},{45,5},{46,6},{47,7},{48,8},{49... | collective-permute-start | bytes 1253384 | tf_op jit(solution)/shard_map/ppermute | solution.py:251
  9.4 0.2 collective-permute-start.5
  9.6 2.1 %collective-permute-start.6 = (bf16[272,768]{1,0:T(8,128)(2,1)S(1)}, bf16[272,768]{1,0:T(8,128)(2,1)S(1)}, u32[]{:S(2)}, u32[]{:S(2)}) collective-permute-start(bf16[272,768]{1,0:T(8,128)(2,1)S(1)} %pack.1.refs_0_), channel_id=1, source_target_pairs={{0,1},{1,0},{2,3},{3,2},{4,5},{5,4},{6,7},{7,6},{8,9},{9,8},{10,11... | collective-permute-start | bytes 1253384 | tf_op jit(solution)/shard_map/ppermute | solution.py:252
  11.6 2.8 %collective-permute-start = (bf16[272,768]{1,0:T(8,128)(2,1)S(1)}, bf16[272,768]{1,0:T(8,128)(2,1)S(1)}, u32[]{:S(2)}, u32[]{:S(2)}) collective-permute-start(bf16[272,768]{1,0:T(8,128)(2,1)S(1)} %pack.1.refs_0_), channel_id=1, source_target_pairs={{98,0},{27,1},{100,2},{29,3},{102,4},{31,5},{96,6},{25,7},{106,8},... | collective-permute-start | bytes 1253384 | tf_op jit(solution)/shard_map/ppermute | solution.py:251
  14.4 0.2 collective-permute-done.1.refs_1_
  14.6 2.1 %collective-permute-start.7 = (bf16[272,768]{1,0:T(8,128)(2,1)S(1)}, bf16[272,768]{1,0:T(8,128)(2,1)S(1)}, u32[]{:S(2)}, u32[]{:S(2)}) collective-permute-start(bf16[272,768]{1,0:T(8,128)(2,1)S(1)} %collective-permute-done.1.refs_1_), channel_id=1, source_target_pairs={{0,1},{1,0},{2,3},{3,2},{4,5},{5,4},{6,7},{7,6},{8,9},{9,8},{10,11... | collective-permute-start | bytes 1253384 | tf_op jit(solution)/shard_map/ppermute | solution.py:252
  16.7 1.3 %collective-permute-done.3.refs_2_ = bf16[272,768]{1,0:T(8,128)(2,1)S(1)} collective-permute-done((bf16[272,768]{1,0:T(8,128)(2,1)S(1)}, bf16[272,768]{1,0:T(8,128)(2,1)S(1)}, u32[]{:S(2)}, u32[]{:S(2)}) %collective-permute-start.3) | collective-permute-done | bytes 417824 | tf_op jit(solution)/shard_map/ppermute | solution.py:251
  18.0 1.3 %collective-permute-start.8 = (bf16[272,768]{1,0:T(8,128)(2,1)S(1)}, bf16[272,768]{1,0:T(8,128)(2,1)S(1)}, u32[]{:S(2)}, u32[]{:S(2)}) collective-permute-start(bf16[272,768]{1,0:T(8,128)(2,1)S(1)} %collective-permute-done.3.refs_2_), channel_id=1, source_target_pairs={{0,1},{1,0},{2,3},{3,2},{4,5},{5,4},{6,7},{7,6},{8,9},{9,8},{10,11... | collective-permute-start | bytes 1253384 | tf_op jit(solution)/shard_map/ppermute | solution.py:252
  19.2 0.2 collective-permute-done.5.refs_3_
  19.5 2.8 %collective-permute-start.2 = (bf16[272,768]{1,0:T(8,128)(2,1)S(1)}, bf16[272,768]{1,0:T(8,128)(2,1)S(1)}, u32[]{:S(2)}, u32[]{:S(2)}) collective-permute-start(bf16[272,768]{1,0:T(8,128)(2,1)S(1)} %collective-permute-done.1.refs_1_), channel_id=1, source_target_pairs={{32,0},{9,1},{34,2},{11,3},{36,4},{13,5},{38,6},{15,7},{40,8},{17,... | collective-permute-start | bytes 1253384 | tf_op jit(solution)/shard_map/ppermute | solution.py:251
  22.2 3.6 %collective-permute-done.refs_4_.refs_3_.refs_0_ = bf16[272,768]{1,0:T(8,128)(2,1)S(1)} collective-permute-done((bf16[272,768]{1,0:T(8,128)(2,1)S(1)}, bf16[272,768]{1,0:T(8,128)(2,1)S(1)}, u32[]{:S(2)}, u32[]{:S(2)}) %collective-permute-start) | collective-permute-done | bytes 417824 | tf_op jit(solution)/shard_map/ppermute | solution.py:251
  25.8 0.5 collective-permute-start.11
  26.3 0.0 collective-permute-done.7.refs_5_.refs_8_.refs_11_
  26.3 1.2 %collective-permute-start.4 = (bf16[272,768]{1,0:T(8,128)(2,1)S(1)}, bf16[272,768]{1,0:T(8,128)(2,1)S(1)}, u32[]{:S(2)}, u32[]{:S(2)}) collective-permute-start(bf16[272,768]{1,0:T(8,128)(2,1)S(1)} %collective-permute-done.3.refs_2_), channel_id=1, source_target_pairs={{6,0},{7,1},{0,2},{1,3},{2,4},{3,5},{4,6},{5,7},{14,8},{15,9},{8,1... | collective-permute-start | bytes 1253384 | tf_op jit(solution)/shard_map/ppermute | solution.py:251
  27.5 0.0 collective-permute-done.8.refs_6_.refs_9_.refs_12_
  27.5 1.4 %collective-permute-start.15 = (bf16[272,768]{1,0:T(8,128)(2,1)S(1)}, bf16[272,768]{1,0:T(8,128)(2,1)S(1)}, u32[]{:S(2)}, u32[]{:S(2)}) collective-permute-start(bf16[272,768]{1,0:T(8,128)(2,1)S(1)} %collective-permute-done.5.refs_3_), channel_id=1, source_target_pairs={{96,0},{25,1},{98,2},{27,3},{100,4},{29,5},{102,6},{31,7},{104,8},... | collective-permute-start | bytes 1253384 | tf_op jit(solution)/shard_map/ppermute | solution.py:251
  28.9 2.1 %pair_sums_0.1.refs_11_ = f32[22,1,256]{2,1,0:T(1,128)S(1)} custom-call(bf16[272,768]{1,0:T(8,128)(2,1)S(1)} %pack.1.refs_0_, bf16[272,768]{1,0:T(8,128)(2,1)S(1)} %collective-permute-done.1.refs_1_, bf16[272,768]{1,0:T(8,128)(2,1)S(1)} %collective-permute-done.3.refs_2_, bf16[272,768]{1,0:T(8,128)(2,1)S(1)} %collective-permute-done.5.refs_3_, ...), custom_call_target="tpu_custom_call" | custom-call | flops 1409286144 | tf_op jit(solution)/shard_map/pair_sums_0/pallas_call | solution.py:220
  31.0 0.0 collective-permute-done.2.refs_6_.refs_5_.refs_1_
  31.0 0.1 collective-permute-start.16
  31.1 0.0 collective-permute-done.10.refs_5_.refs_4_
  31.1 2.7 %collective-permute-start.9 = (bf16[272,768]{1,0:T(8,128)(2,1)S(1)}, bf16[272,768]{1,0:T(8,128)(2,1)S(1)}, u32[]{:S(2)}, u32[]{:S(2)}) collective-permute-start(bf16[272,768]{1,0:T(8,128)(2,1)S(1)} %collective-permute-done.refs_4_.refs_3_.refs_0_), channel_id=1, source_target_pairs={{8,0},{33,1},{10,2},{35,3},{12,4},{37,5},{14,6},{39,7},{16,8},{41,... | collective-permute-start | bytes 1253384 | tf_op jit(solution)/shard_map/ppermute | solution.py:256
  33.7 0.0 collective-permute-done.11.refs_10_.refs_13_
  33.7 3.2 %pair_sums_1.1.refs_14_ = f32[22,1,256]{2,1,0:T(1,128)S(1)} custom-call(bf16[272,768]{1,0:T(8,128)(2,1)S(1)} %pack.1.refs_0_, bf16[272,768]{1,0:T(8,128)(2,1)S(1)} %collective-permute-done.1.refs_1_, bf16[272,768]{1,0:T(8,128)(2,1)S(1)} %collective-permute-done.3.refs_2_, bf16[272,768]{1,0:T(8,128)(2,1)S(1)} %collective-permute-done.5.refs_3_, ...), custom_call_target="tpu_custom_call" | custom-call | flops 2415919104 | tf_op jit(solution)/shard_map/pair_sums_1/pallas_call | solution.py:220
  37.0 1.8 %collective-permute-start.12 = (bf16[272,768]{1,0:T(8,128)(2,1)S(1)}, bf16[272,768]{1,0:T(8,128)(2,1)S(1)}, u32[]{:S(2)}, u32[]{:S(2)}) collective-permute-start(bf16[272,768]{1,0:T(8,128)(2,1)S(1)} %collective-permute-done.refs_4_.refs_3_.refs_0_), channel_id=1, source_target_pairs={{0,1},{1,0},{2,3},{3,2},{4,5},{5,4},{6,7},{7,6},{8,9},{9,8},{10,11... | collective-permute-start | bytes 1253384 | tf_op jit(solution)/shard_map/ppermute | solution.py:259
  38.8 0.2 collective-permute-done.4.refs_6_.refs_2_
  39.0 1.0 %collective-permute-start.13 = (bf16[272,768]{1,0:T(8,128)(2,1)S(1)}, bf16[272,768]{1,0:T(8,128)(2,1)S(1)}, u32[]{:S(2)}, u32[]{:S(2)}) collective-permute-start(bf16[272,768]{1,0:T(8,128)(2,1)S(1)} %collective-permute-done.10.refs_5_.refs_4_), channel_id=1, source_target_pairs={{0,1},{1,0},{2,3},{3,2},{4,5},{5,4},{6,7},{7,6},{8,9},{9,8},{10,11... | collective-permute-start | bytes 1253384 | tf_op jit(solution)/shard_map/ppermute | solution.py:259
  40.0 0.0 collective-permute-done.15.refs_7_
  40.0 2.9 %collective-permute-start.14 = (bf16[272,768]{1,0:T(8,128)(2,1)S(1)}, bf16[272,768]{1,0:T(8,128)(2,1)S(1)}, u32[]{:S(2)}, u32[]{:S(2)}) collective-permute-start(bf16[272,768]{1,0:T(8,128)(2,1)S(1)} %collective-permute-done.2.refs_6_.refs_5_.refs_1_), channel_id=1, source_target_pairs={{0,1},{1,0},{2,3},{3,2},{4,5},{5,4},{6,7},{7,6},{8,9},{9,8},{10,11... | collective-permute-start | bytes 1253384 | tf_op jit(solution)/shard_map/ppermute | solution.py:259
  43.0 0.0 collective-permute-done.16.refs_9_
  43.0 0.0 collective-permute-done.9.refs_8_.refs_3_
  43.0 3.5 %pair_sums_2.1.refs_7_ = f32[22,1,256]{2,1,0:T(1,128)S(1)} custom-call(bf16[272,768]{1,0:T(8,128)(2,1)S(1)} %pack.1.refs_0_, bf16[272,768]{1,0:T(8,128)(2,1)S(1)} %collective-permute-done.1.refs_1_, bf16[272,768]{1,0:T(8,128)(2,1)S(1)} %collective-permute-done.3.refs_2_, bf16[272,768]{1,0:T(8,128)(2,1)S(1)} %collective-permute-done.refs_4_.refs_3_.refs_0_, ...), custom_call_target="tpu_custom_call" | custom-call | flops 2113929216 | tf_op jit(solution)/shard_map/pair_sums_2/pallas_call | solution.py:220
  46.5 0.0 collective-permute-done.12.refs_4_
  46.5 1.2 %pair_sums_3.1 = (f32[10,1,256]{2,1,0:T(1,128)S(1)}, f32[10,1,256]{2,1,0:T(1,128)S(1)}, f32[2,1,256]{2,1,0:T(1,128)S(1)}) custom-call(bf16[272,768]{1,0:T(8,128)(2,1)S(1)} %collective-permute-done.refs_4_.refs_3_.refs_0_, bf16[272,768]{1,0:T(8,128)(2,1)S(1)} %collective-permute-done.2.refs_6_.refs_5_.refs_1_, ...), custom_call_target="tpu_custom_call" | custom-call | flops 553648128 | tf_op jit(solution)/shard_map/pair_sums_3/pallas_call | solution.py:220
  47.7 0.1 collective-permute-start.17
  47.8 1.2 %collective-permute-done.17 = f32[10,1,256]{2,1,0:T(1,128)S(1)} collective-permute-done((f32[10,1,256]{2,1,0:T(1,128)S(1)}, f32[10,1,256]{2,1,0:T(1,128)S(1)}, u32[]{:S(2)}, u32[]{:S(2)}) %collective-permute-start.17) | collective-permute-done | bytes 10272 | tf_op jit(solution)/shard_map/ppermute | solution.py:263
  49.0 3.0 %collective-permute-start.18 = (f32[2,1,256]{2,1,0:T(1,128)S(1)}, f32[2,1,256]{2,1,0:T(1,128)S(1)}, u32[]{:S(2)}, u32[]{:S(2)}) collective-permute-start(f32[2,1,256]{2,1,0:T(1,128)S(1)} %get-tuple-element.23), channel_id=1, source_target_pairs={{0,46},{1,59},{2,40},{3,61},{4,42},{5,63},{6,44},{7,57},{8,54},{9,... | collective-permute-start | bytes 6152 | tf_op jit(solution)/shard_map/ppermute | solution.py:266
  52.0 1.9 %collective-permute-start.19 = (f32[2,1,256]{2,1,0:T(1,128)S(1)}, f32[2,1,256]{2,1,0:T(1,128)S(1)}, u32[]{:S(2)}, u32[]{:S(2)}) collective-permute-start(f32[2,1,256]{2,1,0:T(1,128)S(1)} %get-tuple-element.27), channel_id=1, source_target_pairs={{0,106},{1,123},{2,108},{3,125},{4,110},{5,127},{6,104},{7,121},{8... | collective-permute-start | bytes 6152 | tf_op jit(solution)/shard_map/ppermute | solution.py:266
  54.0 1.2 %collective-permute-start.20 = (f32[2,1,256]{2,1,0:T(1,128)S(1)}, f32[2,1,256]{2,1,0:T(1,128)S(1)}, u32[]{:S(2)}, u32[]{:S(2)}) collective-permute-start(f32[2,1,256]{2,1,0:T(1,128)S(1)} %get-tuple-element.26), channel_id=1, source_target_pairs={{0,26},{1,31},{2,28},{3,25},{4,30},{5,27},{6,24},{7,29},{8,2},{9,7... | collective-permute-start | bytes 6152 | tf_op jit(solution)/shard_map/ppermute | solution.py:266
  55.2 2.5 %collective-permute-start.22 = (f32[2,1,256]{2,1,0:T(1,128)S(1)}, f32[2,1,256]{2,1,0:T(1,128)S(1)}, u32[]{:S(2)}, u32[]{:S(2)}) collective-permute-start(f32[2,1,256]{2,1,0:T(1,128)S(1)} %get-tuple-element.24), channel_id=1, source_target_pairs={{0,102},{1,7},{2,96},{3,1},{4,98},{5,3},{6,100},{7,5},{8,110},{9,1... | collective-permute-start | bytes 6152 | tf_op jit(solution)/shard_map/ppermute | solution.py:266
  57.7 0.0 collective-permute-done.18
  57.7 0.0 collective-permute-done.19
  57.7 0.0 collective-permute-done.20
  57.7 2.0 %collective-permute-done.21 = f32[2,1,256]{2,1,0:T(1,128)S(1)} collective-permute-done((f32[2,1,256]{2,1,0:T(1,128)S(1)}, f32[2,1,256]{2,1,0:T(1,128)S(1)}, u32[]{:S(2)}, u32[]{:S(2)}) %collective-permute-start.21) | collective-permute-done | bytes 2080 | tf_op jit(solution)/shard_map/ppermute | solution.py:266
  59.8 2.8 %collective-permute-start.23 = (f32[256]{0:T(256)S(1)}, f32[256]{0:T(256)S(1)}, u32[]{:S(2)}, u32[]{:S(2)}) collective-permute-start(f32[256]{0:T(256)S(1)} %bitcast.5), channel_id=1, source_target_pairs={{0,1},{1,0},{2,3},{3,2},{4,5},{5,4},{6,7},{7,6},{8,9},{9,8},{10,11... | collective-permute-start | bytes 3080 | tf_op jit(solution)/shard_map/ppermute | solution.py:269
  62.6 0.8 %collective-permute-done.23 = f32[256]{0:T(256)S(1)} collective-permute-done((f32[256]{0:T(256)S(1)}, f32[256]{0:T(256)S(1)}, u32[]{:S(2)}, u32[]{:S(2)}) %collective-permute-start.23) | collective-permute-done | bytes 1056 | tf_op jit(solution)/shard_map/ppermute | solution.py:269
  63.5 0.6 add_log-plus-one_fusion
  (10 shorter events, 0.1 us)
Async XLA Ops:
  1.2 13.4 %collective-permute-start.1 = (bf16[272,768]{1,0:T(8,128)(2,1)S(1)}, bf16[272,768]{1,0:T(8,128)(2,1)S(1)}, u32[]{:S(2)}, u32[]{:S(2)}) collective-permute-start(bf16[272,768]{1,0:T(8,128)(2,1)S(1)} %pack.1.refs_0_), channel_id=1, source_target_pairs={{26,0},{99,1},{28,2},{101,3},{30,4},{103,5},{24,6},{97,7},{2,8},{1... | collective-permute-start | bytes 1253384 | tf_op jit(solution)/shard_map/ppermute | solution.py:251
  5.9 12.1 %collective-permute-start.3 = (bf16[272,768]{1,0:T(8,128)(2,1)S(1)}, bf16[272,768]{1,0:T(8,128)(2,1)S(1)}, u32[]{:S(2)}, u32[]{:S(2)}) collective-permute-start(bf16[272,768]{1,0:T(8,128)(2,1)S(1)} %pack.1.refs_0_), channel_id=1, source_target_pairs={{40,0},{41,1},{42,2},{43,3},{44,4},{45,5},{46,6},{47,7},{48,8},{49... | collective-permute-start | bytes 1253384 | tf_op jit(solution)/shard_map/ppermute | solution.py:251
  9.4 10.1 %collective-permute-start.5 = (bf16[272,768]{1,0:T(8,128)(2,1)S(1)}, bf16[272,768]{1,0:T(8,128)(2,1)S(1)}, u32[]{:S(2)}, u32[]{:S(2)}) collective-permute-start(bf16[272,768]{1,0:T(8,128)(2,1)S(1)} %pack.1.refs_0_), channel_id=1, source_target_pairs={{6,0},{7,1},{0,2},{1,3},{2,4},{3,5},{4,6},{5,7},{14,8},{15,9},{8,1... | collective-permute-start | bytes 1253384 | tf_op jit(solution)/shard_map/ppermute | solution.py:251
  9.6 12.7 %collective-permute-start.6 = (bf16[272,768]{1,0:T(8,128)(2,1)S(1)}, bf16[272,768]{1,0:T(8,128)(2,1)S(1)}, u32[]{:S(2)}, u32[]{:S(2)}) collective-permute-start(bf16[272,768]{1,0:T(8,128)(2,1)S(1)} %pack.1.refs_0_), channel_id=1, source_target_pairs={{0,1},{1,0},{2,3},{3,2},{4,5},{5,4},{6,7},{7,6},{8,9},{9,8},{10,11... | collective-permute-start | bytes 1253384 | tf_op jit(solution)/shard_map/ppermute | solution.py:252
  11.6 14.2 %collective-permute-start = (bf16[272,768]{1,0:T(8,128)(2,1)S(1)}, bf16[272,768]{1,0:T(8,128)(2,1)S(1)}, u32[]{:S(2)}, u32[]{:S(2)}) collective-permute-start(bf16[272,768]{1,0:T(8,128)(2,1)S(1)} %pack.1.refs_0_), channel_id=1, source_target_pairs={{98,0},{27,1},{100,2},{29,3},{102,4},{31,5},{96,6},{25,7},{106,8},... | collective-permute-start | bytes 1253384 | tf_op jit(solution)/shard_map/ppermute | solution.py:251
  14.6 11.7 %collective-permute-start.7 = (bf16[272,768]{1,0:T(8,128)(2,1)S(1)}, bf16[272,768]{1,0:T(8,128)(2,1)S(1)}, u32[]{:S(2)}, u32[]{:S(2)}) collective-permute-start(bf16[272,768]{1,0:T(8,128)(2,1)S(1)} %collective-permute-done.1.refs_1_), channel_id=1, source_target_pairs={{0,1},{1,0},{2,3},{3,2},{4,5},{5,4},{6,7},{7,6},{8,9},{9,8},{10,11... | collective-permute-start | bytes 1253384 | tf_op jit(solution)/shard_map/ppermute | solution.py:252
  18.0 9.5 %collective-permute-start.8 = (bf16[272,768]{1,0:T(8,128)(2,1)S(1)}, bf16[272,768]{1,0:T(8,128)(2,1)S(1)}, u32[]{:S(2)}, u32[]{:S(2)}) collective-permute-start(bf16[272,768]{1,0:T(8,128)(2,1)S(1)} %collective-permute-done.3.refs_2_), channel_id=1, source_target_pairs={{0,1},{1,0},{2,3},{3,2},{4,5},{5,4},{6,7},{7,6},{8,9},{9,8},{10,11... | collective-permute-start | bytes 1253384 | tf_op jit(solution)/shard_map/ppermute | solution.py:252
  19.5 11.5 %collective-permute-start.2 = (bf16[272,768]{1,0:T(8,128)(2,1)S(1)}, bf16[272,768]{1,0:T(8,128)(2,1)S(1)}, u32[]{:S(2)}, u32[]{:S(2)}) collective-permute-start(bf16[272,768]{1,0:T(8,128)(2,1)S(1)} %collective-permute-done.1.refs_1_), channel_id=1, source_target_pairs={{32,0},{9,1},{34,2},{11,3},{36,4},{13,5},{38,6},{15,7},{40,8},{17,... | collective-permute-start | bytes 1253384 | tf_op jit(solution)/shard_map/ppermute | solution.py:251
  22.2 8.8 %collective-permute-start.10 = (bf16[272,768]{1,0:T(8,128)(2,1)S(1)}, bf16[272,768]{1,0:T(8,128)(2,1)S(1)}, u32[]{:S(2)}, u32[]{:S(2)}) collective-permute-start(bf16[272,768]{1,0:T(8,128)(2,1)S(1)} %collective-permute-done.1.refs_1_), channel_id=1, source_target_pairs={{96,0},{25,1},{98,2},{27,3},{100,4},{29,5},{102,6},{31,7},{104,8},... | collective-permute-start | bytes 1253384 | tf_op jit(solution)/shard_map/ppermute | solution.py:251
  25.8 7.9 %collective-permute-start.11 = (bf16[272,768]{1,0:T(8,128)(2,1)S(1)}, bf16[272,768]{1,0:T(8,128)(2,1)S(1)}, u32[]{:S(2)}, u32[]{:S(2)}) collective-permute-start(bf16[272,768]{1,0:T(8,128)(2,1)S(1)} %collective-permute-done.5.refs_3_), channel_id=1, source_target_pairs={{0,1},{1,0},{2,3},{3,2},{4,5},{5,4},{6,7},{7,6},{8,9},{9,8},{10,11... | collective-permute-start | bytes 1253384 | tf_op jit(solution)/shard_map/ppermute | solution.py:252
  26.3 12.7 %collective-permute-start.4 = (bf16[272,768]{1,0:T(8,128)(2,1)S(1)}, bf16[272,768]{1,0:T(8,128)(2,1)S(1)}, u32[]{:S(2)}, u32[]{:S(2)}) collective-permute-start(bf16[272,768]{1,0:T(8,128)(2,1)S(1)} %collective-permute-done.3.refs_2_), channel_id=1, source_target_pairs={{6,0},{7,1},{0,2},{1,3},{2,4},{3,5},{4,6},{5,7},{14,8},{15,9},{8,1... | collective-permute-start | bytes 1253384 | tf_op jit(solution)/shard_map/ppermute | solution.py:251
  27.5 12.5 %collective-permute-start.15 = (bf16[272,768]{1,0:T(8,128)(2,1)S(1)}, bf16[272,768]{1,0:T(8,128)(2,1)S(1)}, u32[]{:S(2)}, u32[]{:S(2)}) collective-permute-start(bf16[272,768]{1,0:T(8,128)(2,1)S(1)} %collective-permute-done.5.refs_3_), channel_id=1, source_target_pairs={{96,0},{25,1},{98,2},{27,3},{100,4},{29,5},{102,6},{31,7},{104,8},... | collective-permute-start | bytes 1253384 | tf_op jit(solution)/shard_map/ppermute | solution.py:251
  31.0 12.0 %collective-permute-start.16 = (bf16[272,768]{1,0:T(8,128)(2,1)S(1)}, bf16[272,768]{1,0:T(8,128)(2,1)S(1)}, u32[]{:S(2)}, u32[]{:S(2)}) collective-permute-start(bf16[272,768]{1,0:T(8,128)(2,1)S(1)} %collective-permute-done.5.refs_3_), channel_id=1, source_target_pairs={{24,0},{97,1},{26,2},{99,3},{28,4},{101,5},{30,6},{103,7},{0,8},{1... | collective-permute-start | bytes 1253384 | tf_op jit(solution)/shard_map/ppermute | solution.py:256
  31.1 11.9 %collective-permute-start.9 = (bf16[272,768]{1,0:T(8,128)(2,1)S(1)}, bf16[272,768]{1,0:T(8,128)(2,1)S(1)}, u32[]{:S(2)}, u32[]{:S(2)}) collective-permute-start(bf16[272,768]{1,0:T(8,128)(2,1)S(1)} %collective-permute-done.refs_4_.refs_3_.refs_0_), channel_id=1, source_target_pairs={{8,0},{33,1},{10,2},{35,3},{12,4},{37,5},{14,6},{39,7},{16,8},{41,... | collective-permute-start | bytes 1253384 | tf_op jit(solution)/shard_map/ppermute | solution.py:256
  37.0 9.5 %collective-permute-start.12 = (bf16[272,768]{1,0:T(8,128)(2,1)S(1)}, bf16[272,768]{1,0:T(8,128)(2,1)S(1)}, u32[]{:S(2)}, u32[]{:S(2)}) collective-permute-start(bf16[272,768]{1,0:T(8,128)(2,1)S(1)} %collective-permute-done.refs_4_.refs_3_.refs_0_), channel_id=1, source_target_pairs={{0,1},{1,0},{2,3},{3,2},{4,5},{5,4},{6,7},{7,6},{8,9},{9,8},{10,11... | collective-permute-start | bytes 1253384 | tf_op jit(solution)/shard_map/ppermute | solution.py:259
  39.0 7.5 %collective-permute-start.13 = (bf16[272,768]{1,0:T(8,128)(2,1)S(1)}, bf16[272,768]{1,0:T(8,128)(2,1)S(1)}, u32[]{:S(2)}, u32[]{:S(2)}) collective-permute-start(bf16[272,768]{1,0:T(8,128)(2,1)S(1)} %collective-permute-done.10.refs_5_.refs_4_), channel_id=1, source_target_pairs={{0,1},{1,0},{2,3},{3,2},{4,5},{5,4},{6,7},{7,6},{8,9},{9,8},{10,11... | collective-permute-start | bytes 1253384 | tf_op jit(solution)/shard_map/ppermute | solution.py:259
  40.0 6.5 %collective-permute-start.14 = (bf16[272,768]{1,0:T(8,128)(2,1)S(1)}, bf16[272,768]{1,0:T(8,128)(2,1)S(1)}, u32[]{:S(2)}, u32[]{:S(2)}) collective-permute-start(bf16[272,768]{1,0:T(8,128)(2,1)S(1)} %collective-permute-done.2.refs_6_.refs_5_.refs_1_), channel_id=1, source_target_pairs={{0,1},{1,0},{2,3},{3,2},{4,5},{5,4},{6,7},{7,6},{8,9},{9,8},{10,11... | collective-permute-start | bytes 1253384 | tf_op jit(solution)/shard_map/ppermute | solution.py:259
  47.7 1.3 %collective-permute-start.17 = (f32[10,1,256]{2,1,0:T(1,128)S(1)}, f32[10,1,256]{2,1,0:T(1,128)S(1)}, u32[]{:S(2)}, u32[]{:S(2)}) collective-permute-start(f32[10,1,256]{2,1,0:T(1,128)S(1)} %get-tuple-element.22), channel_id=1, source_target_pairs={{0,1},{1,0},{2,3},{3,2},{4,5},{5,4},{6,7},{7,6},{8,9},{9,8},{10,11... | collective-permute-start | bytes 30728 | tf_op jit(solution)/shard_map/ppermute | solution.py:263
  49.0 8.7 %collective-permute-start.18 = (f32[2,1,256]{2,1,0:T(1,128)S(1)}, f32[2,1,256]{2,1,0:T(1,128)S(1)}, u32[]{:S(2)}, u32[]{:S(2)}) collective-permute-start(f32[2,1,256]{2,1,0:T(1,128)S(1)} %get-tuple-element.23), channel_id=1, source_target_pairs={{0,46},{1,59},{2,40},{3,61},{4,42},{5,63},{6,44},{7,57},{8,54},{9,... | collective-permute-start | bytes 6152 | tf_op jit(solution)/shard_map/ppermute | solution.py:266
  52.0 5.7 %collective-permute-start.19 = (f32[2,1,256]{2,1,0:T(1,128)S(1)}, f32[2,1,256]{2,1,0:T(1,128)S(1)}, u32[]{:S(2)}, u32[]{:S(2)}) collective-permute-start(f32[2,1,256]{2,1,0:T(1,128)S(1)} %get-tuple-element.27), channel_id=1, source_target_pairs={{0,106},{1,123},{2,108},{3,125},{4,110},{5,127},{6,104},{7,121},{8... | collective-permute-start | bytes 6152 | tf_op jit(solution)/shard_map/ppermute | solution.py:266
  54.0 3.8 %collective-permute-start.20 = (f32[2,1,256]{2,1,0:T(1,128)S(1)}, f32[2,1,256]{2,1,0:T(1,128)S(1)}, u32[]{:S(2)}, u32[]{:S(2)}) collective-permute-start(f32[2,1,256]{2,1,0:T(1,128)S(1)} %get-tuple-element.26), channel_id=1, source_target_pairs={{0,26},{1,31},{2,28},{3,25},{4,30},{5,27},{6,24},{7,29},{8,2},{9,7... | collective-permute-start | bytes 6152 | tf_op jit(solution)/shard_map/ppermute | solution.py:266
  55.2 4.5 %collective-permute-start.21 = (f32[2,1,256]{2,1,0:T(1,128)S(1)}, f32[2,1,256]{2,1,0:T(1,128)S(1)}, u32[]{:S(2)}, u32[]{:S(2)}) collective-permute-start(f32[2,1,256]{2,1,0:T(1,128)S(1)} %get-tuple-element.25), channel_id=1, source_target_pairs={{0,40},{1,99},{2,42},{3,101},{4,44},{5,103},{6,46},{7,97},{8,48},{... | collective-permute-start | bytes 6152 | tf_op jit(solution)/shard_map/ppermute | solution.py:266
  55.2 4.5 %collective-permute-start.22 = (f32[2,1,256]{2,1,0:T(1,128)S(1)}, f32[2,1,256]{2,1,0:T(1,128)S(1)}, u32[]{:S(2)}, u32[]{:S(2)}) collective-permute-start(f32[2,1,256]{2,1,0:T(1,128)S(1)} %get-tuple-element.24), channel_id=1, source_target_pairs={{0,102},{1,7},{2,96},{3,1},{4,98},{5,3},{6,100},{7,5},{8,110},{9,1... | collective-permute-start | bytes 6152 | tf_op jit(solution)/shard_map/ppermute | solution.py:266
  59.8 3.7 %collective-permute-start.23 = (f32[256]{0:T(256)S(1)}, f32[256]{0:T(256)S(1)}, u32[]{:S(2)}, u32[]{:S(2)}) collective-permute-start(f32[256]{0:T(256)S(1)} %bitcast.5), channel_id=1, source_target_pairs={{0,1},{1,0},{2,3},{3,2},{4,5},{5,4},{6,7},{7,6},{8,9},{9,8},{10,11... | collective-permute-start | bytes 3080 | tf_op jit(solution)/shard_map/ppermute | solution.py:269

commit v6 on v5

--- a/solution.py
+++ b/solution.py
@@ -15,10 +15,11 @@
 BOTH = ("cluster", "member")
 CLUSTER_SHIFT = 5
 
-PLAN = ((0, 13), (0, 20), (0, 3), (0, 49), (1, 48), (1, 16), (2, 3), (3, 48), (4, 4), (3, 12))
+PLAN = ((0, 13), (0, 3), (0, 20), (0, 49), (1, 48), (1, 16), (3, 3), (2, 48), (4, 4), (2, 12))
 BLOCKS = len(PLAN) + 1
 EARLY, LATE = (0, 1, 2, 3), (4, 5, 6)
 PHASES = ((4, EARLY), (7, EARLY), (BLOCKS, EARLY), (BLOCKS, EARLY + LATE))
+HELD_BACK = 4
 
 
 def shift(place, by):
@@ -247,13 +248,21 @@
 def shards(embeddings, destination):
     core = core_index()
     mine = [pack(embeddings, destination)]
-    for source, jump in PLAN[:8]:
-        mine.append(lax.ppermute(mine[source], BOTH, fetch((jump, mirror(jump)))))
+    mine += [None] * len(PLAN)
+
+    def bring(k, block):
+        jump = PLAN[k - 1][1]
+        mine[k] = lax.ppermute(block, BOTH, fetch((jump, mirror(jump))))
+
+    after = [k for k in range(1, BLOCKS) if PLAN[k - 1][0] == HELD_BACK]
+    for k in range(1, BLOCKS):
+        if k not in after:
+            bring(k, mine[PLAN[k - 1][0]])
     other = {k: lax.ppermute(mine[k], BOTH, CORE_SWAP) for k in EARLY}
     (sums,) = pair_sums(0, mine, other, None)
-    held, sums = lax.optimization_barrier((mine[4], sums))
-    for source, jump in PLAN[8:]:
-        mine.append(lax.ppermute(held if source == 4 else mine[source], BOTH, fetch((jump, mirror(jump)))))
+    held, sums = lax.optimization_barrier((mine[HELD_BACK], sums))
+    for k in after:
+        bring(k, held)
     (sums,) = pair_sums(1, mine, other, sums)
     later, sums = lax.optimization_barrier(([mine[k] for k in LATE], sums))
     other.update({k: lax.ppermute(block, BOTH, CORE_SWAP) for k, block in zip(LATE, later)})
@@ -264,9 +273,8 @@
     for n in range(SHARE):
         jumps = [SHARES[c][n] for c in (0, 1)]
         home += lax.ppermute(kept[2 * n : 2 * n + 2], BOTH, give(jumps))
-    home = home.reshape(2, ROWS)
-    own, rest = jnp.where(core == 0, home[0], home[1]), jnp.where(core == 0, home[1], home[0])
-    return jnp.log1p(own + lax.ppermute(rest, BOTH, CORE_SWAP))
+    density = home + lax.ppermute(home, BOTH, CORE_SWAP)
+    return jnp.log1p(jnp.where(core == 0, density[0, 0], density[1, 0]))
 
 
 def solution(mesh):

time: 64.1 us -> 63.8 us (level)
  waiting for transfers between devices: 9.56 us -> 10.5 us
  starting transfers between devices: 42.6 us -> 41.7 us
    ppermute x3, starting transfers between devices: 5.79 us -> 2.54 us  [shards(): lax.ppermute(block, BOTH, CORE_SWAP)]
    ppermute x5, starting transfers between devices: 8.72 us -> 10.7 us  [shards(): home += lax.ppermute(kept[2 * n:2 * n + 2], BOTH, give(jumps))]
    ppermute x11, waiting for transfers between devices: 6.34 us -> 7.38 us  [the longest x10 6.56 us: bring(): mine[k] = lax.ppermute(block, BOTH, fetch((jump, mirror(jump))))]
  transfers between devices with their start and end apart: 24 -> 24, of which waited for: 8 -> 8; matrix products, arithmetic and copies ran while one was open for 0% -> 0% of each run, Pallas kernels for 14% -> 13%
where the time goes in v6:
time: 63.8 us; the launch traced here: 63.7 us
  starting transfers between devices  41.7 us (65%)
  Pallas kernels  10.8 us (17%)
  waiting for transfers between devices  10.5 us (16%)
    ppermute x10, starting transfers between devices, bring(): mine[k] = lax.ppermute(block, BOTH, fetch((jump, mirror(jump))))  19.4 us
    ppermute x5, starting transfers between devices, shards(): home += lax.ppermute(kept[2 * n:2 * n + 2], BOTH, give(jumps))  10.7 us
    pallas_call x4, Pallas kernels, pair_sums(): pl.pallas_call(functools.partial(pairs_body, work, mine_used, other_used,...  9.66 us
    ppermute x10, waiting for transfers between devices, bring(): mine[k] = lax.ppermute(block, BOTH, fetch((jump, mirror(jump))))  6.56 us
    ppermute x4, starting transfers between devices, shards(): other = {k: lax.ppermute(mine[k], BOTH, CORE_SWAP) for k in EARLY}  6.11 us
    ppermute x1, starting transfers between devices, shards(): density = home + lax.ppermute(home, BOTH, CORE_SWAP)  2.84 us
    ppermute x3, starting transfers between devices, shards(): lax.ppermute(block, BOTH, CORE_SWAP)  2.54 us
    ppermute x5, waiting for transfers between devices, shards(): home += lax.ppermute(kept[2 * n:2 * n + 2], BOTH, give(jumps))  2 us
  transfers between devices with their start and end apart: 24, of which 8 were waited for; matrix products, arithmetic and copies ran while one was open for 0% of the time, Pallas kernels for 13%

profile of v6, /device:TPU:1, one launch (start us, length us, event | category | flops | bytes accessed | tf_op | source)
XLA Modules:
  0.0 63.7 jit_solution(2552438630830204255)
XLA Ops:
  0.0 1.2 %pack.1.refs_0_ = bf16[272,768]{1,0:T(8,128)(2,1)S(1)} custom-call(bf16[256,768]{1,0:T(8,128)(2,1)} %rows_ref.1, s32[1,256]{1,0:T(1,128)} %bitcast.2), custom_call_target="tpu_custom_call" | custom-call | tf_op jit(solution)/shard_map/pack/pallas_call | solution.py:118
  1.2 4.7 %collective-permute-start.1 = (bf16[272,768]{1,0:T(8,128)(2,1)S(1)}, bf16[272,768]{1,0:T(8,128)(2,1)S(1)}, u32[]{:S(2)}, u32[]{:S(2)}) collective-permute-start(bf16[272,768]{1,0:T(8,128)(2,1)S(1)} %pack.1.refs_0_), channel_id=1, source_target_pairs={{26,0},{99,1},{28,2},{101,3},{30,4},{103,5},{24,6},{97,7},{2,8},{1... | collective-permute-start | bytes 1253384 | tf_op jit(solution)/shard_map/ppermute | solution.py:255
  5.9 0.0 collective-permute-start.5
  5.9 3.7 %collective-permute-start.3 = (bf16[272,768]{1,0:T(8,128)(2,1)S(1)}, bf16[272,768]{1,0:T(8,128)(2,1)S(1)}, u32[]{:S(2)}, u32[]{:S(2)}) collective-permute-start(bf16[272,768]{1,0:T(8,128)(2,1)S(1)} %pack.1.refs_0_), channel_id=1, source_target_pairs={{40,0},{41,1},{42,2},{43,3},{44,4},{45,5},{46,6},{47,7},{48,8},{49... | collective-permute-start | bytes 1253384 | tf_op jit(solution)/shard_map/ppermute | solution.py:255
  9.6 2.1 %collective-permute-start.6 = (bf16[272,768]{1,0:T(8,128)(2,1)S(1)}, bf16[272,768]{1,0:T(8,128)(2,1)S(1)}, u32[]{:S(2)}, u32[]{:S(2)}) collective-permute-start(bf16[272,768]{1,0:T(8,128)(2,1)S(1)} %pack.1.refs_0_), channel_id=1, source_target_pairs={{0,1},{1,0},{2,3},{3,2},{4,5},{5,4},{6,7},{7,6},{8,9},{9,8},{10,11... | collective-permute-start | bytes 1253384 | tf_op jit(solution)/shard_map/ppermute | solution.py:261
  11.6 2.8 %collective-permute-start = (bf16[272,768]{1,0:T(8,128)(2,1)S(1)}, bf16[272,768]{1,0:T(8,128)(2,1)S(1)}, u32[]{:S(2)}, u32[]{:S(2)}) collective-permute-start(bf16[272,768]{1,0:T(8,128)(2,1)S(1)} %pack.1.refs_0_), channel_id=1, source_target_pairs={{98,0},{27,1},{100,2},{29,3},{102,4},{31,5},{96,6},{25,7},{106,8},... | collective-permute-start | bytes 1253384 | tf_op jit(solution)/shard_map/ppermute | solution.py:255
  14.4 0.2 collective-permute-done.1.refs_1_
  14.6 2.1 %collective-permute-start.7 = (bf16[272,768]{1,0:T(8,128)(2,1)S(1)}, bf16[272,768]{1,0:T(8,128)(2,1)S(1)}, u32[]{:S(2)}, u32[]{:S(2)}) collective-permute-start(bf16[272,768]{1,0:T(8,128)(2,1)S(1)} %collective-permute-done.1.refs_1_), channel_id=1, source_target_pairs={{0,1},{1,0},{2,3},{3,2},{4,5},{5,4},{6,7},{7,6},{8,9},{9,8},{10,11... | collective-permute-start | bytes 1253384 | tf_op jit(solution)/shard_map/ppermute | solution.py:261
  16.7 1.0 %collective-permute-done.5.refs_2_ = bf16[272,768]{1,0:T(8,128)(2,1)S(1)} collective-permute-done((bf16[272,768]{1,0:T(8,128)(2,1)S(1)}, bf16[272,768]{1,0:T(8,128)(2,1)S(1)}, u32[]{:S(2)}, u32[]{:S(2)}) %collective-permute-start.5) | collective-permute-done | bytes 417824 | tf_op jit(solution)/shard_map/ppermute | solution.py:255
  17.7 1.5 %collective-permute-start.8 = (bf16[272,768]{1,0:T(8,128)(2,1)S(1)}, bf16[272,768]{1,0:T(8,128)(2,1)S(1)}, u32[]{:S(2)}, u32[]{:S(2)}) collective-permute-start(bf16[272,768]{1,0:T(8,128)(2,1)S(1)} %collective-permute-done.5.refs_2_), channel_id=1, source_target_pairs={{0,1},{1,0},{2,3},{3,2},{4,5},{5,4},{6,7},{7,6},{8,9},{9,8},{10,11... | collective-permute-start | bytes 1253384 | tf_op jit(solution)/shard_map/ppermute | solution.py:261
  19.2 0.0 collective-permute-done.3.refs_3_.refs_2_
  19.2 3.0 %collective-permute-start.2 = (bf16[272,768]{1,0:T(8,128)(2,1)S(1)}, bf16[272,768]{1,0:T(8,128)(2,1)S(1)}, u32[]{:S(2)}, u32[]{:S(2)}) collective-permute-start(bf16[272,768]{1,0:T(8,128)(2,1)S(1)} %collective-permute-done.1.refs_1_), channel_id=1, source_target_pairs={{32,0},{9,1},{34,2},{11,3},{36,4},{13,5},{38,6},{15,7},{40,8},{17,... | collective-permute-start | bytes 1253384 | tf_op jit(solution)/shard_map/ppermute | solution.py:255
  22.1 0.0 collective-permute-done.6.refs_4_.refs_7_.refs_10_
  22.1 0.0 collective-permute-start.10
  22.1 3.7 %collective-permute-done.refs_4_.refs_3_.refs_0_ = bf16[272,768]{1,0:T(8,128)(2,1)S(1)} collective-permute-done((bf16[272,768]{1,0:T(8,128)(2,1)S(1)}, bf16[272,768]{1,0:T(8,128)(2,1)S(1)}, u32[]{:S(2)}, u32[]{:S(2)}) %collective-permute-start) | collective-permute-done | bytes 417824 | tf_op jit(solution)/shard_map/ppermute | solution.py:255
  25.8 0.5 collective-permute-start.11
  26.3 0.0 collective-permute-done.7.refs_5_.refs_8_.refs_11_
  26.3 1.2 %collective-permute-start.4 = (bf16[272,768]{1,0:T(8,128)(2,1)S(1)}, bf16[272,768]{1,0:T(8,128)(2,1)S(1)}, u32[]{:S(2)}, u32[]{:S(2)}) collective-permute-start(bf16[272,768]{1,0:T(8,128)(2,1)S(1)} %collective-permute-done.3.refs_3_.refs_2_), channel_id=1, source_target_pairs={{6,0},{7,1},{0,2},{1,3},{2,4},{3,5},{4,6},{5,7},{14,8},{15,9},{8,1... | collective-permute-start | bytes 1253384 | tf_op jit(solution)/shard_map/ppermute | solution.py:255
  27.5 0.0 collective-permute-done.8.refs_6_.refs_9_.refs_12_
  27.5 1.3 %collective-permute-start.15 = (bf16[272,768]{1,0:T(8,128)(2,1)S(1)}, bf16[272,768]{1,0:T(8,128)(2,1)S(1)}, u32[]{:S(2)}, u32[]{:S(2)}) collective-permute-start(bf16[272,768]{1,0:T(8,128)(2,1)S(1)} %collective-permute-done.5.refs_2_), channel_id=1, source_target_pairs={{96,0},{25,1},{98,2},{27,3},{100,4},{29,5},{102,6},{31,7},{104,8},... | collective-permute-start | bytes 1253384 | tf_op jit(solution)/shard_map/ppermute | solution.py:255
  28.8 2.1 %pair_sums_0.1.refs_11_ = f32[22,1,256]{2,1,0:T(1,128)S(1)} custom-call(bf16[272,768]{1,0:T(8,128)(2,1)S(1)} %pack.1.refs_0_, bf16[272,768]{1,0:T(8,128)(2,1)S(1)} %collective-permute-done.1.refs_1_, bf16[272,768]{1,0:T(8,128)(2,1)S(1)} %collective-permute-done.5.refs_2_, bf16[272,768]{1,0:T(8,128)(2,1)S(1)} %collective-permute-done.3.refs_3_.refs_2_, ...), custom_call_target="tpu_custom_call" | custom-call | flops 1409286144 | tf_op jit(solution)/shard_map/pair_sums_0/pallas_call | solution.py:221
  30.9 0.0 collective-permute-done.2.refs_6_.refs_5_.refs_1_
  30.9 0.1 collective-permute-start.16
  31.0 2.7 %collective-permute-start.9 = (bf16[272,768]{1,0:T(8,128)(2,1)S(1)}, bf16[272,768]{1,0:T(8,128)(2,1)S(1)}, u32[]{:S(2)}, u32[]{:S(2)}) collective-permute-start(bf16[272,768]{1,0:T(8,128)(2,1)S(1)} %collective-permute-done.refs_4_.refs_3_.refs_0_), channel_id=1, source_target_pairs={{8,0},{33,1},{10,2},{35,3},{12,4},{37,5},{14,6},{39,7},{16,8},{41,... | collective-permute-start | bytes 1253384 | tf_op jit(solution)/shard_map/ppermute | solution.py:255
  33.7 0.0 collective-permute-done.11.refs_10_.refs_13_
  33.7 3.1 %pair_sums_1.1.refs_14_ = f32[22,1,256]{2,1,0:T(1,128)S(1)} custom-call(bf16[272,768]{1,0:T(8,128)(2,1)S(1)} %pack.1.refs_0_, bf16[272,768]{1,0:T(8,128)(2,1)S(1)} %collective-permute-done.1.refs_1_, bf16[272,768]{1,0:T(8,128)(2,1)S(1)} %collective-permute-done.5.refs_2_, bf16[272,768]{1,0:T(8,128)(2,1)S(1)} %collective-permute-done.3.refs_3_.refs_2_, ...), custom_call_target="tpu_custom_call" | custom-call | flops 2415919104 | tf_op jit(solution)/shard_map/pair_sums_1/pallas_call | solution.py:221
  36.8 1.5 %collective-permute-start.12 = (bf16[272,768]{1,0:T(8,128)(2,1)S(1)}, bf16[272,768]{1,0:T(8,128)(2,1)S(1)}, u32[]{:S(2)}, u32[]{:S(2)}) collective-permute-start(bf16[272,768]{1,0:T(8,128)(2,1)S(1)} %collective-permute-done.refs_4_.refs_3_.refs_0_), channel_id=1, source_target_pairs={{0,1},{1,0},{2,3},{3,2},{4,5},{5,4},{6,7},{7,6},{8,9},{9,8},{10,11... | collective-permute-start | bytes 1253384 | tf_op jit(solution)/shard_map/ppermute | solution.py:268
  38.3 0.7 %collective-permute-done.4.refs_6_.refs_2_ = bf16[272,768]{1,0:T(8,128)(2,1)S(1)} collective-permute-done((bf16[272,768]{1,0:T(8,128)(2,1)S(1)}, bf16[272,768]{1,0:T(8,128)(2,1)S(1)}, u32[]{:S(2)}, u32[]{:S(2)}) %collective-permute-start.4) | collective-permute-done | bytes 417824 | tf_op jit(solution)/shard_map/ppermute | solution.py:255
  39.0 1.0 %collective-permute-start.13 = (bf16[272,768]{1,0:T(8,128)(2,1)S(1)}, bf16[272,768]{1,0:T(8,128)(2,1)S(1)}, u32[]{:S(2)}, u32[]{:S(2)}) collective-permute-start(bf16[272,768]{1,0:T(8,128)(2,1)S(1)} %collective-permute-done.10.refs_5_.refs_4_), channel_id=1, source_target_pairs={{0,1},{1,0},{2,3},{3,2},{4,5},{5,4},{6,7},{7,6},{8,9},{9,8},{10,11... | collective-permute-start | bytes 1253384 | tf_op jit(solution)/shard_map/ppermute | solution.py:268
  40.0 0.0 collective-permute-done.15.refs_7_
  40.0 0.0 collective-permute-start.14
  40.0 0.9 %collective-permute-done.16.refs_9_ = bf16[272,768]{1,0:T(8,128)(2,1)S(1)} collective-permute-done((bf16[272,768]{1,0:T(8,128)(2,1)S(1)}, bf16[272,768]{1,0:T(8,128)(2,1)S(1)}, u32[]{:S(2)}, u32[]{:S(2)}) %collective-permute-start.16) | collective-permute-done | bytes 417824 | tf_op jit(solution)/shard_map/ppermute | solution.py:255
  41.0 3.3 %pair_sums_2.1.refs_7_ = f32[22,1,256]{2,1,0:T(1,128)S(1)} custom-call(bf16[272,768]{1,0:T(8,128)(2,1)S(1)} %pack.1.refs_0_, bf16[272,768]{1,0:T(8,128)(2,1)S(1)} %collective-permute-done.1.refs_1_, bf16[272,768]{1,0:T(8,128)(2,1)S(1)} %collective-permute-done.3.refs_3_.refs_2_, bf16[272,768]{1,0:T(8,128)(2,1)S(1)} %collective-permute-done.refs_4_.refs_3_.refs_0_, ...), custom_call_target="tpu_custom_call" | custom-call | flops 2113929216 | tf_op jit(solution)/shard_map/pair_sums_2/pallas_call | solution.py:221
  44.2 0.0 collective-permute-done.12.refs_4_
  44.3 1.2 %pair_sums_3.1 = (f32[10,1,256]{2,1,0:T(1,128)S(1)}, f32[10,1,256]{2,1,0:T(1,128)S(1)}, f32[2,1,256]{2,1,0:T(1,128)S(1)}) custom-call(bf16[272,768]{1,0:T(8,128)(2,1)S(1)} %collective-permute-done.refs_4_.refs_3_.refs_0_, bf16[272,768]{1,0:T(8,128)(2,1)S(1)} %collective-permute-done.2.refs_6_.refs_5_.refs_1_, ...), custom_call_target="tpu_custom_call" | custom-call | flops 553648128 | tf_op jit(solution)/shard_map/pair_sums_3/pallas_call | solution.py:221
  45.5 0.2 collective-permute-start.17
  45.7 1.1 %collective-permute-done.17 = f32[10,1,256]{2,1,0:T(1,128)S(1)} collective-permute-done((f32[10,1,256]{2,1,0:T(1,128)S(1)}, f32[10,1,256]{2,1,0:T(1,128)S(1)}, u32[]{:S(2)}, u32[]{:S(2)}) %collective-permute-start.17) | collective-permute-done | bytes 10272 | tf_op jit(solution)/shard_map/ppermute | solution.py:272
  46.8 5.1 %collective-permute-start.18 = (f32[2,1,256]{2,1,0:T(1,128)S(1)}, f32[2,1,256]{2,1,0:T(1,128)S(1)}, u32[]{:S(2)}, u32[]{:S(2)}) collective-permute-start(f32[2,1,256]{2,1,0:T(1,128)S(1)} %get-tuple-element.23), channel_id=1, source_target_pairs={{0,46},{1,59},{2,40},{3,61},{4,42},{5,63},{6,44},{7,57},{8,54},{9,... | collective-permute-start | bytes 6152 | tf_op jit(solution)/shard_map/ppermute | solution.py:275
  51.8 1.8 %collective-permute-start.19 = (f32[2,1,256]{2,1,0:T(1,128)S(1)}, f32[2,1,256]{2,1,0:T(1,128)S(1)}, u32[]{:S(2)}, u32[]{:S(2)}) collective-permute-start(f32[2,1,256]{2,1,0:T(1,128)S(1)} %get-tuple-element.27), channel_id=1, source_target_pairs={{0,106},{1,123},{2,108},{3,125},{4,110},{5,127},{6,104},{7,121},{8... | collective-permute-start | bytes 6152 | tf_op jit(solution)/shard_map/ppermute | solution.py:275
  53.6 1.3 %collective-permute-start.20 = (f32[2,1,256]{2,1,0:T(1,128)S(1)}, f32[2,1,256]{2,1,0:T(1,128)S(1)}, u32[]{:S(2)}, u32[]{:S(2)}) collective-permute-start(f32[2,1,256]{2,1,0:T(1,128)S(1)} %get-tuple-element.26), channel_id=1, source_target_pairs={{0,26},{1,31},{2,28},{3,25},{4,30},{5,27},{6,24},{7,29},{8,2},{9,7... | collective-permute-start | bytes 6152 | tf_op jit(solution)/shard_map/ppermute | solution.py:275
  54.9 0.0 collective-permute-start.21
  54.9 2.5 %collective-permute-start.22 = (f32[2,1,256]{2,1,0:T(1,128)S(1)}, f32[2,1,256]{2,1,0:T(1,128)S(1)}, u32[]{:S(2)}, u32[]{:S(2)}) collective-permute-start(f32[2,1,256]{2,1,0:T(1,128)S(1)} %get-tuple-element.24), channel_id=1, source_target_pairs={{0,102},{1,7},{2,96},{3,1},{4,98},{5,3},{6,100},{7,5},{8,110},{9,1... | collective-permute-start | bytes 6152 | tf_op jit(solution)/shard_map/ppermute | solution.py:275
  57.4 0.0 collective-permute-done.19
  57.5 2.0 %collective-permute-done.21 = f32[2,1,256]{2,1,0:T(1,128)S(1)} collective-permute-done((f32[2,1,256]{2,1,0:T(1,128)S(1)}, f32[2,1,256]{2,1,0:T(1,128)S(1)}, u32[]{:S(2)}, u32[]{:S(2)}) %collective-permute-start.21) | collective-permute-done | bytes 2080 | tf_op jit(solution)/shard_map/ppermute | solution.py:275
  59.4 0.0 collective-permute-done.22
  59.5 2.8 %collective-permute-start.23 = (f32[2,1,256]{2,1,0:T(1,128)S(1)}, f32[2,1,256]{2,1,0:T(1,128)S(1)}, u32[]{:S(2)}, u32[]{:S(2)}) collective-permute-start(f32[2,1,256]{2,1,0:T(1,128)S(1)} %add_add_fusion), channel_id=1, source_target_pairs={{0,1},{1,0},{2,3},{3,2},{4,5},{5,4},{6,7},{7,6},{8,9},{9,8},{10,11... | collective-permute-start | bytes 6152 | tf_op jit(solution)/shard_map/ppermute | solution.py:276
  62.3 0.8 %collective-permute-done.23 = f32[2,1,256]{2,1,0:T(1,128)S(1)} collective-permute-done((f32[2,1,256]{2,1,0:T(1,128)S(1)}, f32[2,1,256]{2,1,0:T(1,128)S(1)}, u32[]{:S(2)}, u32[]{:S(2)}) %collective-permute-start.23) | collective-permute-done | bytes 2080 | tf_op jit(solution)/shard_map/ppermute | solution.py:276
  63.1 0.6 fusion
  (10 shorter events, 0.0 us)
Async XLA Ops:
  1.2 13.4 %collective-permute-start.1 = (bf16[272,768]{1,0:T(8,128)(2,1)S(1)}, bf16[272,768]{1,0:T(8,128)(2,1)S(1)}, u32[]{:S(2)}, u32[]{:S(2)}) collective-permute-start(bf16[272,768]{1,0:T(8,128)(2,1)S(1)} %pack.1.refs_0_), channel_id=1, source_target_pairs={{26,0},{99,1},{28,2},{101,3},{30,4},{103,5},{24,6},{97,7},{2,8},{1... | collective-permute-start | bytes 1253384 | tf_op jit(solution)/shard_map/ppermute | solution.py:255
  5.9 11.8 %collective-permute-start.5 = (bf16[272,768]{1,0:T(8,128)(2,1)S(1)}, bf16[272,768]{1,0:T(8,128)(2,1)S(1)}, u32[]{:S(2)}, u32[]{:S(2)}) collective-permute-start(bf16[272,768]{1,0:T(8,128)(2,1)S(1)} %pack.1.refs_0_), channel_id=1, source_target_pairs={{6,0},{7,1},{0,2},{1,3},{2,4},{3,5},{4,6},{5,7},{14,8},{15,9},{8,1... | collective-permute-start | bytes 1253384 | tf_op jit(solution)/shard_map/ppermute | solution.py:255
  5.9 13.3 %collective-permute-start.3 = (bf16[272,768]{1,0:T(8,128)(2,1)S(1)}, bf16[272,768]{1,0:T(8,128)(2,1)S(1)}, u32[]{:S(2)}, u32[]{:S(2)}) collective-permute-start(bf16[272,768]{1,0:T(8,128)(2,1)S(1)} %pack.1.refs_0_), channel_id=1, source_target_pairs={{40,0},{41,1},{42,2},{43,3},{44,4},{45,5},{46,6},{47,7},{48,8},{49... | collective-permute-start | bytes 1253384 | tf_op jit(solution)/shard_map/ppermute | solution.py:255
  9.6 12.6 %collective-permute-start.6 = (bf16[272,768]{1,0:T(8,128)(2,1)S(1)}, bf16[272,768]{1,0:T(8,128)(2,1)S(1)}, u32[]{:S(2)}, u32[]{:S(2)}) collective-permute-start(bf16[272,768]{1,0:T(8,128)(2,1)S(1)} %pack.1.refs_0_), channel_id=1, source_target_pairs={{0,1},{1,0},{2,3},{3,2},{4,5},{5,4},{6,7},{7,6},{8,9},{9,8},{10,11... | collective-permute-start | bytes 1253384 | tf_op jit(solution)/shard_map/ppermute | solution.py:261
  11.6 14.2 %collective-permute-start = (bf16[272,768]{1,0:T(8,128)(2,1)S(1)}, bf16[272,768]{1,0:T(8,128)(2,1)S(1)}, u32[]{:S(2)}, u32[]{:S(2)}) collective-permute-start(bf16[272,768]{1,0:T(8,128)(2,1)S(1)} %pack.1.refs_0_), channel_id=1, source_target_pairs={{98,0},{27,1},{100,2},{29,3},{102,4},{31,5},{96,6},{25,7},{106,8},... | collective-permute-start | bytes 1253384 | tf_op jit(solution)/shard_map/ppermute | solution.py:255
  14.6 11.7 %collective-permute-start.7 = (bf16[272,768]{1,0:T(8,128)(2,1)S(1)}, bf16[272,768]{1,0:T(8,128)(2,1)S(1)}, u32[]{:S(2)}, u32[]{:S(2)}) collective-permute-start(bf16[272,768]{1,0:T(8,128)(2,1)S(1)} %collective-permute-done.1.refs_1_), channel_id=1, source_target_pairs={{0,1},{1,0},{2,3},{3,2},{4,5},{5,4},{6,7},{7,6},{8,9},{9,8},{10,11... | collective-permute-start | bytes 1253384 | tf_op jit(solution)/shard_map/ppermute | solution.py:261
  17.7 9.8 %collective-permute-start.8 = (bf16[272,768]{1,0:T(8,128)(2,1)S(1)}, bf16[272,768]{1,0:T(8,128)(2,1)S(1)}, u32[]{:S(2)}, u32[]{:S(2)}) collective-permute-start(bf16[272,768]{1,0:T(8,128)(2,1)S(1)} %collective-permute-done.5.refs_2_), channel_id=1, source_target_pairs={{0,1},{1,0},{2,3},{3,2},{4,5},{5,4},{6,7},{7,6},{8,9},{9,8},{10,11... | collective-permute-start | bytes 1253384 | tf_op jit(solution)/shard_map/ppermute | solution.py:261
  19.2 11.7 %collective-permute-start.2 = (bf16[272,768]{1,0:T(8,128)(2,1)S(1)}, bf16[272,768]{1,0:T(8,128)(2,1)S(1)}, u32[]{:S(2)}, u32[]{:S(2)}) collective-permute-start(bf16[272,768]{1,0:T(8,128)(2,1)S(1)} %collective-permute-done.1.refs_1_), channel_id=1, source_target_pairs={{32,0},{9,1},{34,2},{11,3},{36,4},{13,5},{38,6},{15,7},{40,8},{17,... | collective-permute-start | bytes 1253384 | tf_op jit(solution)/shard_map/ppermute | solution.py:255
  22.1 8.9 %collective-permute-start.10 = (bf16[272,768]{1,0:T(8,128)(2,1)S(1)}, bf16[272,768]{1,0:T(8,128)(2,1)S(1)}, u32[]{:S(2)}, u32[]{:S(2)}) collective-permute-start(bf16[272,768]{1,0:T(8,128)(2,1)S(1)} %collective-permute-done.1.refs_1_), channel_id=1, source_target_pairs={{96,0},{25,1},{98,2},{27,3},{100,4},{29,5},{102,6},{31,7},{104,8},... | collective-permute-start | bytes 1253384 | tf_op jit(solution)/shard_map/ppermute | solution.py:255
  25.8 7.8 %collective-permute-start.11 = (bf16[272,768]{1,0:T(8,128)(2,1)S(1)}, bf16[272,768]{1,0:T(8,128)(2,1)S(1)}, u32[]{:S(2)}, u32[]{:S(2)}) collective-permute-start(bf16[272,768]{1,0:T(8,128)(2,1)S(1)} %collective-permute-done.3.refs_3_.refs_2_), channel_id=1, source_target_pairs={{0,1},{1,0},{2,3},{3,2},{4,5},{5,4},{6,7},{7,6},{8,9},{9,8},{10,11... | collective-permute-start | bytes 1253384 | tf_op jit(solution)/shard_map/ppermute | solution.py:261
  26.3 12.7 %collective-permute-start.4 = (bf16[272,768]{1,0:T(8,128)(2,1)S(1)}, bf16[272,768]{1,0:T(8,128)(2,1)S(1)}, u32[]{:S(2)}, u32[]{:S(2)}) collective-permute-start(bf16[272,768]{1,0:T(8,128)(2,1)S(1)} %collective-permute-done.3.refs_3_.refs_2_), channel_id=1, source_target_pairs={{6,0},{7,1},{0,2},{1,3},{2,4},{3,5},{4,6},{5,7},{14,8},{15,9},{8,1... | collective-permute-start | bytes 1253384 | tf_op jit(solution)/shard_map/ppermute | solution.py:255
  27.5 12.5 %collective-permute-start.15 = (bf16[272,768]{1,0:T(8,128)(2,1)S(1)}, bf16[272,768]{1,0:T(8,128)(2,1)S(1)}, u32[]{:S(2)}, u32[]{:S(2)}) collective-permute-start(bf16[272,768]{1,0:T(8,128)(2,1)S(1)} %collective-permute-done.5.refs_2_), channel_id=1, source_target_pairs={{96,0},{25,1},{98,2},{27,3},{100,4},{29,5},{102,6},{31,7},{104,8},... | collective-permute-start | bytes 1253384 | tf_op jit(solution)/shard_map/ppermute | solution.py:255
  30.9 10.1 %collective-permute-start.16 = (bf16[272,768]{1,0:T(8,128)(2,1)S(1)}, bf16[272,768]{1,0:T(8,128)(2,1)S(1)}, u32[]{:S(2)}, u32[]{:S(2)}) collective-permute-start(bf16[272,768]{1,0:T(8,128)(2,1)S(1)} %collective-permute-done.5.refs_2_), channel_id=1, source_target_pairs={{24,0},{97,1},{26,2},{99,3},{28,4},{101,5},{30,6},{103,7},{0,8},{1... | collective-permute-start | bytes 1253384 | tf_op jit(solution)/shard_map/ppermute | solution.py:255
  31.0 10.0 %collective-permute-start.9 = (bf16[272,768]{1,0:T(8,128)(2,1)S(1)}, bf16[272,768]{1,0:T(8,128)(2,1)S(1)}, u32[]{:S(2)}, u32[]{:S(2)}) collective-permute-start(bf16[272,768]{1,0:T(8,128)(2,1)S(1)} %collective-permute-done.refs_4_.refs_3_.refs_0_), channel_id=1, source_target_pairs={{8,0},{33,1},{10,2},{35,3},{12,4},{37,5},{14,6},{39,7},{16,8},{41,... | collective-permute-start | bytes 1253384 | tf_op jit(solution)/shard_map/ppermute | solution.py:255
  36.8 7.5 %collective-permute-start.12 = (bf16[272,768]{1,0:T(8,128)(2,1)S(1)}, bf16[272,768]{1,0:T(8,128)(2,1)S(1)}, u32[]{:S(2)}, u32[]{:S(2)}) collective-permute-start(bf16[272,768]{1,0:T(8,128)(2,1)S(1)} %collective-permute-done.refs_4_.refs_3_.refs_0_), channel_id=1, source_target_pairs={{0,1},{1,0},{2,3},{3,2},{4,5},{5,4},{6,7},{7,6},{8,9},{9,8},{10,11... | collective-permute-start | bytes 1253384 | tf_op jit(solution)/shard_map/ppermute | solution.py:268
  39.0 5.3 %collective-permute-start.13 = (bf16[272,768]{1,0:T(8,128)(2,1)S(1)}, bf16[272,768]{1,0:T(8,128)(2,1)S(1)}, u32[]{:S(2)}, u32[]{:S(2)}) collective-permute-start(bf16[272,768]{1,0:T(8,128)(2,1)S(1)} %collective-permute-done.10.refs_5_.refs_4_), channel_id=1, source_target_pairs={{0,1},{1,0},{2,3},{3,2},{4,5},{5,4},{6,7},{7,6},{8,9},{9,8},{10,11... | collective-permute-start | bytes 1253384 | tf_op jit(solution)/shard_map/ppermute | solution.py:268
  40.0 4.2 %collective-permute-start.14 = (bf16[272,768]{1,0:T(8,128)(2,1)S(1)}, bf16[272,768]{1,0:T(8,128)(2,1)S(1)}, u32[]{:S(2)}, u32[]{:S(2)}) collective-permute-start(bf16[272,768]{1,0:T(8,128)(2,1)S(1)} %collective-permute-done.2.refs_6_.refs_5_.refs_1_), channel_id=1, source_target_pairs={{0,1},{1,0},{2,3},{3,2},{4,5},{5,4},{6,7},{7,6},{8,9},{9,8},{10,11... | collective-permute-start | bytes 1253384 | tf_op jit(solution)/shard_map/ppermute | solution.py:268
  45.5 1.3 %collective-permute-start.17 = (f32[10,1,256]{2,1,0:T(1,128)S(1)}, f32[10,1,256]{2,1,0:T(1,128)S(1)}, u32[]{:S(2)}, u32[]{:S(2)}) collective-permute-start(f32[10,1,256]{2,1,0:T(1,128)S(1)} %get-tuple-element.22), channel_id=1, source_target_pairs={{0,1},{1,0},{2,3},{3,2},{4,5},{5,4},{6,7},{7,6},{8,9},{9,8},{10,11... | collective-permute-start | bytes 30728 | tf_op jit(solution)/shard_map/ppermute | solution.py:272
  46.8 10.7 %collective-permute-start.18 = (f32[2,1,256]{2,1,0:T(1,128)S(1)}, f32[2,1,256]{2,1,0:T(1,128)S(1)}, u32[]{:S(2)}, u32[]{:S(2)}) collective-permute-start(f32[2,1,256]{2,1,0:T(1,128)S(1)} %get-tuple-element.23), channel_id=1, source_target_pairs={{0,46},{1,59},{2,40},{3,61},{4,42},{5,63},{6,44},{7,57},{8,54},{9,... | collective-permute-start | bytes 6152 | tf_op jit(solution)/shard_map/ppermute | solution.py:275
  51.8 5.7 %collective-permute-start.19 = (f32[2,1,256]{2,1,0:T(1,128)S(1)}, f32[2,1,256]{2,1,0:T(1,128)S(1)}, u32[]{:S(2)}, u32[]{:S(2)}) collective-permute-start(f32[2,1,256]{2,1,0:T(1,128)S(1)} %get-tuple-element.27), channel_id=1, source_target_pairs={{0,106},{1,123},{2,108},{3,125},{4,110},{5,127},{6,104},{7,121},{8... | collective-permute-start | bytes 6152 | tf_op jit(solution)/shard_map/ppermute | solution.py:275
  53.6 3.8 %collective-permute-start.20 = (f32[2,1,256]{2,1,0:T(1,128)S(1)}, f32[2,1,256]{2,1,0:T(1,128)S(1)}, u32[]{:S(2)}, u32[]{:S(2)}) collective-permute-start(f32[2,1,256]{2,1,0:T(1,128)S(1)} %get-tuple-element.26), channel_id=1, source_target_pairs={{0,26},{1,31},{2,28},{3,25},{4,30},{5,27},{6,24},{7,29},{8,2},{9,7... | collective-permute-start | bytes 6152 | tf_op jit(solution)/shard_map/ppermute | solution.py:275
  54.9 4.5 %collective-permute-start.21 = (f32[2,1,256]{2,1,0:T(1,128)S(1)}, f32[2,1,256]{2,1,0:T(1,128)S(1)}, u32[]{:S(2)}, u32[]{:S(2)}) collective-permute-start(f32[2,1,256]{2,1,0:T(1,128)S(1)} %get-tuple-element.25), channel_id=1, source_target_pairs={{0,40},{1,99},{2,42},{3,101},{4,44},{5,103},{6,46},{7,97},{8,48},{... | collective-permute-start | bytes 6152 | tf_op jit(solution)/shard_map/ppermute | solution.py:275
  54.9 4.5 %collective-permute-start.22 = (f32[2,1,256]{2,1,0:T(1,128)S(1)}, f32[2,1,256]{2,1,0:T(1,128)S(1)}, u32[]{:S(2)}, u32[]{:S(2)}) collective-permute-start(f32[2,1,256]{2,1,0:T(1,128)S(1)} %get-tuple-element.24), channel_id=1, source_target_pairs={{0,102},{1,7},{2,96},{3,1},{4,98},{5,3},{6,100},{7,5},{8,110},{9,1... | collective-permute-start | bytes 6152 | tf_op jit(solution)/shard_map/ppermute | solution.py:275
  59.5 3.7 %collective-permute-start.23 = (f32[2,1,256]{2,1,0:T(1,128)S(1)}, f32[2,1,256]{2,1,0:T(1,128)S(1)}, u32[]{:S(2)}, u32[]{:S(2)}) collective-permute-start(f32[2,1,256]{2,1,0:T(1,128)S(1)} %add_add_fusion), channel_id=1, source_target_pairs={{0,1},{1,0},{2,3},{3,2},{4,5},{5,4},{6,7},{7,6},{8,9},{9,8},{10,11... | collective-permute-start | bytes 6152 | tf_op jit(solution)/shard_map/ppermute | solution.py:276

commit v7 on v6

--- a/solution.py
+++ b/solution.py
@@ -61,12 +61,8 @@
 assert len(set(HELD)) == BLOCKS and {mirror(o) for o in HELD} == set(HELD)
 
 
-def distance(place):
-    return sum(min(place >> s & 3, -(place >> s) & 3) for s in (0, 2, 4))
-
-
-AFAR = sorted(sorted(HELD)[1:], key=distance, reverse=True)
-SHARES = (AFAR[0::2], AFAR[1::2])
+SHARES = ((20, 23, 29, 13, 15), (3, 61, 53, 49, 51))
+assert sorted(SHARES[0] + SHARES[1]) == sorted(HELD)[1:]
 SHARE = len(SHARES[0])
 GIVEN, HOME = 16, 32
 

time: 63.8 us -> 61.9 us (0.970)
  starting transfers between devices: 41.7 us -> 39.3 us
    ppermute x1, starting transfers between devices: 2.84 us -> 1.56 us  [shards(): density = home + lax.ppermute(home, BOTH, CORE_SWAP)]
    ppermute x5, starting transfers between devices: 10.7 us -> 9.51 us  [shards(): home += lax.ppermute(kept[2 * n:2 * n + 2], BOTH, give(jumps))]
  transfers between devices with their start and end apart: 24 -> 24, of which waited for: 8 -> 9; matrix products, arithmetic and copies ran while one was open for 0% -> 0% of each run, Pallas kernels for 13% -> 14%
where the time goes in v7:
time: 61.9 us; the launch traced here: 61.7 us
  starting transfers between devices  39.3 us (63%)
  waiting for transfers between devices  11 us (18%)
  Pallas kernels  10.8 us (17%)
    ppermute x10, starting transfers between devices, bring(): mine[k] = lax.ppermute(block, BOTH, fetch((jump, mirror(jump))))  19.4 us
    pallas_call x4, Pallas kernels, pair_sums(): pl.pallas_call(functools.partial(pairs_body, work, mine_used, other_used,...  9.66 us
    ppermute x5, starting transfers between devices, shards(): home += lax.ppermute(kept[2 * n:2 * n + 2], BOTH, give(jumps))  9.51 us
    ppermute x10, waiting for transfers between devices, bring(): mine[k] = lax.ppermute(block, BOTH, fetch((jump, mirror(jump))))  6.56 us
    ppermute x4, starting transfers between devices, shards(): other = {k: lax.ppermute(mine[k], BOTH, CORE_SWAP) for k in EARLY}  6.11 us
    ppermute x3, starting transfers between devices, shards(): lax.ppermute(block, BOTH, CORE_SWAP)  2.54 us
    ppermute x5, waiting for transfers between devices, shards(): home += lax.ppermute(kept[2 * n:2 * n + 2], BOTH, give(jumps))  2.5 us
    ppermute x1, starting transfers between devices, shards(): density = home + lax.ppermute(home, BOTH, CORE_SWAP)  1.56 us
  transfers between devices with their start and end apart: 24, of which 9 were waited for; matrix products, arithmetic and copies ran while one was open for 0% of the time, Pallas kernels for 14%

profile of v7, /device:TPU:1, one launch (start us, length us, event | category | flops | bytes accessed | tf_op | source)
XLA Modules:
  0.0 61.7 jit_solution(5692597686917440704)
XLA Ops:
  0.0 1.2 %pack.1.refs_0_ = bf16[272,768]{1,0:T(8,128)(2,1)S(1)} custom-call(bf16[256,768]{1,0:T(8,128)(2,1)} %rows_ref.1, s32[1,256]{1,0:T(1,128)} %bitcast.2), custom_call_target="tpu_custom_call" | custom-call | tf_op jit(solution)/shard_map/pack/pallas_call | solution.py:114
  1.2 4.7 %collective-permute-start.1 = (bf16[272,768]{1,0:T(8,128)(2,1)S(1)}, bf16[272,768]{1,0:T(8,128)(2,1)S(1)}, u32[]{:S(2)}, u32[]{:S(2)}) collective-permute-start(bf16[272,768]{1,0:T(8,128)(2,1)S(1)} %pack.1.refs_0_), channel_id=1, source_target_pairs={{26,0},{99,1},{28,2},{101,3},{30,4},{103,5},{24,6},{97,7},{2,8},{1... | collective-permute-start | bytes 1253384 | tf_op jit(solution)/shard_map/ppermute | solution.py:251
  5.9 0.0 collective-permute-start.5
  5.9 3.7 %collective-permute-start.3 = (bf16[272,768]{1,0:T(8,128)(2,1)S(1)}, bf16[272,768]{1,0:T(8,128)(2,1)S(1)}, u32[]{:S(2)}, u32[]{:S(2)}) collective-permute-start(bf16[272,768]{1,0:T(8,128)(2,1)S(1)} %pack.1.refs_0_), channel_id=1, source_target_pairs={{40,0},{41,1},{42,2},{43,3},{44,4},{45,5},{46,6},{47,7},{48,8},{49... | collective-permute-start | bytes 1253384 | tf_op jit(solution)/shard_map/ppermute | solution.py:251
  9.6 2.1 %collective-permute-start.6 = (bf16[272,768]{1,0:T(8,128)(2,1)S(1)}, bf16[272,768]{1,0:T(8,128)(2,1)S(1)}, u32[]{:S(2)}, u32[]{:S(2)}) collective-permute-start(bf16[272,768]{1,0:T(8,128)(2,1)S(1)} %pack.1.refs_0_), channel_id=1, source_target_pairs={{0,1},{1,0},{2,3},{3,2},{4,5},{5,4},{6,7},{7,6},{8,9},{9,8},{10,11... | collective-permute-start | bytes 1253384 | tf_op jit(solution)/shard_map/ppermute | solution.py:257
  11.6 2.8 %collective-permute-start = (bf16[272,768]{1,0:T(8,128)(2,1)S(1)}, bf16[272,768]{1,0:T(8,128)(2,1)S(1)}, u32[]{:S(2)}, u32[]{:S(2)}) collective-permute-start(bf16[272,768]{1,0:T(8,128)(2,1)S(1)} %pack.1.refs_0_), channel_id=1, source_target_pairs={{98,0},{27,1},{100,2},{29,3},{102,4},{31,5},{96,6},{25,7},{106,8},... | collective-permute-start | bytes 1253384 | tf_op jit(solution)/shard_map/ppermute | solution.py:251
  14.4 0.2 collective-permute-done.1.refs_1_
  14.6 2.1 %collective-permute-start.7 = (bf16[272,768]{1,0:T(8,128)(2,1)S(1)}, bf16[272,768]{1,0:T(8,128)(2,1)S(1)}, u32[]{:S(2)}, u32[]{:S(2)}) collective-permute-start(bf16[272,768]{1,0:T(8,128)(2,1)S(1)} %collective-permute-done.1.refs_1_), channel_id=1, source_target_pairs={{0,1},{1,0},{2,3},{3,2},{4,5},{5,4},{6,7},{7,6},{8,9},{9,8},{10,11... | collective-permute-start | bytes 1253384 | tf_op jit(solution)/shard_map/ppermute | solution.py:257
  16.7 1.0 %collective-permute-done.5.refs_2_ = bf16[272,768]{1,0:T(8,128)(2,1)S(1)} collective-permute-done((bf16[272,768]{1,0:T(8,128)(2,1)S(1)}, bf16[272,768]{1,0:T(8,128)(2,1)S(1)}, u32[]{:S(2)}, u32[]{:S(2)}) %collective-permute-start.5) | collective-permute-done | bytes 417824 | tf_op jit(solution)/shard_map/ppermute | solution.py:251
  17.7 1.5 %collective-permute-start.8 = (bf16[272,768]{1,0:T(8,128)(2,1)S(1)}, bf16[272,768]{1,0:T(8,128)(2,1)S(1)}, u32[]{:S(2)}, u32[]{:S(2)}) collective-permute-start(bf16[272,768]{1,0:T(8,128)(2,1)S(1)} %collective-permute-done.5.refs_2_), channel_id=1, source_target_pairs={{0,1},{1,0},{2,3},{3,2},{4,5},{5,4},{6,7},{7,6},{8,9},{9,8},{10,11... | collective-permute-start | bytes 1253384 | tf_op jit(solution)/shard_map/ppermute | solution.py:257
  19.2 0.0 collective-permute-done.3.refs_3_.refs_2_
  19.2 3.0 %collective-permute-start.2 = (bf16[272,768]{1,0:T(8,128)(2,1)S(1)}, bf16[272,768]{1,0:T(8,128)(2,1)S(1)}, u32[]{:S(2)}, u32[]{:S(2)}) collective-permute-start(bf16[272,768]{1,0:T(8,128)(2,1)S(1)} %collective-permute-done.1.refs_1_), channel_id=1, source_target_pairs={{32,0},{9,1},{34,2},{11,3},{36,4},{13,5},{38,6},{15,7},{40,8},{17,... | collective-permute-start | bytes 1253384 | tf_op jit(solution)/shard_map/ppermute | solution.py:251
  22.1 0.0 collective-permute-done.6.refs_4_.refs_7_.refs_10_
  22.1 3.7 %collective-permute-done.refs_4_.refs_3_.refs_0_ = bf16[272,768]{1,0:T(8,128)(2,1)S(1)} collective-permute-done((bf16[272,768]{1,0:T(8,128)(2,1)S(1)}, bf16[272,768]{1,0:T(8,128)(2,1)S(1)}, u32[]{:S(2)}, u32[]{:S(2)}) %collective-permute-start) | collective-permute-done | bytes 417824 | tf_op jit(solution)/shard_map/ppermute | solution.py:251
  25.8 0.5 collective-permute-start.11
  26.3 0.0 collective-permute-done.7.refs_5_.refs_8_.refs_11_
  26.3 1.2 %collective-permute-start.4 = (bf16[272,768]{1,0:T(8,128)(2,1)S(1)}, bf16[272,768]{1,0:T(8,128)(2,1)S(1)}, u32[]{:S(2)}, u32[]{:S(2)}) collective-permute-start(bf16[272,768]{1,0:T(8,128)(2,1)S(1)} %collective-permute-done.3.refs_3_.refs_2_), channel_id=1, source_target_pairs={{6,0},{7,1},{0,2},{1,3},{2,4},{3,5},{4,6},{5,7},{14,8},{15,9},{8,1... | collective-permute-start | bytes 1253384 | tf_op jit(solution)/shard_map/ppermute | solution.py:251
  27.5 0.0 collective-permute-done.8.refs_6_.refs_9_.refs_12_
  27.5 1.3 %collective-permute-start.15 = (bf16[272,768]{1,0:T(8,128)(2,1)S(1)}, bf16[272,768]{1,0:T(8,128)(2,1)S(1)}, u32[]{:S(2)}, u32[]{:S(2)}) collective-permute-start(bf16[272,768]{1,0:T(8,128)(2,1)S(1)} %collective-permute-done.5.refs_2_), channel_id=1, source_target_pairs={{96,0},{25,1},{98,2},{27,3},{100,4},{29,5},{102,6},{31,7},{104,8},... | collective-permute-start | bytes 1253384 | tf_op jit(solution)/shard_map/ppermute | solution.py:251
  28.8 2.1 %pair_sums_0.1.refs_11_ = f32[22,1,256]{2,1,0:T(1,128)S(1)} custom-call(bf16[272,768]{1,0:T(8,128)(2,1)S(1)} %pack.1.refs_0_, bf16[272,768]{1,0:T(8,128)(2,1)S(1)} %collective-permute-done.1.refs_1_, bf16[272,768]{1,0:T(8,128)(2,1)S(1)} %collective-permute-done.5.refs_2_, bf16[272,768]{1,0:T(8,128)(2,1)S(1)} %collective-permute-done.3.refs_3_.refs_2_, ...), custom_call_target="tpu_custom_call" | custom-call | flops 1409286144 | tf_op jit(solution)/shard_map/pair_sums_0/pallas_call | solution.py:217
  30.9 0.1 collective-permute-start.16
  31.0 2.7 %collective-permute-start.9 = (bf16[272,768]{1,0:T(8,128)(2,1)S(1)}, bf16[272,768]{1,0:T(8,128)(2,1)S(1)}, u32[]{:S(2)}, u32[]{:S(2)}) collective-permute-start(bf16[272,768]{1,0:T(8,128)(2,1)S(1)} %collective-permute-done.refs_4_.refs_3_.refs_0_), channel_id=1, source_target_pairs={{8,0},{33,1},{10,2},{35,3},{12,4},{37,5},{14,6},{39,7},{16,8},{41,... | collective-permute-start | bytes 1253384 | tf_op jit(solution)/shard_map/ppermute | solution.py:251
  33.7 0.0 collective-permute-done.11.refs_10_.refs_13_
  33.7 3.1 %pair_sums_1.1.refs_14_ = f32[22,1,256]{2,1,0:T(1,128)S(1)} custom-call(bf16[272,768]{1,0:T(8,128)(2,1)S(1)} %pack.1.refs_0_, bf16[272,768]{1,0:T(8,128)(2,1)S(1)} %collective-permute-done.1.refs_1_, bf16[272,768]{1,0:T(8,128)(2,1)S(1)} %collective-permute-done.5.refs_2_, bf16[272,768]{1,0:T(8,128)(2,1)S(1)} %collective-permute-done.3.refs_3_.refs_2_, ...), custom_call_target="tpu_custom_call" | custom-call | flops 2415919104 | tf_op jit(solution)/shard_map/pair_sums_1/pallas_call | solution.py:217
  36.8 1.5 %collective-permute-start.12 = (bf16[272,768]{1,0:T(8,128)(2,1)S(1)}, bf16[272,768]{1,0:T(8,128)(2,1)S(1)}, u32[]{:S(2)}, u32[]{:S(2)}) collective-permute-start(bf16[272,768]{1,0:T(8,128)(2,1)S(1)} %collective-permute-done.refs_4_.refs_3_.refs_0_), channel_id=1, source_target_pairs={{0,1},{1,0},{2,3},{3,2},{4,5},{5,4},{6,7},{7,6},{8,9},{9,8},{10,11... | collective-permute-start | bytes 1253384 | tf_op jit(solution)/shard_map/ppermute | solution.py:264
  38.3 0.7 %collective-permute-done.4.refs_6_.refs_2_ = bf16[272,768]{1,0:T(8,128)(2,1)S(1)} collective-permute-done((bf16[272,768]{1,0:T(8,128)(2,1)S(1)}, bf16[272,768]{1,0:T(8,128)(2,1)S(1)}, u32[]{:S(2)}, u32[]{:S(2)}) %collective-permute-start.4) | collective-permute-done | bytes 417824 | tf_op jit(solution)/shard_map/ppermute | solution.py:251
  39.0 1.0 %collective-permute-start.13 = (bf16[272,768]{1,0:T(8,128)(2,1)S(1)}, bf16[272,768]{1,0:T(8,128)(2,1)S(1)}, u32[]{:S(2)}, u32[]{:S(2)}) collective-permute-start(bf16[272,768]{1,0:T(8,128)(2,1)S(1)} %collective-permute-done.10.refs_5_.refs_4_), channel_id=1, source_target_pairs={{0,1},{1,0},{2,3},{3,2},{4,5},{5,4},{6,7},{7,6},{8,9},{9,8},{10,11... | collective-permute-start | bytes 1253384 | tf_op jit(solution)/shard_map/ppermute | solution.py:264
  40.0 0.0 collective-permute-done.15.refs_7_
  40.0 0.0 collective-permute-start.14
  40.0 0.9 %collective-permute-done.16.refs_9_ = bf16[272,768]{1,0:T(8,128)(2,1)S(1)} collective-permute-done((bf16[272,768]{1,0:T(8,128)(2,1)S(1)}, bf16[272,768]{1,0:T(8,128)(2,1)S(1)}, u32[]{:S(2)}, u32[]{:S(2)}) %collective-permute-start.16) | collective-permute-done | bytes 417824 | tf_op jit(solution)/shard_map/ppermute | solution.py:251
  41.0 3.3 %pair_sums_2.1.refs_7_ = f32[22,1,256]{2,1,0:T(1,128)S(1)} custom-call(bf16[272,768]{1,0:T(8,128)(2,1)S(1)} %pack.1.refs_0_, bf16[272,768]{1,0:T(8,128)(2,1)S(1)} %collective-permute-done.1.refs_1_, bf16[272,768]{1,0:T(8,128)(2,1)S(1)} %collective-permute-done.3.refs_3_.refs_2_, bf16[272,768]{1,0:T(8,128)(2,1)S(1)} %collective-permute-done.refs_4_.refs_3_.refs_0_, ...), custom_call_target="tpu_custom_call" | custom-call | flops 2113929216 | tf_op jit(solution)/shard_map/pair_sums_2/pallas_call | solution.py:217
  44.2 0.0 collective-permute-done.12.refs_4_
  44.3 0.0 collective-permute-done.13.refs_5_
  44.3 1.2 %pair_sums_3.1 = (f32[10,1,256]{2,1,0:T(1,128)S(1)}, f32[10,1,256]{2,1,0:T(1,128)S(1)}, f32[2,1,256]{2,1,0:T(1,128)S(1)}) custom-call(bf16[272,768]{1,0:T(8,128)(2,1)S(1)} %collective-permute-done.refs_4_.refs_3_.refs_0_, bf16[272,768]{1,0:T(8,128)(2,1)S(1)} %collective-permute-done.2.refs_6_.refs_5_.refs_1_, ...), custom_call_target="tpu_custom_call" | custom-call | flops 553648128 | tf_op jit(solution)/shard_map/pair_sums_3/pallas_call | solution.py:217
  45.5 0.2 collective-permute-start.17
  45.7 1.1 %collective-permute-done.17 = f32[10,1,256]{2,1,0:T(1,128)S(1)} collective-permute-done((f32[10,1,256]{2,1,0:T(1,128)S(1)}, f32[10,1,256]{2,1,0:T(1,128)S(1)}, u32[]{:S(2)}, u32[]{:S(2)}) %collective-permute-start.17) | collective-permute-done | bytes 10272 | tf_op jit(solution)/shard_map/ppermute | solution.py:268
  46.8 2.1 %collective-permute-start.18 = (f32[2,1,256]{2,1,0:T(1,128)S(1)}, f32[2,1,256]{2,1,0:T(1,128)S(1)}, u32[]{:S(2)}, u32[]{:S(2)}) collective-permute-start(f32[2,1,256]{2,1,0:T(1,128)S(1)} %get-tuple-element.23), channel_id=1, source_target_pairs={{0,40},{1,7},{2,42},{3,1},{4,44},{5,3},{6,46},{7,5},{8,48},{9,15},... | collective-permute-start | bytes 6152 | tf_op jit(solution)/shard_map/ppermute | solution.py:271
  48.9 2.8 %collective-permute-start.19 = (f32[2,1,256]{2,1,0:T(1,128)S(1)}, f32[2,1,256]{2,1,0:T(1,128)S(1)}, u32[]{:S(2)}, u32[]{:S(2)}) collective-permute-start(f32[2,1,256]{2,1,0:T(1,128)S(1)} %get-tuple-element.27), channel_id=1, source_target_pairs={{0,46},{1,123},{2,40},{3,125},{4,42},{5,127},{6,44},{7,121},{8,54}... | collective-permute-start | bytes 6152 | tf_op jit(solution)/shard_map/ppermute | solution.py:271
  51.7 1.7 %collective-permute-start.20 = (f32[2,1,256]{2,1,0:T(1,128)S(1)}, f32[2,1,256]{2,1,0:T(1,128)S(1)}, u32[]{:S(2)}, u32[]{:S(2)}) collective-permute-start(f32[2,1,256]{2,1,0:T(1,128)S(1)} %get-tuple-element.26), channel_id=1, source_target_pairs={{0,58},{1,107},{2,60},{3,109},{4,62},{5,111},{6,56},{7,105},{8,34}... | collective-permute-start | bytes 6152 | tf_op jit(solution)/shard_map/ppermute | solution.py:271
  53.3 1.8 %collective-permute-start.21 = (f32[2,1,256]{2,1,0:T(1,128)S(1)}, f32[2,1,256]{2,1,0:T(1,128)S(1)}, u32[]{:S(2)}, u32[]{:S(2)}) collective-permute-start(f32[2,1,256]{2,1,0:T(1,128)S(1)} %get-tuple-element.25), channel_id=1, source_target_pairs={{0,26},{1,99},{2,28},{3,101},{4,30},{5,103},{6,24},{7,97},{8,2},{9... | collective-permute-start | bytes 6152 | tf_op jit(solution)/shard_map/ppermute | solution.py:271
  55.1 1.1 %collective-permute-start.22 = (f32[2,1,256]{2,1,0:T(1,128)S(1)}, f32[2,1,256]{2,1,0:T(1,128)S(1)}, u32[]{:S(2)}, u32[]{:S(2)}) collective-permute-start(f32[2,1,256]{2,1,0:T(1,128)S(1)} %get-tuple-element.24), channel_id=1, source_target_pairs={{0,30},{1,103},{2,24},{3,97},{4,26},{5,99},{6,28},{7,101},{8,6},{9... | collective-permute-start | bytes 6152 | tf_op jit(solution)/shard_map/ppermute | solution.py:271
  56.3 0.0 collective-permute-done.18
  56.3 2.1 %collective-permute-done.20 = f32[2,1,256]{2,1,0:T(1,128)S(1)} collective-permute-done((f32[2,1,256]{2,1,0:T(1,128)S(1)}, f32[2,1,256]{2,1,0:T(1,128)S(1)}, u32[]{:S(2)}, u32[]{:S(2)}) %collective-permute-start.20) | collective-permute-done | bytes 2080 | tf_op jit(solution)/shard_map/ppermute | solution.py:271
  58.3 0.0 collective-permute-done.21
  58.3 0.4 collective-permute-done.22
  58.8 1.6 %collective-permute-start.23 = (f32[2,1,256]{2,1,0:T(1,128)S(1)}, f32[2,1,256]{2,1,0:T(1,128)S(1)}, u32[]{:S(2)}, u32[]{:S(2)}) collective-permute-start(f32[2,1,256]{2,1,0:T(1,128)S(1)} %add_add_fusion), channel_id=1, source_target_pairs={{0,1},{1,0},{2,3},{3,2},{4,5},{5,4},{6,7},{7,6},{8,9},{9,8},{10,11... | collective-permute-start | bytes 6152 | tf_op jit(solution)/shard_map/ppermute | solution.py:272
  60.3 0.8 %collective-permute-done.23 = f32[2,1,256]{2,1,0:T(1,128)S(1)} collective-permute-done((f32[2,1,256]{2,1,0:T(1,128)S(1)}, f32[2,1,256]{2,1,0:T(1,128)S(1)}, u32[]{:S(2)}, u32[]{:S(2)}) %collective-permute-start.23) | collective-permute-done | bytes 2080 | tf_op jit(solution)/shard_map/ppermute | solution.py:272
  61.2 0.6 fusion
  (10 shorter events, 0.0 us)
Async XLA Ops:
  1.2 13.4 %collective-permute-start.1 = (bf16[272,768]{1,0:T(8,128)(2,1)S(1)}, bf16[272,768]{1,0:T(8,128)(2,1)S(1)}, u32[]{:S(2)}, u32[]{:S(2)}) collective-permute-start(bf16[272,768]{1,0:T(8,128)(2,1)S(1)} %pack.1.refs_0_), channel_id=1, source_target_pairs={{26,0},{99,1},{28,2},{101,3},{30,4},{103,5},{24,6},{97,7},{2,8},{1... | collective-permute-start | bytes 1253384 | tf_op jit(solution)/shard_map/ppermute | solution.py:251
  5.9 11.8 %collective-permute-start.5 = (bf16[272,768]{1,0:T(8,128)(2,1)S(1)}, bf16[272,768]{1,0:T(8,128)(2,1)S(1)}, u32[]{:S(2)}, u32[]{:S(2)}) collective-permute-start(bf16[272,768]{1,0:T(8,128)(2,1)S(1)} %pack.1.refs_0_), channel_id=1, source_target_pairs={{6,0},{7,1},{0,2},{1,3},{2,4},{3,5},{4,6},{5,7},{14,8},{15,9},{8,1... | collective-permute-start | bytes 1253384 | tf_op jit(solution)/shard_map/ppermute | solution.py:251
  5.9 13.3 %collective-permute-start.3 = (bf16[272,768]{1,0:T(8,128)(2,1)S(1)}, bf16[272,768]{1,0:T(8,128)(2,1)S(1)}, u32[]{:S(2)}, u32[]{:S(2)}) collective-permute-start(bf16[272,768]{1,0:T(8,128)(2,1)S(1)} %pack.1.refs_0_), channel_id=1, source_target_pairs={{40,0},{41,1},{42,2},{43,3},{44,4},{45,5},{46,6},{47,7},{48,8},{49... | collective-permute-start | bytes 1253384 | tf_op jit(solution)/shard_map/ppermute | solution.py:251
  9.6 12.6 %collective-permute-start.6 = (bf16[272,768]{1,0:T(8,128)(2,1)S(1)}, bf16[272,768]{1,0:T(8,128)(2,1)S(1)}, u32[]{:S(2)}, u32[]{:S(2)}) collective-permute-start(bf16[272,768]{1,0:T(8,128)(2,1)S(1)} %pack.1.refs_0_), channel_id=1, source_target_pairs={{0,1},{1,0},{2,3},{3,2},{4,5},{5,4},{6,7},{7,6},{8,9},{9,8},{10,11... | collective-permute-start | bytes 1253384 | tf_op jit(solution)/shard_map/ppermute | solution.py:257
  11.6 14.2 %collective-permute-start = (bf16[272,768]{1,0:T(8,128)(2,1)S(1)}, bf16[272,768]{1,0:T(8,128)(2,1)S(1)}, u32[]{:S(2)}, u32[]{:S(2)}) collective-permute-start(bf16[272,768]{1,0:T(8,128)(2,1)S(1)} %pack.1.refs_0_), channel_id=1, source_target_pairs={{98,0},{27,1},{100,2},{29,3},{102,4},{31,5},{96,6},{25,7},{106,8},... | collective-permute-start | bytes 1253384 | tf_op jit(solution)/shard_map/ppermute | solution.py:251
  14.6 11.7 %collective-permute-start.7 = (bf16[272,768]{1,0:T(8,128)(2,1)S(1)}, bf16[272,768]{1,0:T(8,128)(2,1)S(1)}, u32[]{:S(2)}, u32[]{:S(2)}) collective-permute-start(bf16[272,768]{1,0:T(8,128)(2,1)S(1)} %collective-permute-done.1.refs_1_), channel_id=1, source_target_pairs={{0,1},{1,0},{2,3},{3,2},{4,5},{5,4},{6,7},{7,6},{8,9},{9,8},{10,11... | collective-permute-start | bytes 1253384 | tf_op jit(solution)/shard_map/ppermute | solution.py:257
  17.7 9.8 %collective-permute-start.8 = (bf16[272,768]{1,0:T(8,128)(2,1)S(1)}, bf16[272,768]{1,0:T(8,128)(2,1)S(1)}, u32[]{:S(2)}, u32[]{:S(2)}) collective-permute-start(bf16[272,768]{1,0:T(8,128)(2,1)S(1)} %collective-permute-done.5.refs_2_), channel_id=1, source_target_pairs={{0,1},{1,0},{2,3},{3,2},{4,5},{5,4},{6,7},{7,6},{8,9},{9,8},{10,11... | collective-permute-start | bytes 1253384 | tf_op jit(solution)/shard_map/ppermute | solution.py:257
  19.2 11.7 %collective-permute-start.2 = (bf16[272,768]{1,0:T(8,128)(2,1)S(1)}, bf16[272,768]{1,0:T(8,128)(2,1)S(1)}, u32[]{:S(2)}, u32[]{:S(2)}) collective-permute-start(bf16[272,768]{1,0:T(8,128)(2,1)S(1)} %collective-permute-done.1.refs_1_), channel_id=1, source_target_pairs={{32,0},{9,1},{34,2},{11,3},{36,4},{13,5},{38,6},{15,7},{40,8},{17,... | collective-permute-start | bytes 1253384 | tf_op jit(solution)/shard_map/ppermute | solution.py:251
  22.1 8.9 %collective-permute-start.10 = (bf16[272,768]{1,0:T(8,128)(2,1)S(1)}, bf16[272,768]{1,0:T(8,128)(2,1)S(1)}, u32[]{:S(2)}, u32[]{:S(2)}) collective-permute-start(bf16[272,768]{1,0:T(8,128)(2,1)S(1)} %collective-permute-done.1.refs_1_), channel_id=1, source_target_pairs={{96,0},{25,1},{98,2},{27,3},{100,4},{29,5},{102,6},{31,7},{104,8},... | collective-permute-start | bytes 1253384 | tf_op jit(solution)/shard_map/ppermute | solution.py:251
  25.8 7.8 %collective-permute-start.11 = (bf16[272,768]{1,0:T(8,128)(2,1)S(1)}, bf16[272,768]{1,0:T(8,128)(2,1)S(1)}, u32[]{:S(2)}, u32[]{:S(2)}) collective-permute-start(bf16[272,768]{1,0:T(8,128)(2,1)S(1)} %collective-permute-done.3.refs_3_.refs_2_), channel_id=1, source_target_pairs={{0,1},{1,0},{2,3},{3,2},{4,5},{5,4},{6,7},{7,6},{8,9},{9,8},{10,11... | collective-permute-start | bytes 1253384 | tf_op jit(solution)/shard_map/ppermute | solution.py:257
  26.3 12.7 %collective-permute-start.4 = (bf16[272,768]{1,0:T(8,128)(2,1)S(1)}, bf16[272,768]{1,0:T(8,128)(2,1)S(1)}, u32[]{:S(2)}, u32[]{:S(2)}) collective-permute-start(bf16[272,768]{1,0:T(8,128)(2,1)S(1)} %collective-permute-done.3.refs_3_.refs_2_), channel_id=1, source_target_pairs={{6,0},{7,1},{0,2},{1,3},{2,4},{3,5},{4,6},{5,7},{14,8},{15,9},{8,1... | collective-permute-start | bytes 1253384 | tf_op jit(solution)/shard_map/ppermute | solution.py:251
  27.5 12.5 %collective-permute-start.15 = (bf16[272,768]{1,0:T(8,128)(2,1)S(1)}, bf16[272,768]{1,0:T(8,128)(2,1)S(1)}, u32[]{:S(2)}, u32[]{:S(2)}) collective-permute-start(bf16[272,768]{1,0:T(8,128)(2,1)S(1)} %collective-permute-done.5.refs_2_), channel_id=1, source_target_pairs={{96,0},{25,1},{98,2},{27,3},{100,4},{29,5},{102,6},{31,7},{104,8},... | collective-permute-start | bytes 1253384 | tf_op jit(solution)/shard_map/ppermute | solution.py:251
  30.9 10.1 %collective-permute-start.16 = (bf16[272,768]{1,0:T(8,128)(2,1)S(1)}, bf16[272,768]{1,0:T(8,128)(2,1)S(1)}, u32[]{:S(2)}, u32[]{:S(2)}) collective-permute-start(bf16[272,768]{1,0:T(8,128)(2,1)S(1)} %collective-permute-done.5.refs_2_), channel_id=1, source_target_pairs={{24,0},{97,1},{26,2},{99,3},{28,4},{101,5},{30,6},{103,7},{0,8},{1... | collective-permute-start | bytes 1253384 | tf_op jit(solution)/shard_map/ppermute | solution.py:251
  31.0 10.0 %collective-permute-start.9 = (bf16[272,768]{1,0:T(8,128)(2,1)S(1)}, bf16[272,768]{1,0:T(8,128)(2,1)S(1)}, u32[]{:S(2)}, u32[]{:S(2)}) collective-permute-start(bf16[272,768]{1,0:T(8,128)(2,1)S(1)} %collective-permute-done.refs_4_.refs_3_.refs_0_), channel_id=1, source_target_pairs={{8,0},{33,1},{10,2},{35,3},{12,4},{37,5},{14,6},{39,7},{16,8},{41,... | collective-permute-start | bytes 1253384 | tf_op jit(solution)/shard_map/ppermute | solution.py:251
  36.8 7.5 %collective-permute-start.12 = (bf16[272,768]{1,0:T(8,128)(2,1)S(1)}, bf16[272,768]{1,0:T(8,128)(2,1)S(1)}, u32[]{:S(2)}, u32[]{:S(2)}) collective-permute-start(bf16[272,768]{1,0:T(8,128)(2,1)S(1)} %collective-permute-done.refs_4_.refs_3_.refs_0_), channel_id=1, source_target_pairs={{0,1},{1,0},{2,3},{3,2},{4,5},{5,4},{6,7},{7,6},{8,9},{9,8},{10,11... | collective-permute-start | bytes 1253384 | tf_op jit(solution)/shard_map/ppermute | solution.py:264
  39.0 5.3 %collective-permute-start.13 = (bf16[272,768]{1,0:T(8,128)(2,1)S(1)}, bf16[272,768]{1,0:T(8,128)(2,1)S(1)}, u32[]{:S(2)}, u32[]{:S(2)}) collective-permute-start(bf16[272,768]{1,0:T(8,128)(2,1)S(1)} %collective-permute-done.10.refs_5_.refs_4_), channel_id=1, source_target_pairs={{0,1},{1,0},{2,3},{3,2},{4,5},{5,4},{6,7},{7,6},{8,9},{9,8},{10,11... | collective-permute-start | bytes 1253384 | tf_op jit(solution)/shard_map/ppermute | solution.py:264
  40.0 4.2 %collective-permute-start.14 = (bf16[272,768]{1,0:T(8,128)(2,1)S(1)}, bf16[272,768]{1,0:T(8,128)(2,1)S(1)}, u32[]{:S(2)}, u32[]{:S(2)}) collective-permute-start(bf16[272,768]{1,0:T(8,128)(2,1)S(1)} %collective-permute-done.2.refs_6_.refs_5_.refs_1_), channel_id=1, source_target_pairs={{0,1},{1,0},{2,3},{3,2},{4,5},{5,4},{6,7},{7,6},{8,9},{9,8},{10,11... | collective-permute-start | bytes 1253384 | tf_op jit(solution)/shard_map/ppermute | solution.py:264
  45.5 1.2 %collective-permute-start.17 = (f32[10,1,256]{2,1,0:T(1,128)S(1)}, f32[10,1,256]{2,1,0:T(1,128)S(1)}, u32[]{:S(2)}, u32[]{:S(2)}) collective-permute-start(f32[10,1,256]{2,1,0:T(1,128)S(1)} %get-tuple-element.22), channel_id=1, source_target_pairs={{0,1},{1,0},{2,3},{3,2},{4,5},{5,4},{6,7},{7,6},{8,9},{9,8},{10,11... | collective-permute-start | bytes 30728 | tf_op jit(solution)/shard_map/ppermute | solution.py:268
  46.8 9.5 %collective-permute-start.18 = (f32[2,1,256]{2,1,0:T(1,128)S(1)}, f32[2,1,256]{2,1,0:T(1,128)S(1)}, u32[]{:S(2)}, u32[]{:S(2)}) collective-permute-start(f32[2,1,256]{2,1,0:T(1,128)S(1)} %get-tuple-element.23), channel_id=1, source_target_pairs={{0,40},{1,7},{2,42},{3,1},{4,44},{5,3},{6,46},{7,5},{8,48},{9,15},... | collective-permute-start | bytes 6152 | tf_op jit(solution)/shard_map/ppermute | solution.py:271
  48.9 7.4 %collective-permute-start.19 = (f32[2,1,256]{2,1,0:T(1,128)S(1)}, f32[2,1,256]{2,1,0:T(1,128)S(1)}, u32[]{:S(2)}, u32[]{:S(2)}) collective-permute-start(f32[2,1,256]{2,1,0:T(1,128)S(1)} %get-tuple-element.27), channel_id=1, source_target_pairs={{0,46},{1,123},{2,40},{3,125},{4,42},{5,127},{6,44},{7,121},{8,54}... | collective-permute-start | bytes 6152 | tf_op jit(solution)/shard_map/ppermute | solution.py:271
  51.7 6.7 %collective-permute-start.20 = (f32[2,1,256]{2,1,0:T(1,128)S(1)}, f32[2,1,256]{2,1,0:T(1,128)S(1)}, u32[]{:S(2)}, u32[]{:S(2)}) collective-permute-start(f32[2,1,256]{2,1,0:T(1,128)S(1)} %get-tuple-element.26), channel_id=1, source_target_pairs={{0,58},{1,107},{2,60},{3,109},{4,62},{5,111},{6,56},{7,105},{8,34}... | collective-permute-start | bytes 6152 | tf_op jit(solution)/shard_map/ppermute | solution.py:271
  53.3 5.0 %collective-permute-start.21 = (f32[2,1,256]{2,1,0:T(1,128)S(1)}, f32[2,1,256]{2,1,0:T(1,128)S(1)}, u32[]{:S(2)}, u32[]{:S(2)}) collective-permute-start(f32[2,1,256]{2,1,0:T(1,128)S(1)} %get-tuple-element.25), channel_id=1, source_target_pairs={{0,26},{1,99},{2,28},{3,101},{4,30},{5,103},{6,24},{7,97},{8,2},{9... | collective-permute-start | bytes 6152 | tf_op jit(solution)/shard_map/ppermute | solution.py:271
  55.1 3.6 %collective-permute-start.22 = (f32[2,1,256]{2,1,0:T(1,128)S(1)}, f32[2,1,256]{2,1,0:T(1,128)S(1)}, u32[]{:S(2)}, u32[]{:S(2)}) collective-permute-start(f32[2,1,256]{2,1,0:T(1,128)S(1)} %get-tuple-element.24), channel_id=1, source_target_pairs={{0,30},{1,103},{2,24},{3,97},{4,26},{5,99},{6,28},{7,101},{8,6},{9... | collective-permute-start | bytes 6152 | tf_op jit(solution)/shard_map/ppermute | solution.py:271
  58.8 2.4 %collective-permute-start.23 = (f32[2,1,256]{2,1,0:T(1,128)S(1)}, f32[2,1,256]{2,1,0:T(1,128)S(1)}, u32[]{:S(2)}, u32[]{:S(2)}) collective-permute-start(f32[2,1,256]{2,1,0:T(1,128)S(1)} %add_add_fusion), channel_id=1, source_target_pairs={{0,1},{1,0},{2,3},{3,2},{4,5},{5,4},{6,7},{7,6},{8,9},{9,8},{10,11... | collective-permute-start | bytes 6152 | tf_op jit(solution)/shard_map/ppermute | solution.py:272

commit v8 on v7

--- a/solution.py
+++ b/solution.py
@@ -61,7 +61,7 @@
 assert len(set(HELD)) == BLOCKS and {mirror(o) for o in HELD} == set(HELD)
 
 
-SHARES = ((20, 23, 29, 13, 15), (3, 61, 53, 49, 51))
+SHARES = ((20, 29, 23, 13, 15), (3, 53, 61, 49, 51))
 assert sorted(SHARES[0] + SHARES[1]) == sorted(HELD)[1:]
 SHARE = len(SHARES[0])
 GIVEN, HOME = 16, 32

time: 61.9 us -> 63.5 us (1.026); the launches traced: 61.7 us -> 62.5 us
    ppermute x5, starting transfers between devices: 9.51 us -> 10.5 us  [shards(): home += lax.ppermute(kept[2 * n:2 * n + 2], BOTH, give(jumps))]
where the time goes in v8:
time: 63.5 us; the launch traced here: 62.5 us
  starting transfers between devices  39.8 us (63%)
  waiting for transfers between devices  11.2 us (18%)
  Pallas kernels  10.8 us (17%)
    ppermute x10, starting transfers between devices, bring(): mine[k] = lax.ppermute(block, BOTH, fetch((jump, mirror(jump))))  19.4 us
    ppermute x5, starting transfers between devices, shards(): home += lax.ppermute(kept[2 * n:2 * n + 2], BOTH, give(jumps))  10.5 us
    pallas_call x4, Pallas kernels, pair_sums(): pl.pallas_call(functools.partial(pairs_body, work, mine_used, other_used,...  9.66 us
    ppermute x10, waiting for transfers between devices, bring(): mine[k] = lax.ppermute(block, BOTH, fetch((jump, mirror(jump))))  6.56 us
    ppermute x4, starting transfers between devices, shards(): other = {k: lax.ppermute(mine[k], BOTH, CORE_SWAP) for k in EARLY}  6.11 us
    ppermute x5, waiting for transfers between devices, shards(): home += lax.ppermute(kept[2 * n:2 * n + 2], BOTH, give(jumps))  2.74 us
    ppermute x3, starting transfers between devices, shards(): lax.ppermute(block, BOTH, CORE_SWAP)  2.54 us
  transfers between devices with their start and end apart: 24, of which 9 were waited for; matrix products, arithmetic and copies ran while one was open for 0% of the time, Pallas kernels for 14%

profile of v8, /device:TPU:1, one launch (start us, length us, event | category | flops | bytes accessed | tf_op | source)
XLA Modules:
  0.0 62.5 jit_solution(10408263643204360511)
XLA Ops:
  0.0 1.2 %pack.1.refs_0_ = bf16[272,768]{1,0:T(8,128)(2,1)S(1)} custom-call(bf16[256,768]{1,0:T(8,128)(2,1)} %rows_ref.1, s32[1,256]{1,0:T(1,128)} %bitcast.2), custom_call_target="tpu_custom_call" | custom-call | tf_op jit(solution)/shard_map/pack/pallas_call | solution.py:114
  1.2 4.7 %collective-permute-start.1 = (bf16[272,768]{1,0:T(8,128)(2,1)S(1)}, bf16[272,768]{1,0:T(8,128)(2,1)S(1)}, u32[]{:S(2)}, u32[]{:S(2)}) collective-permute-start(bf16[272,768]{1,0:T(8,128)(2,1)S(1)} %pack.1.refs_0_), channel_id=1, source_target_pairs={{26,0},{99,1},{28,2},{101,3},{30,4},{103,5},{24,6},{97,7},{2,8},{1... | collective-permute-start | bytes 1253384 | tf_op jit(solution)/shard_map/ppermute | solution.py:251
  5.9 0.0 collective-permute-start.5
  5.9 3.7 %collective-permute-start.3 = (bf16[272,768]{1,0:T(8,128)(2,1)S(1)}, bf16[272,768]{1,0:T(8,128)(2,1)S(1)}, u32[]{:S(2)}, u32[]{:S(2)}) collective-permute-start(bf16[272,768]{1,0:T(8,128)(2,1)S(1)} %pack.1.refs_0_), channel_id=1, source_target_pairs={{40,0},{41,1},{42,2},{43,3},{44,4},{45,5},{46,6},{47,7},{48,8},{49... | collective-permute-start | bytes 1253384 | tf_op jit(solution)/shard_map/ppermute | solution.py:251
  9.6 2.1 %collective-permute-start.6 = (bf16[272,768]{1,0:T(8,128)(2,1)S(1)}, bf16[272,768]{1,0:T(8,128)(2,1)S(1)}, u32[]{:S(2)}, u32[]{:S(2)}) collective-permute-start(bf16[272,768]{1,0:T(8,128)(2,1)S(1)} %pack.1.refs_0_), channel_id=1, source_target_pairs={{0,1},{1,0},{2,3},{3,2},{4,5},{5,4},{6,7},{7,6},{8,9},{9,8},{10,11... | collective-permute-start | bytes 1253384 | tf_op jit(solution)/shard_map/ppermute | solution.py:257
  11.6 2.8 %collective-permute-start = (bf16[272,768]{1,0:T(8,128)(2,1)S(1)}, bf16[272,768]{1,0:T(8,128)(2,1)S(1)}, u32[]{:S(2)}, u32[]{:S(2)}) collective-permute-start(bf16[272,768]{1,0:T(8,128)(2,1)S(1)} %pack.1.refs_0_), channel_id=1, source_target_pairs={{98,0},{27,1},{100,2},{29,3},{102,4},{31,5},{96,6},{25,7},{106,8},... | collective-permute-start | bytes 1253384 | tf_op jit(solution)/shard_map/ppermute | solution.py:251
  14.4 0.2 collective-permute-done.1.refs_1_
  14.6 2.1 %collective-permute-start.7 = (bf16[272,768]{1,0:T(8,128)(2,1)S(1)}, bf16[272,768]{1,0:T(8,128)(2,1)S(1)}, u32[]{:S(2)}, u32[]{:S(2)}) collective-permute-start(bf16[272,768]{1,0:T(8,128)(2,1)S(1)} %collective-permute-done.1.refs_1_), channel_id=1, source_target_pairs={{0,1},{1,0},{2,3},{3,2},{4,5},{5,4},{6,7},{7,6},{8,9},{9,8},{10,11... | collective-permute-start | bytes 1253384 | tf_op jit(solution)/shard_map/ppermute | solution.py:257
  16.7 1.0 %collective-permute-done.5.refs_2_ = bf16[272,768]{1,0:T(8,128)(2,1)S(1)} collective-permute-done((bf16[272,768]{1,0:T(8,128)(2,1)S(1)}, bf16[272,768]{1,0:T(8,128)(2,1)S(1)}, u32[]{:S(2)}, u32[]{:S(2)}) %collective-permute-start.5) | collective-permute-done | bytes 417824 | tf_op jit(solution)/shard_map/ppermute | solution.py:251
  17.7 1.5 %collective-permute-start.8 = (bf16[272,768]{1,0:T(8,128)(2,1)S(1)}, bf16[272,768]{1,0:T(8,128)(2,1)S(1)}, u32[]{:S(2)}, u32[]{:S(2)}) collective-permute-start(bf16[272,768]{1,0:T(8,128)(2,1)S(1)} %collective-permute-done.5.refs_2_), channel_id=1, source_target_pairs={{0,1},{1,0},{2,3},{3,2},{4,5},{5,4},{6,7},{7,6},{8,9},{9,8},{10,11... | collective-permute-start | bytes 1253384 | tf_op jit(solution)/shard_map/ppermute | solution.py:257
  19.2 0.0 collective-permute-done.3.refs_3_.refs_2_
  19.2 3.0 %collective-permute-start.2 = (bf16[272,768]{1,0:T(8,128)(2,1)S(1)}, bf16[272,768]{1,0:T(8,128)(2,1)S(1)}, u32[]{:S(2)}, u32[]{:S(2)}) collective-permute-start(bf16[272,768]{1,0:T(8,128)(2,1)S(1)} %collective-permute-done.1.refs_1_), channel_id=1, source_target_pairs={{32,0},{9,1},{34,2},{11,3},{36,4},{13,5},{38,6},{15,7},{40,8},{17,... | collective-permute-start | bytes 1253384 | tf_op jit(solution)/shard_map/ppermute | solution.py:251
  22.1 0.0 collective-permute-done.6.refs_4_.refs_7_.refs_10_
  22.1 0.0 collective-permute-start.10
  22.1 3.7 %collective-permute-done.refs_4_.refs_3_.refs_0_ = bf16[272,768]{1,0:T(8,128)(2,1)S(1)} collective-permute-done((bf16[272,768]{1,0:T(8,128)(2,1)S(1)}, bf16[272,768]{1,0:T(8,128)(2,1)S(1)}, u32[]{:S(2)}, u32[]{:S(2)}) %collective-permute-start) | collective-permute-done | bytes 417824 | tf_op jit(solution)/shard_map/ppermute | solution.py:251
  25.8 0.5 collective-permute-start.11
  26.3 0.0 collective-permute-done.7.refs_5_.refs_8_.refs_11_
  26.3 1.2 %collective-permute-start.4 = (bf16[272,768]{1,0:T(8,128)(2,1)S(1)}, bf16[272,768]{1,0:T(8,128)(2,1)S(1)}, u32[]{:S(2)}, u32[]{:S(2)}) collective-permute-start(bf16[272,768]{1,0:T(8,128)(2,1)S(1)} %collective-permute-done.3.refs_3_.refs_2_), channel_id=1, source_target_pairs={{6,0},{7,1},{0,2},{1,3},{2,4},{3,5},{4,6},{5,7},{14,8},{15,9},{8,1... | collective-permute-start | bytes 1253384 | tf_op jit(solution)/shard_map/ppermute | solution.py:251
  27.5 1.3 %collective-permute-start.15 = (bf16[272,768]{1,0:T(8,128)(2,1)S(1)}, bf16[272,768]{1,0:T(8,128)(2,1)S(1)}, u32[]{:S(2)}, u32[]{:S(2)}) collective-permute-start(bf16[272,768]{1,0:T(8,128)(2,1)S(1)} %collective-permute-done.5.refs_2_), channel_id=1, source_target_pairs={{96,0},{25,1},{98,2},{27,3},{100,4},{29,5},{102,6},{31,7},{104,8},... | collective-permute-start | bytes 1253384 | tf_op jit(solution)/shard_map/ppermute | solution.py:251
  28.8 2.1 %pair_sums_0.1.refs_11_ = f32[22,1,256]{2,1,0:T(1,128)S(1)} custom-call(bf16[272,768]{1,0:T(8,128)(2,1)S(1)} %pack.1.refs_0_, bf16[272,768]{1,0:T(8,128)(2,1)S(1)} %collective-permute-done.1.refs_1_, bf16[272,768]{1,0:T(8,128)(2,1)S(1)} %collective-permute-done.5.refs_2_, bf16[272,768]{1,0:T(8,128)(2,1)S(1)} %collective-permute-done.3.refs_3_.refs_2_, ...), custom_call_target="tpu_custom_call" | custom-call | flops 1409286144 | tf_op jit(solution)/shard_map/pair_sums_0/pallas_call | solution.py:217
  30.9 0.0 collective-permute-done.2.refs_6_.refs_5_.refs_1_
  30.9 0.1 collective-permute-start.16
  31.0 2.7 %collective-permute-start.9 = (bf16[272,768]{1,0:T(8,128)(2,1)S(1)}, bf16[272,768]{1,0:T(8,128)(2,1)S(1)}, u32[]{:S(2)}, u32[]{:S(2)}) collective-permute-start(bf16[272,768]{1,0:T(8,128)(2,1)S(1)} %collective-permute-done.refs_4_.refs_3_.refs_0_), channel_id=1, source_target_pairs={{8,0},{33,1},{10,2},{35,3},{12,4},{37,5},{14,6},{39,7},{16,8},{41,... | collective-permute-start | bytes 1253384 | tf_op jit(solution)/shard_map/ppermute | solution.py:251
  33.7 0.0 collective-permute-done.11.refs_10_.refs_13_
  33.7 3.1 %pair_sums_1.1.refs_14_ = f32[22,1,256]{2,1,0:T(1,128)S(1)} custom-call(bf16[272,768]{1,0:T(8,128)(2,1)S(1)} %pack.1.refs_0_, bf16[272,768]{1,0:T(8,128)(2,1)S(1)} %collective-permute-done.1.refs_1_, bf16[272,768]{1,0:T(8,128)(2,1)S(1)} %collective-permute-done.5.refs_2_, bf16[272,768]{1,0:T(8,128)(2,1)S(1)} %collective-permute-done.3.refs_3_.refs_2_, ...), custom_call_target="tpu_custom_call" | custom-call | flops 2415919104 | tf_op jit(solution)/shard_map/pair_sums_1/pallas_call | solution.py:217
  36.8 1.5 %collective-permute-start.12 = (bf16[272,768]{1,0:T(8,128)(2,1)S(1)}, bf16[272,768]{1,0:T(8,128)(2,1)S(1)}, u32[]{:S(2)}, u32[]{:S(2)}) collective-permute-start(bf16[272,768]{1,0:T(8,128)(2,1)S(1)} %collective-permute-done.refs_4_.refs_3_.refs_0_), channel_id=1, source_target_pairs={{0,1},{1,0},{2,3},{3,2},{4,5},{5,4},{6,7},{7,6},{8,9},{9,8},{10,11... | collective-permute-start | bytes 1253384 | tf_op jit(solution)/shard_map/ppermute | solution.py:264
  38.3 0.7 %collective-permute-done.4.refs_6_.refs_2_ = bf16[272,768]{1,0:T(8,128)(2,1)S(1)} collective-permute-done((bf16[272,768]{1,0:T(8,128)(2,1)S(1)}, bf16[272,768]{1,0:T(8,128)(2,1)S(1)}, u32[]{:S(2)}, u32[]{:S(2)}) %collective-permute-start.4) | collective-permute-done | bytes 417824 | tf_op jit(solution)/shard_map/ppermute | solution.py:251
  39.0 1.0 %collective-permute-start.13 = (bf16[272,768]{1,0:T(8,128)(2,1)S(1)}, bf16[272,768]{1,0:T(8,128)(2,1)S(1)}, u32[]{:S(2)}, u32[]{:S(2)}) collective-permute-start(bf16[272,768]{1,0:T(8,128)(2,1)S(1)} %collective-permute-done.10.refs_5_.refs_4_), channel_id=1, source_target_pairs={{0,1},{1,0},{2,3},{3,2},{4,5},{5,4},{6,7},{7,6},{8,9},{9,8},{10,11... | collective-permute-start | bytes 1253384 | tf_op jit(solution)/shard_map/ppermute | solution.py:264
  40.0 0.0 collective-permute-done.15.refs_7_
  40.0 0.0 collective-permute-start.14
  40.0 0.9 %collective-permute-done.16.refs_9_ = bf16[272,768]{1,0:T(8,128)(2,1)S(1)} collective-permute-done((bf16[272,768]{1,0:T(8,128)(2,1)S(1)}, bf16[272,768]{1,0:T(8,128)(2,1)S(1)}, u32[]{:S(2)}, u32[]{:S(2)}) %collective-permute-start.16) | collective-permute-done | bytes 417824 | tf_op jit(solution)/shard_map/ppermute | solution.py:251
  41.0 3.3 %pair_sums_2.1.refs_7_ = f32[22,1,256]{2,1,0:T(1,128)S(1)} custom-call(bf16[272,768]{1,0:T(8,128)(2,1)S(1)} %pack.1.refs_0_, bf16[272,768]{1,0:T(8,128)(2,1)S(1)} %collective-permute-done.1.refs_1_, bf16[272,768]{1,0:T(8,128)(2,1)S(1)} %collective-permute-done.3.refs_3_.refs_2_, bf16[272,768]{1,0:T(8,128)(2,1)S(1)} %collective-permute-done.refs_4_.refs_3_.refs_0_, ...), custom_call_target="tpu_custom_call" | custom-call | flops 2113929216 | tf_op jit(solution)/shard_map/pair_sums_2/pallas_call | solution.py:217
  44.2 0.0 collective-permute-done.12.refs_4_
  44.3 0.0 collective-permute-done.14.refs_6_
  44.3 1.2 %pair_sums_3.1 = (f32[10,1,256]{2,1,0:T(1,128)S(1)}, f32[10,1,256]{2,1,0:T(1,128)S(1)}, f32[2,1,256]{2,1,0:T(1,128)S(1)}) custom-call(bf16[272,768]{1,0:T(8,128)(2,1)S(1)} %collective-permute-done.refs_4_.refs_3_.refs_0_, bf16[272,768]{1,0:T(8,128)(2,1)S(1)} %collective-permute-done.2.refs_6_.refs_5_.refs_1_, ...), custom_call_target="tpu_custom_call" | custom-call | flops 553648128 | tf_op jit(solution)/shard_map/pair_sums_3/pallas_call | solution.py:217
  45.5 0.2 collective-permute-start.17
  45.7 1.1 %collective-permute-done.17 = f32[10,1,256]{2,1,0:T(1,128)S(1)} collective-permute-done((f32[10,1,256]{2,1,0:T(1,128)S(1)}, f32[10,1,256]{2,1,0:T(1,128)S(1)}, u32[]{:S(2)}, u32[]{:S(2)}) %collective-permute-start.17) | collective-permute-done | bytes 10272 | tf_op jit(solution)/shard_map/ppermute | solution.py:268
  46.8 2.1 %collective-permute-start.18 = (f32[2,1,256]{2,1,0:T(1,128)S(1)}, f32[2,1,256]{2,1,0:T(1,128)S(1)}, u32[]{:S(2)}, u32[]{:S(2)}) collective-permute-start(f32[2,1,256]{2,1,0:T(1,128)S(1)} %get-tuple-element.23), channel_id=1, source_target_pairs={{0,40},{1,7},{2,42},{3,1},{4,44},{5,3},{6,46},{7,5},{8,48},{9,15},... | collective-permute-start | bytes 6152 | tf_op jit(solution)/shard_map/ppermute | solution.py:271
  48.9 1.4 %collective-permute-start.19 = (f32[2,1,256]{2,1,0:T(1,128)S(1)}, f32[2,1,256]{2,1,0:T(1,128)S(1)}, u32[]{:S(2)}, u32[]{:S(2)}) collective-permute-start(f32[2,1,256]{2,1,0:T(1,128)S(1)} %get-tuple-element.27), channel_id=1, source_target_pairs={{0,58},{1,107},{2,60},{3,109},{4,62},{5,111},{6,56},{7,105},{8,34}... | collective-permute-start | bytes 6152 | tf_op jit(solution)/shard_map/ppermute | solution.py:271
  50.3 4.2 %collective-permute-start.20 = (f32[2,1,256]{2,1,0:T(1,128)S(1)}, f32[2,1,256]{2,1,0:T(1,128)S(1)}, u32[]{:S(2)}, u32[]{:S(2)}) collective-permute-start(f32[2,1,256]{2,1,0:T(1,128)S(1)} %get-tuple-element.26), channel_id=1, source_target_pairs={{0,46},{1,123},{2,40},{3,125},{4,42},{5,127},{6,44},{7,121},{8,54}... | collective-permute-start | bytes 6152 | tf_op jit(solution)/shard_map/ppermute | solution.py:271
  54.5 1.8 %collective-permute-start.21 = (f32[2,1,256]{2,1,0:T(1,128)S(1)}, f32[2,1,256]{2,1,0:T(1,128)S(1)}, u32[]{:S(2)}, u32[]{:S(2)}) collective-permute-start(f32[2,1,256]{2,1,0:T(1,128)S(1)} %get-tuple-element.25), channel_id=1, source_target_pairs={{0,26},{1,99},{2,28},{3,101},{4,30},{5,103},{6,24},{7,97},{8,2},{9... | collective-permute-start | bytes 6152 | tf_op jit(solution)/shard_map/ppermute | solution.py:271
  56.4 0.9 %collective-permute-start.22 = (f32[2,1,256]{2,1,0:T(1,128)S(1)}, f32[2,1,256]{2,1,0:T(1,128)S(1)}, u32[]{:S(2)}, u32[]{:S(2)}) collective-permute-start(f32[2,1,256]{2,1,0:T(1,128)S(1)} %get-tuple-element.24), channel_id=1, source_target_pairs={{0,30},{1,103},{2,24},{3,97},{4,26},{5,99},{6,28},{7,101},{8,6},{9... | collective-permute-start | bytes 6152 | tf_op jit(solution)/shard_map/ppermute | solution.py:271
  57.2 0.0 collective-permute-done.18
  57.2 2.1 %collective-permute-done.21 = f32[2,1,256]{2,1,0:T(1,128)S(1)} collective-permute-done((f32[2,1,256]{2,1,0:T(1,128)S(1)}, f32[2,1,256]{2,1,0:T(1,128)S(1)}, u32[]{:S(2)}, u32[]{:S(2)}) %collective-permute-start.21) | collective-permute-done | bytes 2080 | tf_op jit(solution)/shard_map/ppermute | solution.py:271
  59.4 0.6 collective-permute-done.22
  60.0 1.1 %collective-permute-start.23 = (f32[2,1,256]{2,1,0:T(1,128)S(1)}, f32[2,1,256]{2,1,0:T(1,128)S(1)}, u32[]{:S(2)}, u32[]{:S(2)}) collective-permute-start(f32[2,1,256]{2,1,0:T(1,128)S(1)} %add_add_fusion), channel_id=1, source_target_pairs={{0,1},{1,0},{2,3},{3,2},{4,5},{5,4},{6,7},{7,6},{8,9},{9,8},{10,11... | collective-permute-start | bytes 6152 | tf_op jit(solution)/shard_map/ppermute | solution.py:272
  61.1 0.8 %collective-permute-done.23 = f32[2,1,256]{2,1,0:T(1,128)S(1)} collective-permute-done((f32[2,1,256]{2,1,0:T(1,128)S(1)}, f32[2,1,256]{2,1,0:T(1,128)S(1)}, u32[]{:S(2)}, u32[]{:S(2)}) %collective-permute-start.23) | collective-permute-done | bytes 2080 | tf_op jit(solution)/shard_map/ppermute | solution.py:272
  61.9 0.6 fusion
  (10 shorter events, 0.0 us)
Async XLA Ops:
  1.2 13.4 %collective-permute-start.1 = (bf16[272,768]{1,0:T(8,128)(2,1)S(1)}, bf16[272,768]{1,0:T(8,128)(2,1)S(1)}, u32[]{:S(2)}, u32[]{:S(2)}) collective-permute-start(bf16[272,768]{1,0:T(8,128)(2,1)S(1)} %pack.1.refs_0_), channel_id=1, source_target_pairs={{26,0},{99,1},{28,2},{101,3},{30,4},{103,5},{24,6},{97,7},{2,8},{1... | collective-permute-start | bytes 1253384 | tf_op jit(solution)/shard_map/ppermute | solution.py:251
  5.9 11.8 %collective-permute-start.5 = (bf16[272,768]{1,0:T(8,128)(2,1)S(1)}, bf16[272,768]{1,0:T(8,128)(2,1)S(1)}, u32[]{:S(2)}, u32[]{:S(2)}) collective-permute-start(bf16[272,768]{1,0:T(8,128)(2,1)S(1)} %pack.1.refs_0_), channel_id=1, source_target_pairs={{6,0},{7,1},{0,2},{1,3},{2,4},{3,5},{4,6},{5,7},{14,8},{15,9},{8,1... | collective-permute-start | bytes 1253384 | tf_op jit(solution)/shard_map/ppermute | solution.py:251
  5.9 13.3 %collective-permute-start.3 = (bf16[272,768]{1,0:T(8,128)(2,1)S(1)}, bf16[272,768]{1,0:T(8,128)(2,1)S(1)}, u32[]{:S(2)}, u32[]{:S(2)}) collective-permute-start(bf16[272,768]{1,0:T(8,128)(2,1)S(1)} %pack.1.refs_0_), channel_id=1, source_target_pairs={{40,0},{41,1},{42,2},{43,3},{44,4},{45,5},{46,6},{47,7},{48,8},{49... | collective-permute-start | bytes 1253384 | tf_op jit(solution)/shard_map/ppermute | solution.py:251
  9.6 12.6 %collective-permute-start.6 = (bf16[272,768]{1,0:T(8,128)(2,1)S(1)}, bf16[272,768]{1,0:T(8,128)(2,1)S(1)}, u32[]{:S(2)}, u32[]{:S(2)}) collective-permute-start(bf16[272,768]{1,0:T(8,128)(2,1)S(1)} %pack.1.refs_0_), channel_id=1, source_target_pairs={{0,1},{1,0},{2,3},{3,2},{4,5},{5,4},{6,7},{7,6},{8,9},{9,8},{10,11... | collective-permute-start | bytes 1253384 | tf_op jit(solution)/shard_map/ppermute | solution.py:257
  11.6 14.2 %collective-permute-start = (bf16[272,768]{1,0:T(8,128)(2,1)S(1)}, bf16[272,768]{1,0:T(8,128)(2,1)S(1)}, u32[]{:S(2)}, u32[]{:S(2)}) collective-permute-start(bf16[272,768]{1,0:T(8,128)(2,1)S(1)} %pack.1.refs_0_), channel_id=1, source_target_pairs={{98,0},{27,1},{100,2},{29,3},{102,4},{31,5},{96,6},{25,7},{106,8},... | collective-permute-start | bytes 1253384 | tf_op jit(solution)/shard_map/ppermute | solution.py:251
  14.6 11.7 %collective-permute-start.7 = (bf16[272,768]{1,0:T(8,128)(2,1)S(1)}, bf16[272,768]{1,0:T(8,128)(2,1)S(1)}, u32[]{:S(2)}, u32[]{:S(2)}) collective-permute-start(bf16[272,768]{1,0:T(8,128)(2,1)S(1)} %collective-permute-done.1.refs_1_), channel_id=1, source_target_pairs={{0,1},{1,0},{2,3},{3,2},{4,5},{5,4},{6,7},{7,6},{8,9},{9,8},{10,11... | collective-permute-start | bytes 1253384 | tf_op jit(solution)/shard_map/ppermute | solution.py:257
  17.7 9.8 %collective-permute-start.8 = (bf16[272,768]{1,0:T(8,128)(2,1)S(1)}, bf16[272,768]{1,0:T(8,128)(2,1)S(1)}, u32[]{:S(2)}, u32[]{:S(2)}) collective-permute-start(bf16[272,768]{1,0:T(8,128)(2,1)S(1)} %collective-permute-done.5.refs_2_), channel_id=1, source_target_pairs={{0,1},{1,0},{2,3},{3,2},{4,5},{5,4},{6,7},{7,6},{8,9},{9,8},{10,11... | collective-permute-start | bytes 1253384 | tf_op jit(solution)/shard_map/ppermute | solution.py:257
  19.2 11.7 %collective-permute-start.2 = (bf16[272,768]{1,0:T(8,128)(2,1)S(1)}, bf16[272,768]{1,0:T(8,128)(2,1)S(1)}, u32[]{:S(2)}, u32[]{:S(2)}) collective-permute-start(bf16[272,768]{1,0:T(8,128)(2,1)S(1)} %collective-permute-done.1.refs_1_), channel_id=1, source_target_pairs={{32,0},{9,1},{34,2},{11,3},{36,4},{13,5},{38,6},{15,7},{40,8},{17,... | collective-permute-start | bytes 1253384 | tf_op jit(solution)/shard_map/ppermute | solution.py:251
  22.1 8.9 %collective-permute-start.10 = (bf16[272,768]{1,0:T(8,128)(2,1)S(1)}, bf16[272,768]{1,0:T(8,128)(2,1)S(1)}, u32[]{:S(2)}, u32[]{:S(2)}) collective-permute-start(bf16[272,768]{1,0:T(8,128)(2,1)S(1)} %collective-permute-done.1.refs_1_), channel_id=1, source_target_pairs={{96,0},{25,1},{98,2},{27,3},{100,4},{29,5},{102,6},{31,7},{104,8},... | collective-permute-start | bytes 1253384 | tf_op jit(solution)/shard_map/ppermute | solution.py:251
  25.8 7.8 %collective-permute-start.11 = (bf16[272,768]{1,0:T(8,128)(2,1)S(1)}, bf16[272,768]{1,0:T(8,128)(2,1)S(1)}, u32[]{:S(2)}, u32[]{:S(2)}) collective-permute-start(bf16[272,768]{1,0:T(8,128)(2,1)S(1)} %collective-permute-done.3.refs_3_.refs_2_), channel_id=1, source_target_pairs={{0,1},{1,0},{2,3},{3,2},{4,5},{5,4},{6,7},{7,6},{8,9},{9,8},{10,11... | collective-permute-start | bytes 1253384 | tf_op jit(solution)/shard_map/ppermute | solution.py:257
  26.3 12.7 %collective-permute-start.4 = (bf16[272,768]{1,0:T(8,128)(2,1)S(1)}, bf16[272,768]{1,0:T(8,128)(2,1)S(1)}, u32[]{:S(2)}, u32[]{:S(2)}) collective-permute-start(bf16[272,768]{1,0:T(8,128)(2,1)S(1)} %collective-permute-done.3.refs_3_.refs_2_), channel_id=1, source_target_pairs={{6,0},{7,1},{0,2},{1,3},{2,4},{3,5},{4,6},{5,7},{14,8},{15,9},{8,1... | collective-permute-start | bytes 1253384 | tf_op jit(solution)/shard_map/ppermute | solution.py:251
  27.5 12.5 %collective-permute-start.15 = (bf16[272,768]{1,0:T(8,128)(2,1)S(1)}, bf16[272,768]{1,0:T(8,128)(2,1)S(1)}, u32[]{:S(2)}, u32[]{:S(2)}) collective-permute-start(bf16[272,768]{1,0:T(8,128)(2,1)S(1)} %collective-permute-done.5.refs_2_), channel_id=1, source_target_pairs={{96,0},{25,1},{98,2},{27,3},{100,4},{29,5},{102,6},{31,7},{104,8},... | collective-permute-start | bytes 1253384 | tf_op jit(solution)/shard_map/ppermute | solution.py:251
  30.9 10.1 %collective-permute-start.16 = (bf16[272,768]{1,0:T(8,128)(2,1)S(1)}, bf16[272,768]{1,0:T(8,128)(2,1)S(1)}, u32[]{:S(2)}, u32[]{:S(2)}) collective-permute-start(bf16[272,768]{1,0:T(8,128)(2,1)S(1)} %collective-permute-done.5.refs_2_), channel_id=1, source_target_pairs={{24,0},{97,1},{26,2},{99,3},{28,4},{101,5},{30,6},{103,7},{0,8},{1... | collective-permute-start | bytes 1253384 | tf_op jit(solution)/shard_map/ppermute | solution.py:251
  31.0 10.0 %collective-permute-start.9 = (bf16[272,768]{1,0:T(8,128)(2,1)S(1)}, bf16[272,768]{1,0:T(8,128)(2,1)S(1)}, u32[]{:S(2)}, u32[]{:S(2)}) collective-permute-start(bf16[272,768]{1,0:T(8,128)(2,1)S(1)} %collective-permute-done.refs_4_.refs_3_.refs_0_), channel_id=1, source_target_pairs={{8,0},{33,1},{10,2},{35,3},{12,4},{37,5},{14,6},{39,7},{16,8},{41,... | collective-permute-start | bytes 1253384 | tf_op jit(solution)/shard_map/ppermute | solution.py:251
  36.8 7.5 %collective-permute-start.12 = (bf16[272,768]{1,0:T(8,128)(2,1)S(1)}, bf16[272,768]{1,0:T(8,128)(2,1)S(1)}, u32[]{:S(2)}, u32[]{:S(2)}) collective-permute-start(bf16[272,768]{1,0:T(8,128)(2,1)S(1)} %collective-permute-done.refs_4_.refs_3_.refs_0_), channel_id=1, source_target_pairs={{0,1},{1,0},{2,3},{3,2},{4,5},{5,4},{6,7},{7,6},{8,9},{9,8},{10,11... | collective-permute-start | bytes 1253384 | tf_op jit(solution)/shard_map/ppermute | solution.py:264
  39.0 5.3 %collective-permute-start.13 = (bf16[272,768]{1,0:T(8,128)(2,1)S(1)}, bf16[272,768]{1,0:T(8,128)(2,1)S(1)}, u32[]{:S(2)}, u32[]{:S(2)}) collective-permute-start(bf16[272,768]{1,0:T(8,128)(2,1)S(1)} %collective-permute-done.10.refs_5_.refs_4_), channel_id=1, source_target_pairs={{0,1},{1,0},{2,3},{3,2},{4,5},{5,4},{6,7},{7,6},{8,9},{9,8},{10,11... | collective-permute-start | bytes 1253384 | tf_op jit(solution)/shard_map/ppermute | solution.py:264
  40.0 4.2 %collective-permute-start.14 = (bf16[272,768]{1,0:T(8,128)(2,1)S(1)}, bf16[272,768]{1,0:T(8,128)(2,1)S(1)}, u32[]{:S(2)}, u32[]{:S(2)}) collective-permute-start(bf16[272,768]{1,0:T(8,128)(2,1)S(1)} %collective-permute-done.2.refs_6_.refs_5_.refs_1_), channel_id=1, source_target_pairs={{0,1},{1,0},{2,3},{3,2},{4,5},{5,4},{6,7},{7,6},{8,9},{9,8},{10,11... | collective-permute-start | bytes 1253384 | tf_op jit(solution)/shard_map/ppermute | solution.py:264
  45.5 1.2 %collective-permute-start.17 = (f32[10,1,256]{2,1,0:T(1,128)S(1)}, f32[10,1,256]{2,1,0:T(1,128)S(1)}, u32[]{:S(2)}, u32[]{:S(2)}) collective-permute-start(f32[10,1,256]{2,1,0:T(1,128)S(1)} %get-tuple-element.22), channel_id=1, source_target_pairs={{0,1},{1,0},{2,3},{3,2},{4,5},{5,4},{6,7},{7,6},{8,9},{9,8},{10,11... | collective-permute-start | bytes 30728 | tf_op jit(solution)/shard_map/ppermute | solution.py:268
  46.8 10.5 %collective-permute-start.18 = (f32[2,1,256]{2,1,0:T(1,128)S(1)}, f32[2,1,256]{2,1,0:T(1,128)S(1)}, u32[]{:S(2)}, u32[]{:S(2)}) collective-permute-start(f32[2,1,256]{2,1,0:T(1,128)S(1)} %get-tuple-element.23), channel_id=1, source_target_pairs={{0,40},{1,7},{2,42},{3,1},{4,44},{5,3},{6,46},{7,5},{8,48},{9,15},... | collective-permute-start | bytes 6152 | tf_op jit(solution)/shard_map/ppermute | solution.py:271
  48.9 8.3 %collective-permute-start.19 = (f32[2,1,256]{2,1,0:T(1,128)S(1)}, f32[2,1,256]{2,1,0:T(1,128)S(1)}, u32[]{:S(2)}, u32[]{:S(2)}) collective-permute-start(f32[2,1,256]{2,1,0:T(1,128)S(1)} %get-tuple-element.27), channel_id=1, source_target_pairs={{0,58},{1,107},{2,60},{3,109},{4,62},{5,111},{6,56},{7,105},{8,34}... | collective-permute-start | bytes 6152 | tf_op jit(solution)/shard_map/ppermute | solution.py:271
  50.3 6.9 %collective-permute-start.20 = (f32[2,1,256]{2,1,0:T(1,128)S(1)}, f32[2,1,256]{2,1,0:T(1,128)S(1)}, u32[]{:S(2)}, u32[]{:S(2)}) collective-permute-start(f32[2,1,256]{2,1,0:T(1,128)S(1)} %get-tuple-element.26), channel_id=1, source_target_pairs={{0,46},{1,123},{2,40},{3,125},{4,42},{5,127},{6,44},{7,121},{8,54}... | collective-permute-start | bytes 6152 | tf_op jit(solution)/shard_map/ppermute | solution.py:271
  54.5 4.8 %collective-permute-start.21 = (f32[2,1,256]{2,1,0:T(1,128)S(1)}, f32[2,1,256]{2,1,0:T(1,128)S(1)}, u32[]{:S(2)}, u32[]{:S(2)}) collective-permute-start(f32[2,1,256]{2,1,0:T(1,128)S(1)} %get-tuple-element.25), channel_id=1, source_target_pairs={{0,26},{1,99},{2,28},{3,101},{4,30},{5,103},{6,24},{7,97},{8,2},{9... | collective-permute-start | bytes 6152 | tf_op jit(solution)/shard_map/ppermute | solution.py:271
  56.4 3.6 %collective-permute-start.22 = (f32[2,1,256]{2,1,0:T(1,128)S(1)}, f32[2,1,256]{2,1,0:T(1,128)S(1)}, u32[]{:S(2)}, u32[]{:S(2)}) collective-permute-start(f32[2,1,256]{2,1,0:T(1,128)S(1)} %get-tuple-element.24), channel_id=1, source_target_pairs={{0,30},{1,103},{2,24},{3,97},{4,26},{5,99},{6,28},{7,101},{8,6},{9... | collective-permute-start | bytes 6152 | tf_op jit(solution)/shard_map/ppermute | solution.py:271
  60.0 1.9 %collective-permute-start.23 = (f32[2,1,256]{2,1,0:T(1,128)S(1)}, f32[2,1,256]{2,1,0:T(1,128)S(1)}, u32[]{:S(2)}, u32[]{:S(2)}) collective-permute-start(f32[2,1,256]{2,1,0:T(1,128)S(1)} %add_add_fusion), channel_id=1, source_target_pairs={{0,1},{1,0},{2,3},{3,2},{4,5},{5,4},{6,7},{7,6},{8,9},{9,8},{10,11... | collective-permute-start | bytes 6152 | tf_op jit(solution)/shard_map/ppermute | solution.py:272
